TPU v7x, 32 devices: a whole 2x2x4 slice. The times are simulated.
32 devices in a mesh: dp: 4 (over z), seq: 8 (over y, x, core).
Axes of the slice: x: 2, y: 2, z: 4, core: 2. Of those that a mesh axis runs over, the one named last changes fastest.
Arguments:
- lin_q: bfloat16 [4096, 32, 128], P(('dp', 'seq')), parts along dimension 0, may hold values from -6 to 6
- lin_k: bfloat16 [4096, 32, 128], P(('dp', 'seq')), parts along dimension 0, may hold values from -6 to 6
- lin_v: bfloat16 [4096, 32, 128], P(('dp', 'seq')), parts along dimension 0, may hold values from -6 to 6
- lin_decay: bfloat16 [4096, 32], P(('dp', 'seq')), parts along dimension 0, may hold values from -1 to 0
- lin_gain: float32 [4096], replicated, may hold values from 0.5 to 1.5
- soft_q: bfloat16 [4096, 32, 128], P(('dp', 'seq')), parts along dimension 0, may hold values from -6 to 6
- soft_k: bfloat16 [4096, 32, 128], P(('dp', 'seq')), parts along dimension 0, may hold values from -6 to 6
- soft_v: bfloat16 [4096, 32, 128], P(('dp', 'seq')), parts along dimension 0, may hold values from -6 to 6
- block_bits: int32 [32, 8], P('dp'), parts along dimension 0, may hold values 0 or 1
- agent_ids: int32 [32], P('dp'), parts along dimension 0, may hold values from 0 to 7
Outputs:
- lin_out: bfloat16 [4096, 32, 128], P(('dp', 'seq')), parts along dimension 0
- soft_out: bfloat16 [4096, 32, 128], P(('dp', 'seq')), parts along dimension 0
There are 4 independent parts, one for each index of `dp`. A program takes and returns all parts, laid end to end along the dimension named above; an argument that names none is the same for every part. Nothing has to cross between parts.
All inputs are finite; a program needn't handle non-finite values.
Results may differ from a plain program's by a relative error of at most 0.0049.
Values may be sent and summed in bfloat16 or wider, within the bound.
No kernel may reach another device: no remote copies, remote signals or barrier semaphores. Data moves between devices by JAX's collectives and lax.ppermute only.
A program may use at most 128 MiB of HBM per device.

v0:
```python
import jax
import jax.numpy as jnp
from jax import lax
from jax.sharding import PartitionSpec as P

SPAN = 128
MB = 128


EPSILON = 1e-06


def carried_in(part, axis, combine, identity):
    place = lax.axis_index(axis)
    gathered = jax.tree.map(lambda a: lax.all_gather(a, axis), part)
    state = jax.tree.map(lambda a, e: jnp.zeros_like(a) + jnp.asarray(e, a.dtype), part, identity)

    def one(lap, state):
        return combine(
            state, jax.tree.map(lambda a: lax.dynamic_index_in_dim(a, lap, 0, False), gathered)
        )

    return lax.fori_loop(0, place, one, state)


def span_terms(queries, keys_in, values, decays):
    length, group, width = queries.shape
    blocks = length // SPAN
    shaped_q = queries.reshape(blocks, SPAN, group, width)
    shaped_k = keys_in.reshape(blocks, SPAN, group, width)
    shaped_v = values.reshape(blocks, SPAN, group, width)
    cumul = jnp.cumsum(decays.astype(jnp.float32).reshape(blocks, SPAN, group), axis=1)
    row_ids = lax.broadcasted_iota(jnp.int32, (SPAN, SPAN), 0)
    col_ids = lax.broadcasted_iota(jnp.int32, (SPAN, SPAN), 1)
    lower = (col_ids <= row_ids)[None, :, :, None]
    spread_diff = cumul[:, :, None, :] - cumul[:, None, :, :]
    damping = jnp.where(lower, jnp.exp(jnp.where(lower, spread_diff, 0.0)), 0.0)
    scores = jnp.einsum("bthd,bshd->btsh", shaped_q, shaped_k, preferred_element_type=jnp.float32)
    weights = (scores * damping).astype(jnp.bfloat16)
    intra = jnp.einsum("btsh,bshd->bthd", weights, shaped_v, preferred_element_type=jnp.float32)
    q_scaled = shaped_q.astype(jnp.float32) * jnp.exp(cumul)[..., None]
    totals = cumul[:, -1, :]
    decayed = (
        shaped_k.astype(jnp.float32) * jnp.exp(totals[:, None, :] - cumul)[..., None]
    ).astype(jnp.bfloat16)
    states = jnp.einsum("bshd,bshe->bhde", decayed, shaped_v, preferred_element_type=jnp.float32)
    return (intra, q_scaled, totals, states)


def span_starts(totals, states):

    def advance(carried, inputs):
        log_rate, block_state = inputs
        return (jnp.exp(log_rate)[:, None, None] * carried + block_state, carried)

    final, starts = lax.scan(advance, jnp.zeros_like(states[0]), (totals, states))
    return (starts, final)


def finish(intra, q_scaled, starts):
    inter = jnp.einsum("bthd,bhde->bthe", q_scaled, starts, precision=lax.Precision.HIGHEST)
    mixed = intra + inter
    return mixed.reshape(-1, mixed.shape[2], mixed.shape[3])


def normalize(mixed, gain):
    shaped = mixed.reshape(mixed.shape[0], -1)
    power = jnp.mean(shaped * shaped, axis=1, keepdims=True)
    return (shaped * lax.rsqrt(power + EPSILON) * gain).astype(jnp.bfloat16).reshape(mixed.shape)


def visibility(block_bits, agent_ids):
    blocks_total = block_bits.shape[0]
    same_agent = agent_ids[:, None] == agent_ids[None, :]
    row_ids = lax.broadcasted_iota(jnp.int32, (blocks_total, blocks_total), 0)
    col_ids = lax.broadcasted_iota(jnp.int32, (blocks_total, blocks_total), 1)
    return ((block_bits == 1) | same_agent) & (col_ids <= row_ids)


def attend(queries, keys_in, values, allowed_blocks):
    length = queries.shape[0]
    tile_rows = min(512, length)
    scale = queries.shape[-1] ** (-0.5)
    col_ids = lax.broadcasted_iota(jnp.int32, (tile_rows, length), 1)

    def one_tile(tile_index):
        first_row = tile_index * tile_rows
        tile_q = lax.dynamic_slice_in_dim(queries, first_row, tile_rows, 0)
        scores = (
            jnp.einsum("thd,shd->hts", tile_q, keys_in, preferred_element_type=jnp.float32) * scale
        )
        block_rows = lax.dynamic_slice_in_dim(allowed_blocks, first_row // MB, tile_rows // MB, 0)
        permitted = jnp.repeat(jnp.repeat(block_rows, MB, axis=0), MB, axis=1)
        row_ids = lax.broadcasted_iota(jnp.int32, (tile_rows, length), 0) + first_row
        permitted = permitted & (col_ids <= row_ids)
        scores = jnp.where(permitted[None], scores, -jnp.inf)
        summit = jnp.max(scores, axis=2, keepdims=True)
        expos = jnp.exp(scores - summit)
        probs = (expos / jnp.sum(expos, axis=2, keepdims=True)).astype(jnp.bfloat16)
        return jnp.einsum("hts,shd->thd", probs, values, preferred_element_type=jnp.float32).astype(
            jnp.bfloat16
        )

    tiles = lax.map(one_tile, jnp.arange(length // tile_rows))
    return tiles.reshape(queries.shape)


def per_device(
    lin_q, lin_k, lin_v, lin_decay, lin_gain, soft_q, soft_k, soft_v, block_bits, agent_ids
):
    groups = lax.axis_size("seq")
    tok_rows, lin_heads, width = lin_q.shape
    soft_heads = soft_q.shape[1]
    intra, q_scaled, totals, states = span_terms(lin_q, lin_k, lin_v, lin_decay)
    starts, final = span_starts(totals, states)
    before = jnp.cumsum(totals, axis=0) - totals
    device_log = jnp.sum(totals, axis=0)

    def combine(earlier, later):
        return (earlier[0] + later[0], jnp.exp(later[0])[:, None, None] * earlier[1] + later[1])

    identity = (jnp.zeros_like(device_log), jnp.zeros_like(final))
    incoming = carried_in((device_log, final), "seq", combine, identity)
    entry = starts + jnp.exp(before)[:, :, None, None] * incoming[1][None]
    mixed = finish(intra, q_scaled, entry)
    lin_out = normalize(mixed, lin_gain)
    allowed_blocks = visibility(block_bits, agent_ids)
    local_soft = soft_heads // groups
    queries = lax.all_to_all(
        soft_q.reshape(tok_rows, groups, local_soft, width),
        "seq",
        split_axis=1,
        concat_axis=0,
        tiled=True,
    )
    keys_in = lax.all_to_all(
        soft_k.reshape(tok_rows, groups, local_soft, width),
        "seq",
        split_axis=1,
        concat_axis=0,
        tiled=True,
    )
    values = lax.all_to_all(
        soft_v.reshape(tok_rows, groups, local_soft, width),
        "seq",
        split_axis=1,
        concat_axis=0,
        tiled=True,
    )
    attended = attend(queries[:, 0], keys_in[:, 0], values[:, 0], allowed_blocks)[:, None]
    soft_out = lax.all_to_all(attended, "seq", split_axis=0, concat_axis=1, tiled=True).reshape(
        tok_rows, soft_heads, width
    )
    return (lin_out, soft_out)


def solution(mesh):
    return jax.shard_map(
        per_device,
        mesh=mesh,
        in_specs=(
            P(("dp", "seq"), None, None),
            P(("dp", "seq"), None, None),
            P(("dp", "seq"), None, None),
            P(("dp", "seq"), None),
            P(),
            P(("dp", "seq"), None, None),
            P(("dp", "seq"), None, None),
            P(("dp", "seq"), None, None),
            P("dp", None),
            P("dp"),
        ),
        out_specs=(P(("dp", "seq"), None, None), P(("dp", "seq"), None, None)),
        check_vma=False,
    )
```

profile of v0, /device:TPU:31, one launch (start us, length us, event | category | flops | bytes accessed | tf_op | source)
XLA Modules:
  0.0 194.0 jit_solution(15781010338314852564)
XLA Ops:
  8.3 1.7 multiply_convert_fusion
  10.1 2.3 %convolution_add_fusion = f32[32,128,128]{2,1,0:T(8,128)} fusion(bf16[128,32,128]{2,1,0:T(8,128)(2,1)S(1)} %multiply_convert_fusion, f32[32]{0:T(128)S(1)} %get-tuple-element.218, bf16[128,32,128]{2,1,0:T(8,128)(2,1)S(1)} %copy-done.1), kind=kOutput, calls=%fused_computation.40 | convolution fusion | flops 134742016 | bytes 4194432 | tf_op jit(solution)/shard_map/bshd,bshe->bhde/dot_general | solution.py:46
  15.0 4.5 %all-to-all-start = ((bf16[128,8,4,128]{3,0,2,1:T(8,128)(2,1)}), bf16[128,8,4,128]{3,0,2,1:T(8,128)(2,1)S(1)}, u32[]{:S(2)}, u32[]{:S(2)}) async-start(bf16[128,8,4,128]{3,0,2,1:T(8,128)(2,1)} %bitcast.16), calls=%async_computation | async-start | bytes 2097152 | tf_op jit(solution)/shard_map/all_to_all | solution.py:129
  20.9 17.5 %all-to-all-done = bf16[128,8,4,128]{3,0,2,1:T(8,128)(2,1)S(1)} async-done(((bf16[128,8,4,128]{3,0,2,1:T(8,128)(2,1)}), bf16[128,8,4,128]{3,0,2,1:T(8,128)(2,1)S(1)}, u32[]{:S(2)}, u32[]{:S(2)}) %all-to-all-start) | async-done | bytes 1048608 | tf_op jit(solution)/shard_map/all_to_all | solution.py:129
  38.4 8.2 %all-to-all-start.1 = ((bf16[128,8,4,128]{3,0,2,1:T(8,128)(2,1)}), bf16[128,8,4,128]{3,0,2,1:T(8,128)(2,1)S(1)}, u32[]{:S(2)}, u32[]{:S(2)}) async-start(bf16[128,8,4,128]{3,0,2,1:T(8,128)(2,1)} %bitcast.20), calls=%async_computation.1 | async-start | bytes 2097152 | tf_op jit(solution)/shard_map/all_to_all | solution.py:136
  46.6 1.4 copy.96
  48.0 17.1 %all-to-all-done.1 = bf16[128,8,4,128]{3,0,2,1:T(8,128)(2,1)S(1)} async-done(((bf16[128,8,4,128]{3,0,2,1:T(8,128)(2,1)}), bf16[128,8,4,128]{3,0,2,1:T(8,128)(2,1)S(1)}, u32[]{:S(2)}, u32[]{:S(2)}) %all-to-all-start.1) | async-done | bytes 1048608 | tf_op jit(solution)/shard_map/all_to_all | solution.py:136
  65.1 7.0 %all-to-all-start.2 = ((bf16[128,8,4,128]{3,0,2,1:T(8,128)(2,1)}), bf16[128,8,4,128]{3,0,2,1:T(8,128)(2,1)S(1)}, u32[]{:S(2)}, u32[]{:S(2)}) async-start(bf16[128,8,4,128]{3,0,2,1:T(8,128)(2,1)} %bitcast.24), calls=%async_computation.2 | async-start | bytes 2097152 | tf_op jit(solution)/shard_map/all_to_all | solution.py:143
  74.2 21.0 %all-to-all-done.2 = bf16[128,8,4,128]{3,0,2,1:T(8,128)(2,1)S(1)} async-done(((bf16[128,8,4,128]{3,0,2,1:T(8,128)(2,1)}), bf16[128,8,4,128]{3,0,2,1:T(8,128)(2,1)S(1)}, u32[]{:S(2)}, u32[]{:S(2)}) %all-to-all-start.2) | async-done | bytes 1048608 | tf_op jit(solution)/shard_map/all_to_all | solution.py:143
  96.3 33.3 %while.31 = (s32[]{:T(128)}, bf16[2,512,4,128]{3,1,0,2:T(8,128)(2,1)}, s32[2]{0:T(128)S(1)}, pred[8,8]{1,0:T(8,128)(4,1)S(1)}, bf16[1024,4,128]{2,0,1:T(8,128)(2...) while((s32[]{:T(128)}, ...), condition=%wide.region_7.8_spmd.clone, body=%wide.region_4.7_spmd.clone.sunk | while | flops 1087636992 | bytes 26244092 | solution.py:104
  97.6 1.6 broadcast_in_dim.119
  99.8 7.5 %fusion.72 = (f32[4,512]{1,0:T(4,128)S(1)}, f32[4,512,1024]{2,1,0:T(8,128)}) fusion(pred[512,1024]{1,0:T(8,128)(4,1)S(1)} %fusion.71, bf16[1024,4,128]{2,0,1:T(8,128)(2,1)} %get-tuple-element.363, bf16[1024,4,128]{2,0,1:T(8,128)(2,1)S(1)} %get-tuple-element.362, s32[]{:T(128)S(6)} %select_n.92), kind=kOutput, calls=%fused_computation.64.clone.1 | convolution fusion | flops 545260544 | bytes 10493956 | tf_op jit(solution)/shard_map/while/body/eval_jaxpr/sub | solution.py:98
  107.3 5.7 %fusion.73 = bf16[2,512,4,128]{3,1,0,2:T(8,128)(2,1)} fusion(bf16[2,512,4,128]{3,1,0,2:T(8,128)(2,1)} %get-tuple-element.344, s32[]{:T(128)} %get-tuple-element.343, bf16[1024,4,128]{2,0,1:T(8,128)(2,1)S(1)} %copy-done.7, f32[4,512,1024]{2,1,0:T(8,128)} %get-tuple-element.302, f32[4,512]{1,0:T(4,128)S(1)} %get-tuple-element.303), kind=kOutput, calls=%fused_computation.16.clone.1 | convolution fusion | flops 541327360 | bytes 9970176 | tf_op jit(solution)/shard_map/while/body/eval_jaxpr/hts,shd->thd/dot_general | solution.py:100
  114.3 1.6 broadcast_in_dim.119
  116.5 7.5 %fusion.72 = (f32[4,512]{1,0:T(4,128)S(1)}, f32[4,512,1024]{2,1,0:T(8,128)}) fusion(pred[512,1024]{1,0:T(8,128)(4,1)S(1)} %fusion.71, bf16[1024,4,128]{2,0,1:T(8,128)(2,1)} %get-tuple-element.363, bf16[1024,4,128]{2,0,1:T(8,128)(2,1)S(1)} %get-tuple-element.362, s32[]{:T(128)S(6)} %select_n.92), kind=kOutput, calls=%fused_computation.64.clone.1 | convolution fusion | flops 545260544 | bytes 10493956 | tf_op jit(solution)/shard_map/while/body/eval_jaxpr/sub | solution.py:98
  124.0 5.6 %fusion.73 = bf16[2,512,4,128]{3,1,0,2:T(8,128)(2,1)} fusion(bf16[2,512,4,128]{3,1,0,2:T(8,128)(2,1)} %get-tuple-element.344, s32[]{:T(128)} %get-tuple-element.343, bf16[1024,4,128]{2,0,1:T(8,128)(2,1)S(1)} %copy-done.7, f32[4,512,1024]{2,1,0:T(8,128)} %get-tuple-element.302, f32[4,512]{1,0:T(4,128)S(1)} %get-tuple-element.303), kind=kOutput, calls=%fused_computation.16.clone.1 | convolution fusion | flops 541327360 | bytes 9970176 | tf_op jit(solution)/shard_map/while/body/eval_jaxpr/hts,shd->thd/dot_general | solution.py:100
  129.6 3.1 %copy.99 = bf16[1024,1,4,128]{3,2,1,0:T(4,128)(2,1)} copy(bf16[1024,1,4,128]{3,0,2,1:T(8,128)(2,1)} %bitcast.111) | data formatting | bytes 2097152 | tf_op jit(solution)/shard_map/broadcast_in_dim;reshape | solution.py:150
  132.7 6.6 %all-to-all-start.3 = ((bf16[1024,1,4,128]{3,2,1,0:T(4,128)(2,1)}), bf16[1024,1,4,128]{3,2,1,0:T(4,128)(2,1)S(1)}, u32[]{:S(2)}, u32[]{:S(2)}) async-start(bf16[1024,1,4,128]{3,2,1,0:T(4,128)(2,1)} %copy.99), calls=%async_computation.3 | async-start | bytes 2097152 | tf_op jit(solution)/shard_map/all_to_all | solution.py:151
  139.4 15.8 %all-gather = f32[8,1,32]{2,1,0:T(1,128)S(1)} all-gather(f32[1,1,32]{2,1,0:T(1,128)S(1)} %get-tuple-element.222), channel_id=2, replica_groups=mesh['dp'=4,'seq'=8] {'seq'}, dimensions={0}, use_global_device_ids=true | all-gather | bytes 1152 | tf_op jit(solution)/shard_map/all_gather | solution.py:15
  155.2 1.9 %convert_multiply_fusion = f32[128,32,128]{2,1,0:T(8,128)} fusion(bf16[128,32,128]{2,1,0:T(8,128)(2,1)S(1)} %copy-done, f32[128,32]{1,0:T(8,128)S(1)} %get-tuple-element.220), kind=kLoop, calls=%fused_computation.37 | loop fusion | flops 1048576 | bytes 3162112 | tf_op jit(solution)/shard_map/mul | solution.py:41
  157.2 4.4 %fusion.39 = f32[32,128,128]{1,2,0:T(8,128)} fusion(bf16[128,32,128]{2,1,0:T(8,128)(2,1)S(1)} %copy-done, bf16[128,32,128]{2,1,0:T(8,128)(2,1)} %param.15, f32[128,32]{0,1:T(8,128)S(1)} %copy.84, pred[128,128]{0,1:T(8,128)(4,1)S(1)} %iota_compare_fusion.1, bf16[128,32,128]{2,1,0:T(8,128)(2,1)S(1)} %copy-done.2), kind=kOutput, calls=%fused_computation.42 | convolution fusion | flops 271056896 | bytes 5275648 | tf_op jit(solution)/shard_map/btsh,bshd->bthd/dot_general | solution.py:40
  161.9 1.7 copy.103
  163.7 14.2 %while.30 = (s32[]{:T(128)}, f32[32,128,128]{2,1,0:T(8,128)S(1)}, s32[]{:T(128)}, f32[8,32]{1,0:T(8,128)S(1)}, f32[8,32,128,128]{3,2,1,0:T(8,128)}, /*index=5*/s32[]{:T(128)}, s32[]{:T(128)}, s32[]{:T(128)}) while((s32[]{:T(128)}, f32[32,128,128]{2,1,0:T(8,128)S(1)}, s32[]{:T(128)}, f32[8,32]{1,0:T(8,128)S(1)}, f32[8,32,128,128]{3,2,1,0:T(8,128)}, ...), condition=%wide.region_2.3_spmd, body=%wide.region_1.2_spmd.sunk | while | flops 1048581 | bytes 6291967 | solution.py:23
  163.8 2.0 %bitcast_add_fusion.3 = f32[32,128,128]{2,1,0:T(8,128)S(1)} fusion(f32[8,32,128,128]{3,2,1,0:T(8,128)} %get-tuple-element.324, s32[]{:T(128)S(6)} %select_n.88, f32[32,128,128]{2,1,0:T(8,128)S(1)} %get-tuple-element.313, f32[32]{0:T(128)S(1)} %exponential_bitcast_fusion.2), kind=kLoop, calls=%fused_computation.1.clone.1 | loop fusion | flops 1048576 | bytes 6291588 | tf_op jit(solution)/shard_map/while/body/add | solution.py:120
  165.8 2.0 %bitcast_add_fusion.3 = f32[32,128,128]{2,1,0:T(8,128)S(1)} fusion(f32[8,32,128,128]{3,2,1,0:T(8,128)} %get-tuple-element.324, s32[]{:T(128)S(6)} %select_n.88, f32[32,128,128]{2,1,0:T(8,128)S(1)} %get-tuple-element.313, f32[32]{0:T(128)S(1)} %exponential_bitcast_fusion.2), kind=kLoop, calls=%fused_computation.1.clone.1 | loop fusion | flops 1048576 | bytes 6291588 | tf_op jit(solution)/shard_map/while/body/add | solution.py:120
  167.8 2.0 %bitcast_add_fusion.3 = f32[32,128,128]{2,1,0:T(8,128)S(1)} fusion(f32[8,32,128,128]{3,2,1,0:T(8,128)} %get-tuple-element.324, s32[]{:T(128)S(6)} %select_n.88, f32[32,128,128]{2,1,0:T(8,128)S(1)} %get-tuple-element.313, f32[32]{0:T(128)S(1)} %exponential_bitcast_fusion.2), kind=kLoop, calls=%fused_computation.1.clone.1 | loop fusion | flops 1048576 | bytes 6291588 | tf_op jit(solution)/shard_map/while/body/add | solution.py:120
  169.9 2.0 %bitcast_add_fusion.3 = f32[32,128,128]{2,1,0:T(8,128)S(1)} fusion(f32[8,32,128,128]{3,2,1,0:T(8,128)} %get-tuple-element.324, s32[]{:T(128)S(6)} %select_n.88, f32[32,128,128]{2,1,0:T(8,128)S(1)} %get-tuple-element.313, f32[32]{0:T(128)S(1)} %exponential_bitcast_fusion.2), kind=kLoop, calls=%fused_computation.1.clone.1 | loop fusion | flops 1048576 | bytes 6291588 | tf_op jit(solution)/shard_map/while/body/add | solution.py:120
  171.9 2.0 %bitcast_add_fusion.3 = f32[32,128,128]{2,1,0:T(8,128)S(1)} fusion(f32[8,32,128,128]{3,2,1,0:T(8,128)} %get-tuple-element.324, s32[]{:T(128)S(6)} %select_n.88, f32[32,128,128]{2,1,0:T(8,128)S(1)} %get-tuple-element.313, f32[32]{0:T(128)S(1)} %exponential_bitcast_fusion.2), kind=kLoop, calls=%fused_computation.1.clone.1 | loop fusion | flops 1048576 | bytes 6291588 | tf_op jit(solution)/shard_map/while/body/add | solution.py:120
  173.9 2.0 %bitcast_add_fusion.3 = f32[32,128,128]{2,1,0:T(8,128)S(1)} fusion(f32[8,32,128,128]{3,2,1,0:T(8,128)} %get-tuple-element.324, s32[]{:T(128)S(6)} %select_n.88, f32[32,128,128]{2,1,0:T(8,128)S(1)} %get-tuple-element.313, f32[32]{0:T(128)S(1)} %exponential_bitcast_fusion.2), kind=kLoop, calls=%fused_computation.1.clone.1 | loop fusion | flops 1048576 | bytes 6291588 | tf_op jit(solution)/shard_map/while/body/add | solution.py:120
  176.0 2.0 %bitcast_add_fusion.3 = f32[32,128,128]{2,1,0:T(8,128)S(1)} fusion(f32[8,32,128,128]{3,2,1,0:T(8,128)} %get-tuple-element.324, s32[]{:T(128)S(6)} %select_n.88, f32[32,128,128]{2,1,0:T(8,128)S(1)} %get-tuple-element.313, f32[32]{0:T(128)S(1)} %exponential_bitcast_fusion.2), kind=kLoop, calls=%fused_computation.1.clone.1 | loop fusion | flops 1048576 | bytes 6291588 | tf_op jit(solution)/shard_map/while/body/add | solution.py:120
  178.0 6.8 %fusion.30 = (f32[128]{0:T(128)S(1)}, f32[32,128,128]{2,1,0:T(8,128)S(1)}) fusion(f32[128,32,128]{2,1,0:T(8,128)} %convert_multiply_fusion, f32[32,128,128]{2,1,0:T(8,128)S(1)} %get-tuple-element.163, f32[32]{0:T(128)S(1)} %get-tuple-element.217, f32[32,128,128]{1,2,0:T(8,128)} %fusion.39), kind=kOutput, calls=%fused_computation.33 | convolution fusion | flops 807403392 | bytes 8389248 | tf_op jit(solution)/shard_map/bthd,bhde->bthe/dot_general | solution.py:61
  185.5 1.7 copy.102
  (66 shorter events, 12.1 us)
Async XLA Ops:
  7.2 2.9 %copy-start.1 = (bf16[128,32,128]{2,1,0:T(8,128)(2,1)S(1)}, bf16[128,32,128]{2,1,0:T(8,128)(2,1)}, u32[]{:S(2)}) copy-start(bf16[128,32,128]{2,1,0:T(8,128)(2,1)} %param.16) | copy-start | bytes 3145732
  7.2 156.3 %all-gather.4.cloned.1.call-start = ((), (), s32[]{:S(2)}) async-start(), calls=%async_computation.4 | async-start | bytes 18874368 | tf_op jit(solution)/shard_map/all_gather | solution.py:15
  12.4 1.2 copy-start.3
  13.6 5.9 %copy-start.4 = (bf16[128,32,128]{2,1,0:T(8,128)(2,1)S(1)}, bf16[128,32,128]{2,1,0:T(8,128)(2,1)}, u32[]{:S(2)}) copy-start(bf16[128,32,128]{2,1,0:T(8,128)(2,1)} %param.20) | copy-start | bytes 3145732
  15.0 23.4 %all-to-all-start = ((bf16[128,8,4,128]{3,0,2,1:T(8,128)(2,1)}), bf16[128,8,4,128]{3,0,2,1:T(8,128)(2,1)S(1)}, u32[]{:S(2)}, u32[]{:S(2)}) async-start(bf16[128,8,4,128]{3,0,2,1:T(8,128)(2,1)} %bitcast.16), calls=%async_computation | async-start | bytes 2097152 | tf_op jit(solution)/shard_map/all_to_all | solution.py:129
  19.5 27.1 %copy-start.5 = (bf16[128,32,128]{2,1,0:T(8,128)(2,1)S(1)}, bf16[128,32,128]{2,1,0:T(8,128)(2,1)}, u32[]{:S(2)}) copy-start(bf16[128,32,128]{2,1,0:T(8,128)(2,1)} %param.21) | copy-start | bytes 3145732
  38.4 26.7 %all-to-all-start.1 = ((bf16[128,8,4,128]{3,0,2,1:T(8,128)(2,1)}), bf16[128,8,4,128]{3,0,2,1:T(8,128)(2,1)S(1)}, u32[]{:S(2)}, u32[]{:S(2)}) async-start(bf16[128,8,4,128]{3,0,2,1:T(8,128)(2,1)} %bitcast.20), calls=%async_computation.1 | async-start | bytes 2097152 | tf_op jit(solution)/shard_map/all_to_all | solution.py:136
  46.6 25.5 %copy-start.9 = (s32[8,8]{1,0:T(8,128)S(1)}, s32[8,8]{1,0:T(8,128)}, u32[]{:S(2)}) copy-start(s32[8,8]{1,0:T(8,128)} %param.22) | copy-start | bytes 772
  46.6 25.5 %copy-start.10 = (s32[8]{0:T(128)S(1)}, s32[8]{0:T(128)}, u32[]{:S(2)}) copy-start(s32[8]{0:T(128)} %param.23) | copy-start | bytes 100
  65.1 30.1 %all-to-all-start.2 = ((bf16[128,8,4,128]{3,0,2,1:T(8,128)(2,1)}), bf16[128,8,4,128]{3,0,2,1:T(8,128)(2,1)S(1)}, u32[]{:S(2)}, u32[]{:S(2)}) async-start(bf16[128,8,4,128]{3,0,2,1:T(8,128)(2,1)} %bitcast.24), calls=%async_computation.2 | async-start | bytes 2097152 | tf_op jit(solution)/shard_map/all_to_all | solution.py:143
  74.2 22.0 %copy-start.6 = (bf16[128,8,4,128]{3,0,1,2:T(8,128)(2,1)S(1)}, bf16[128,8,4,128]{3,0,1,2:T(8,128)(2,1)}, u32[]{:S(2)}) copy-start(bf16[128,8,4,128]{3,0,1,2:T(8,128)(2,1)} %copy.93) | copy-start | bytes 3145732
  99.8 7.5 %copy-start.7 = (bf16[1024,4,128]{2,0,1:T(8,128)(2,1)S(1)}, bf16[1024,4,128]{2,0,1:T(8,128)(2,1)}, u32[]{:S(2)}) copy-start(bf16[1024,4,128]{2,0,1:T(8,128)(2,1)} %get-tuple-element.364) | copy-start | bytes 3145732 | tf_op jit(solution)/shard_map/while
  116.5 7.5 %copy-start.7 = (bf16[1024,4,128]{2,0,1:T(8,128)(2,1)S(1)}, bf16[1024,4,128]{2,0,1:T(8,128)(2,1)}, u32[]{:S(2)}) copy-start(bf16[1024,4,128]{2,0,1:T(8,128)(2,1)} %get-tuple-element.364) | copy-start | bytes 3145732 | tf_op jit(solution)/shard_map/while
  129.6 25.6 %copy-start = (bf16[128,32,128]{2,1,0:T(8,128)(2,1)S(1)}, bf16[128,32,128]{2,1,0:T(8,128)(2,1)}, u32[]{:S(2)}) copy-start(bf16[128,32,128]{2,1,0:T(8,128)(2,1)} %param.14) | copy-start | bytes 3145732
  132.7 28.9 %all-to-all-start.3 = ((bf16[1024,1,4,128]{3,2,1,0:T(4,128)(2,1)}), bf16[1024,1,4,128]{3,2,1,0:T(4,128)(2,1)S(1)}, u32[]{:S(2)}, u32[]{:S(2)}) async-start(bf16[1024,1,4,128]{3,2,1,0:T(4,128)(2,1)} %copy.99), calls=%async_computation.3 | async-start | bytes 2097152 | tf_op jit(solution)/shard_map/all_to_all | solution.py:151
  139.3 17.8 %copy-start.2 = (bf16[128,32,128]{2,1,0:T(8,128)(2,1)S(1)}, bf16[128,32,128]{2,1,0:T(8,128)(2,1)}, u32[]{:S(2)}) copy-start(bf16[128,32,128]{2,1,0:T(8,128)(2,1)} %param.16) | copy-start | bytes 3145732
  177.9 6.8 %copy-start.8 = (f32[4096]{0:T(1024)S(1)}, f32[4096]{0:T(1024)}, u32[]{:S(2)}) copy-start(f32[4096]{0:T(1024)} %param.18) | copy-start | bytes 49156
Sparse Core Ops, SparseCore 0:
  12.5 119.8 all-gather.3
where the time goes:
time: 195 us; the launch traced here: 194 us
  waiting for transfers between devices  55.5 us (28%)
  matrix products  39.8 us (20%)
  starting transfers between devices  26.4 us (14%)
  other arithmetic  20.4 us (10%)
  local copies, waits for them, and re-layouts  20.1 us (10%)
  blocking collectives  15.8 us (8%)
  between operations  14.2 us (7%)
    all_to_all x1, waiting for transfers between devices, per_device(): lax.all_to_all(soft_v.reshape(tok_rows, groups, local_soft, width), 'seq'...  21 us
    all_to_all x1, waiting for transfers between devices, per_device(): lax.all_to_all(soft_q.reshape(tok_rows, groups, local_soft, width), 'seq'...  17.5 us
    all_to_all x1, waiting for transfers between devices, per_device(): lax.all_to_all(soft_k.reshape(tok_rows, groups, local_soft, width), 'seq'...  17.1 us
    all_gather x1, blocking collectives, carried_in(): gathered = jax.tree.map(lambda a: lax.all_gather(a, axis), part)  15.8 us
    sub x2, matrix products, one_tile(): expos = jnp.exp(scores - summit)  15 us
    add x7, other arithmetic, combine(): jnp.exp(later[0])[:, None, None] * earlier[1] + later[1]  13.8 us
    dot_general x2, matrix products, one_tile(): jnp.einsum('hts,shd->thd', probs, values, preferred_element_type=jnp.floa...  11.3 us
    unnamed x25, local copies, waits for them, and re-layouts  8.72 us
  transfers between devices with their start and end apart: 5, of which 3 were waited for; matrix products, arithmetic and copies ran while one was open for 26% of the time, Pallas kernels for 0%

commit v1 on v0

v1 whole, which is shorter than its diff:
```python
import functools

import jax
import jax.numpy as jnp
from jax import lax
from jax.experimental import pallas as pl
from jax.experimental.pallas import tpu as pltpu
from jax.sharding import PartitionSpec as P

EPSILON = 1e-06
PAIR = 2
PARTS = 2
TURN = 8
LOG2E = 1.4426950408889634
VMEM = pl.BlockSpec(memory_space=pltpu.VMEM)
SMEM = pl.BlockSpec(memory_space=pltpu.SMEM)
ANY = pl.BlockSpec(memory_space=pl.ANY)


def params(mib):
    return pltpu.CompilerParams(vmem_limit_bytes=mib << 20)


def cost(flops, nbytes, exps=0):
    return pl.CostEstimate(flops=flops, bytes_accessed=nbytes, transcendentals=exps)


def shape(dims, dtype):
    return jax.ShapeDtypeStruct(dims, dtype)


def turns(heads):
    step = min(TURN, heads)
    return [(at, step) for at in range(0, heads, step)]


def nt(a, b):
    return lax.dot_general(a, b, (((1,), (1,)), ((), ())), preferred_element_type=jnp.float32)


def tn(a, b):
    return lax.dot_general(a, b, (((0,), (0,)), ((), ())), preferred_element_type=jnp.float32)


def nn(a, b):
    return lax.dot_general(a, b, (((1,), (0,)), ((), ())), preferred_element_type=jnp.float32)


def triangle(size):
    rows = lax.broadcasted_iota(jnp.int32, (size, size), 0)
    cols = lax.broadcasted_iota(jnp.int32, (size, size), 1)
    return cols <= rows


def pack(place, arrays, chips, hosted, parts):
    rows, heads, width = arrays[0].shape
    each = hosted // parts

    def kernel(place_ref, q_ref, k_ref, v_ref, *rest):
        outs, turned = rest[:-1], rest[-1]
        for which, ref in enumerate((q_ref, k_ref, v_ref)):
            for at, step in turns(heads):
                turned[which, at : at + step] = jnp.swapaxes(ref[:, at : at + step, :], 0, 1)
        chip = place_ref[0] // PAIR
        for m in range(chips):
            first = (chip ^ m) * hosted
            for part in range(parts):
                for which in range(3):
                    outs[m * parts + part][which] = turned[which, pl.ds(first + part * each, each)]

    outs = pl.pallas_call(
        kernel,
        out_shape=[shape((3, each, rows, width), jnp.bfloat16)] * (chips * parts),
        in_specs=[SMEM, VMEM, VMEM, VMEM],
        out_specs=[VMEM] * (chips * parts),
        scratch_shapes=[pltpu.VMEM((3, heads, rows, width), jnp.bfloat16)],
        compiler_params=params(24),
        cost_estimate=cost(0, 12 * rows * heads * width),
        name="pack",
    )(place, *arrays)
    return [outs[m * parts : (m + 1) * parts] for m in range(chips)]


def attend(place, bits, agents, own, other):
    chips = len(own)
    _, each, rows, width = own[0].shape
    slots = PAIR * chips
    scale = width**-0.5 * LOG2E

    def kernel(place_ref, bits_ref, agents_ref, *rest):
        ins, outs = rest[:slots], rest[slots : slots + chips]
        held, scores, top, total, mixed, done, sems = rest[slots + chips :]
        me = place_ref[0]
        chip, core = me // PAIR, me % PAIR
        copies = [pltpu.make_async_copy(ins[j], held.at[j], sems.at[j]) for j in range(slots)]
        for copy in copies:
            copy.start()
        for copy in copies:
            copy.wait()
        lower = triangle(rows)

        def block_of(j):
            return PAIR * (chip ^ (j % chips)) + jnp.where(j < chips, core, PAIR - 1 - core)

        def sees(query_block, j):
            key_block = block_of(j)
            open_ = (bits_ref[query_block, key_block] == 1) | (
                agents_ref[query_block] == agents_ref[key_block]
            )
            return (key_block < query_block) & open_

        def one_query(i, carry):
            query_block = block_of(i)
            for h in range(each):
                s = jnp.where(lower, nt(held[i, 0, h], held[i, 1, h]), -1e30)
                scores[slots, h] = s
                top[h] = s

            def score(j, carry):
                @pl.when(sees(query_block, j))
                def _():
                    for h in range(each):
                        s = nt(held[i, 0, h], held[j, 1, h])
                        scores[j, h] = s
                        top[h] = jnp.maximum(top[h], s)

                return carry

            lax.fori_loop(0, slots, score, 0)
            for h in range(each):
                summit = jnp.max(top[h], axis=1, keepdims=True)
                top[h] = jnp.broadcast_to(summit, (rows, rows))
                p = jnp.exp2((scores[slots, h] - summit) * scale)
                total[h] = p
                mixed[h] = nn(p.astype(jnp.bfloat16), held[i, 2, h])

            def weigh(j, carry):
                @pl.when(sees(query_block, j))
                def _():
                    for h in range(each):
                        p = jnp.exp2((scores[j, h] - top[h]) * scale)
                        total[h] += p
                        mixed[h] += nn(p.astype(jnp.bfloat16), held[j, 2, h])

                return carry

            lax.fori_loop(0, slots, weigh, 0)
            for h in range(each):
                sums = jnp.sum(total[h], axis=1, keepdims=True)
                done[i, h] = (mixed[h] / sums).astype(jnp.bfloat16)
            return carry

        lax.fori_loop(0, chips, one_query, 0)
        for m in range(chips):
            outs[m][...] = done[m]

    pairs = chips * slots // 2
    return pl.pallas_call(
        kernel,
        out_shape=[shape((each, rows, width), jnp.bfloat16)] * chips,
        in_specs=[SMEM, SMEM, SMEM] + [ANY] * slots,
        out_specs=[VMEM] * chips,
        scratch_shapes=[
            pltpu.VMEM((slots, 3, each, rows, width), jnp.bfloat16),
            pltpu.VMEM((slots + 1, each, rows, rows), jnp.float32),
            pltpu.VMEM((each, rows, rows), jnp.float32),
            pltpu.VMEM((each, rows, rows), jnp.float32),
            pltpu.VMEM((each, rows, width), jnp.float32),
            pltpu.VMEM((chips, each, rows, width), jnp.bfloat16),
            pltpu.SemaphoreType.DMA((slots,)),
        ],
        compiler_params=params(24),
        cost_estimate=cost(
            4 * pairs * each * rows * rows * width,
            2 * (3 * slots + chips) * each * rows * width,
            pairs * each * rows * rows,
        ),
        name="attend",
    )(place, bits, agents, *own, *other)


def unpack(place, pieces, heads):
    chips, parts = len(pieces), len(pieces[0])
    each, rows, width = pieces[0][0].shape

    def kernel(place_ref, *rest):
        ins, out_ref, turned = rest[:-2], rest[-2], rest[-1]
        chip = place_ref[0] // PAIR
        for m in range(chips):
            for part in range(parts):
                first = (chip ^ m) * (each * parts) + part * each
                turned[pl.ds(first, each)] = ins[m * parts + part][...]
        for at, step in turns(heads):
            out_ref[:, at : at + step, :] = jnp.swapaxes(turned[at : at + step], 0, 1)

    return pl.pallas_call(
        kernel,
        out_shape=shape((rows, heads, width), jnp.bfloat16),
        in_specs=[SMEM] + [VMEM] * (chips * parts),
        out_specs=VMEM,
        scratch_shapes=[pltpu.VMEM((heads, rows, width), jnp.bfloat16)],
        compiler_params=params(16),
        cost_estimate=cost(0, 4 * rows * heads * width),
        name="unpack",
    )(place, *[piece for row in pieces for piece in row])


def decay_sums(decay_ref):
    decay = decay_ref[...]
    lower = triangle(decay.shape[0]).astype(jnp.bfloat16)
    return nn(lower, decay), lax.dot_general(
        decay, lower, (((0,), (1,)), ((), ())), preferred_element_type=jnp.float32
    )


def block_state(keys, values, decay):
    rows, heads, width = keys.shape

    def kernel(k_ref, v_ref, decay_ref, out_ref):
        cumul, _ = decay_sums(decay_ref)
        last = cumul[rows - 1 : rows, :]
        left = jnp.exp(last - cumul)
        for at, step in turns(heads):
            k = jnp.swapaxes(k_ref[:, at : at + step, :], 0, 1)
            v = jnp.swapaxes(v_ref[:, at : at + step, :], 0, 1)
            for h in range(step):
                kept = k[h].astype(jnp.float32) * left[:, at + h : at + h + 1]
                out_ref[at + h] = tn(kept.astype(jnp.bfloat16), v[h])
        out_ref[heads] = jnp.zeros((width, width), jnp.float32)
        out_ref[heads, 0:1, 0:heads] = last

    return pl.pallas_call(
        kernel,
        out_shape=shape((heads + 1, width, width), jnp.float32),
        in_specs=[VMEM] * 3,
        out_specs=VMEM,
        compiler_params=params(24),
        cost_estimate=cost(2 * heads * rows * width * width, 8 * rows * heads * width),
        name="block_state",
    )(keys, values, decay)


def within(queries, keys, values, decay):
    rows, heads, width = queries.shape

    def kernel(q_ref, k_ref, v_ref, decay_ref, out_ref):
        cumul, cumul_row = decay_sums(decay_ref)
        lower = triangle(rows)
        for at, step in turns(heads):
            q = jnp.swapaxes(q_ref[:, at : at + step, :], 0, 1)
            k = jnp.swapaxes(k_ref[:, at : at + step, :], 0, 1)
            v = jnp.swapaxes(v_ref[:, at : at + step, :], 0, 1)
            for h in range(step):
                i = at + h
                apart = cumul[:, i : i + 1] - cumul_row[i : i + 1, :]
                damping = jnp.where(lower, jnp.exp(jnp.where(lower, apart, 0.0)), 0.0)
                weights = (nt(q[h], k[h]) * damping).astype(jnp.bfloat16)
                out_ref[i] = nn(weights, v[h])

    return pl.pallas_call(
        kernel,
        out_shape=shape((heads, rows, width), jnp.float32),
        in_specs=[VMEM] * 4,
        out_specs=VMEM,
        compiler_params=params(24),
        cost_estimate=cost(4 * heads * rows * rows * width, 10 * rows * heads * width, heads * rows * rows),
        name="within",
    )(queries, keys, values, decay)


def write_packed(out_ref, state, logs):
    half = state.shape[0]
    out_ref[0:half] = state.astype(jnp.bfloat16)
    write_logs(out_ref, half, logs)


def write_logs(out_ref, half, logs):
    width = out_ref.shape[-1]
    first = logs.astype(jnp.bfloat16).astype(jnp.float32)
    second = (logs - first).astype(jnp.bfloat16).astype(jnp.float32)
    third = logs - first - second
    row = lax.broadcasted_iota(jnp.int32, (width, width), 0)
    packed = jnp.where(row == 0, first, jnp.where(row == 1, second, jnp.where(row == 2, third, 0.0)))
    out_ref[half] = packed.astype(jnp.bfloat16)


def read_logs(ref, half):
    block = ref[half].astype(jnp.float32)
    return block[0:1, :] + block[1:2, :] + block[2:3, :]


def join_cores(place, own, other):
    heads, width = own.shape[0] - 1, own.shape[-1]
    half = heads // PAIR

    def kernel(place_ref, own_ref, other_ref, total_ref, logs_ref, packed_ref):
        core = place_ref[0] % PAIR
        own_logs, other_logs = own_ref[heads, 0:1, :], other_ref[heads, 0:1, :]
        own_half = jnp.where(core == 0, own_logs[:, 0:half], own_logs[:, half:heads])
        other_half = jnp.where(core == 0, other_logs[:, 0:half], other_logs[:, half:heads])
        later = jnp.exp(jnp.where(core == 0, other_half, own_half))
        own_factor = jnp.where(core == 0, later, 1.0)
        other_factor = jnp.where(core == 0, 1.0, later)
        for h in range(half):
            at = core * half + h
            total = own_ref[at] * own_factor[:, h : h + 1] + other_ref[at] * other_factor[:, h : h + 1]
            total_ref[h] = total
            packed_ref[h] = total.astype(jnp.bfloat16)
        logs_ref[...] = jnp.zeros_like(logs_ref)
        logs_ref[0:1, 0:half] = own_half + other_half
        write_logs(packed_ref, half, logs_ref[0:1, :])

    return pl.pallas_call(
        kernel,
        out_shape=[
            shape((half, width, width), jnp.float32),
            shape((8, width), jnp.float32),
            shape((half + 1, width, width), jnp.bfloat16),
        ],
        in_specs=[SMEM, VMEM, VMEM],
        out_specs=[VMEM] * 3,
        compiler_params=params(24),
        cost_estimate=cost(3 * half * width * width, 14 * half * width * width),
        name="join_cores",
    )(place, own, other)


def climb(place, bit, last, total, logs, entry, got):
    half, width = total.shape[0], total.shape[-1]

    def kernel(place_ref, *refs):
        total_ref, logs_ref = refs[0], refs[1]
        entry_ref = None if entry is None else refs[2]
        got_ref = refs[2 if entry is None else 3]
        outs = refs[3 if entry is None else 4 :]
        upper = (place_ref[0] >> bit) & 1
        got_logs = read_logs(got_ref, half)
        own_logs, before = logs_ref[0:1, :], logs_ref[1:2, :]
        into = jnp.where(upper == 1, jnp.exp(before), 0.0)
        own_factor = jnp.where(upper == 1, 1.0, jnp.exp(got_logs))
        got_factor = jnp.where(upper == 1, jnp.exp(own_logs), 1.0)
        for h in range(half):
            arrived = got_ref[h].astype(jnp.float32)
            carried = arrived * into[:, h : h + 1]
            outs[0][h] = carried if entry is None else carried + entry_ref[h]
            if not last:
                joined = total_ref[h] * own_factor[:, h : h + 1] + arrived * got_factor[:, h : h + 1]
                outs[1][h] = joined
                outs[3][h] = joined.astype(jnp.bfloat16)
        if not last:
            outs[2][...] = jnp.zeros_like(outs[2])
            outs[2][0:1, :] = own_logs + got_logs
            outs[2][1:2, :] = before + jnp.where(upper == 1, got_logs, 0.0)
            write_logs(outs[3], half, own_logs + got_logs)

    state = shape((half, width, width), jnp.float32)
    out_shape = [state]
    if not last:
        out_shape += [state, shape((8, width), jnp.float32), shape((half + 1, width, width), jnp.bfloat16)]
    ins = [total, logs] + ([] if entry is None else [entry]) + [got]
    return pl.pallas_call(
        kernel,
        out_shape=out_shape,
        in_specs=[SMEM] + [VMEM] * len(ins),
        out_specs=[VMEM] * len(out_shape),
        compiler_params=params(24),
        cost_estimate=cost(4 * half * width * width, 16 * half * width * width),
        name="climb",
    )(place, *ins)


def finish(place, queries, decay, gain, inner, neighbour, entry_own, entry_other):
    rows, heads, width = queries.shape
    half = heads // PAIR

    def kernel(
        place_ref, q_ref, decay_ref, gain_ref, inner_ref, near_ref, own_ref, other_ref, out_ref, mixed
    ):
        core = place_ref[0] % PAIR
        cumul, _ = decay_sums(decay_ref)
        grown = jnp.exp(cumul)
        near_logs = near_ref[heads, 0:1, :]
        far = jnp.where(core == 0, 1.0, jnp.exp(near_logs))
        near = jnp.where(core == 0, 0.0, 1.0)
        power = jnp.zeros((rows, width), jnp.float32)
        for at, step in turns(heads):
            q = jnp.swapaxes(q_ref[:, at : at + step, :], 0, 1)
            for h in range(step):
                i = at + h
                mine, theirs = own_ref[i % half], other_ref[i % half]
                chip_entry = jnp.where(core == i // half, mine, theirs)
                entry = chip_entry * far[:, i : i + 1] + near_ref[i] * near
                coarse = entry.astype(jnp.bfloat16)
                fine = (entry - coarse.astype(jnp.float32)).astype(jnp.bfloat16)
                brought = (nn(q[h], coarse) + nn(q[h], fine)) * grown[:, i : i + 1]
                mix = inner_ref[i] + brought
                mixed[i] = mix
                power += mix * mix
        mean = jnp.sum(power, axis=1, keepdims=True) / (heads * width)
        norm = lax.rsqrt(mean + EPSILON)
        for at, step in turns(heads):
            normed = [
                (mixed[at + h] * norm * gain_ref[at + h : at + h + 1, :]).astype(jnp.bfloat16)
                for h in range(step)
            ]
            out_ref[:, at : at + step, :] = jnp.swapaxes(jnp.stack(normed), 0, 1)

    return pl.pallas_call(
        kernel,
        out_shape=shape((rows, heads, width), jnp.bfloat16),
        in_specs=[SMEM] + [VMEM] * 7,
        out_specs=VMEM,
        scratch_shapes=[pltpu.VMEM((heads, rows, width), jnp.float32)],
        compiler_params=params(32),
        cost_estimate=cost(4 * heads * rows * width * width, 20 * rows * heads * width),
        name="finish",
    )(place, queries, decay, gain, inner, neighbour, entry_own, entry_other)


def swapped(count, mask):
    return [(i, i ^ mask) for i in range(count)]


def per_device(
    lin_q, lin_k, lin_v, lin_decay, lin_gain, soft_q, soft_k, soft_v, block_bits, agent_ids
):
    count = lax.axis_size("seq")
    chips = count // PAIR
    rows, heads, width = soft_q.shape
    lin_heads = lin_q.shape[1]
    hosted = heads // chips
    parts = min(PARTS, hosted)
    place = lax.axis_index("seq").astype(jnp.int32).reshape(1)
    send = functools.partial(lax.ppermute, axis_name="seq")

    packed = pack(place, (soft_q, soft_k, soft_v), chips, hosted, parts)
    own = [[packed[0][part]] for part in range(parts)]
    for m in range(1, chips):
        before = None
        for part in range(parts):
            outgoing = packed[m][part]
            if before is not None:
                outgoing, before = lax.optimization_barrier((outgoing, before))
                own[part - 1][m] = before
            before = send(outgoing, perm=swapped(count, PAIR * m))
            own[part].append(before)

    state = block_state(lin_k, lin_v, lin_decay)
    near = send(state, perm=swapped(count, 1))
    total, logs, outgoing = join_cores(place, state, near)
    entry = None
    levels = (count // PAIR).bit_length() - 1
    for level in range(levels):
        bit = level + PAIR.bit_length() - 1
        last = level == levels - 1
        mask = 1 << bit
        pairs = [(i, j) for i, j in swapped(count, mask) if not last or i < j]
        got = send(outgoing, perm=pairs)
        out = climb(place, bit, last, total, logs, entry, got)
        entry = out[0]
        if not last:
            total, logs, outgoing = out[1:]
    entry_other = send(entry, perm=swapped(count, 1))
    inner = within(lin_q, lin_k, lin_v, lin_decay)
    lin_out = finish(
        place, lin_q, lin_decay, lin_gain.reshape(lin_heads, width), inner, near, entry, entry_other
    )

    back = [[] for _ in range(chips)]
    for part in range(parts):
        other = [send(block, perm=swapped(count, 1)) for block in own[part]]
        mixed = attend(place, block_bits, agent_ids, own[part], other)
        for m in range(chips):
            back[m].append(mixed[m] if m == 0 else send(mixed[m], perm=swapped(count, PAIR * m)))
    soft_out = unpack(place, back, heads)
    return (lin_out, soft_out)


def solution(mesh):
    rows = P(("dp", "seq"), None, None)
    return jax.shard_map(
        per_device,
        mesh=mesh,
        in_specs=(rows, rows, rows, P(("dp", "seq"), None), P(), rows, rows, rows, P("dp", None), P("dp")),
        out_specs=(rows, rows),
        check_vma=False,
    )
```

time: 195 us -> 107 us (0.55)
  the two profiles are of different devices: /device:TPU:31 before, /device:TPU:0 now
where the time goes in v1:
time: 107 us; the launch traced here: 105 us
  waiting for transfers between devices  44.9 us (42%)
  Pallas kernels  31.8 us (30%)
  starting transfers between devices  24.5 us (23%)
  local copies, waits for them, and re-layouts  3.31 us (3%)
    ppermute x2, waiting for transfers between devices, per_device(): got = send(outgoing, perm=pairs)  24.4 us
    ppermute x6, waiting for transfers between devices, per_device(): before = send(outgoing, perm=swapped(count, PAIR * m))  14.9 us
    pallas_call x2, Pallas kernels, attend(): pl.pallas_call(kernel, out_shape=[shape((each, rows, width), jnp.bfloat16...  14.5 us
    ppermute x6, starting transfers between devices, per_device(): send(mixed[m], perm=swapped(count, PAIR * m))  7.65 us
    ppermute x6, starting transfers between devices, per_device(): before = send(outgoing, perm=swapped(count, PAIR * m))  7.46 us
    ppermute x2, starting transfers between devices, per_device(): got = send(outgoing, perm=pairs)  7.14 us
    pallas_call x1, Pallas kernels, within(): pl.pallas_call(kernel, out_shape=shape((heads, rows, width), jnp.float32)...  5.01 us
    ppermute x1, waiting for transfers between devices, per_device(): near = send(state, perm=swapped(count, 1))  4.09 us
  transfers between devices with their start and end apart: 24, of which 8 were waited for; matrix products, arithmetic and copies ran while one was open for 0% of the time, Pallas kernels for 22%

profile of v1, /device:TPU:0, one launch (start us, length us, event | category | flops | bytes accessed | tf_op | source)
XLA Modules:
  0.0 105.3 jit_solution(2890787119009738358)
XLA Ops:
  0.6 0.8 copy.14.decay_ref
  1.4 1.2 %copy-done.1 = bf16[128,32,128]{2,1,0:T(8,128)(2,1)S(1)} copy-done((bf16[128,32,128]{2,1,0:T(8,128)(2,1)S(1)}, bf16[128,32,128]{2,1,0:T(8,128)(2,1)}, u32[]{:S(2)}) %copy-start.1) | copy-done | bytes 1048600
  2.7 1.2 %copy-done.3 = bf16[128,32,128]{2,1,0:T(8,128)(2,1)S(1)} copy-done((bf16[128,32,128]{2,1,0:T(8,128)(2,1)S(1)}, bf16[128,32,128]{2,1,0:T(8,128)(2,1)}, u32[]{:S(2)}) %copy-start.3) | copy-done | bytes 1048600
  3.9 3.5 %block_state.1.own_ref = f32[33,128,128]{2,1,0:T(8,128)} custom-call(bf16[128,32,128]{2,1,0:T(8,128)(2,1)S(1)} %copy-done.1, bf16[128,32,128]{2,1,0:T(8,128)(2,1)S(1)} %copy-done.3, bf16[128,32]{1,0:T(8,128)(2,1)S(1)} %copy.14.decay_ref), custom_call_target="tpu_custom_call" | custom-call | flops 134217728 | bytes 4194304 | tf_op jit(solution)/shard_map/block_state/pallas_call | solution.py:232
  7.4 0.4 collective-permute-start
  7.8 4.1 %collective-permute-done.other_ref.near_ref = f32[33,128,128]{2,1,0:T(8,128)S(1)} collective-permute-done((f32[33,128,128]{2,1,0:T(8,128)}, f32[33,128,128]{2,1,0:T(8,128)S(1)}, u32[]{:S(2)}, u32[]{:S(2)}) %collective-permute-start) | collective-permute-done | bytes 2162720 | tf_op jit(solution)/shard_map/ppermute | solution.py:449
  11.9 2.1 %join_cores.1 = (f32[16,128,128]{2,1,0:T(8,128)S(1)}, f32[8,128]{1,0:T(8,128)S(1)}, bf16[17,128,128]{2,1,0:T(8,128)(2,1)S(1)}) custom-call(s32[1]{0:T(128)} %bitcast.place_ref, f32[33,128,128]{2,1,0:T(8,128)} %block_state.1.own_ref, f32[33,128,128]{2,1,0:T(8,128)S(1)} %collective-permute-done.other_ref.near_ref), custom_call_target="tpu_custom_call" | custom-call | flops 786432 | bytes 3670016 | tf_op jit(solution)/shard_map/join_cores/pallas_call | solution.py:313
  14.0 2.9 %collective-permute-start.1 = (bf16[17,128,128]{2,1,0:T(8,128)(2,1)S(1)}, bf16[17,128,128]{2,1,0:T(8,128)(2,1)S(1)}, u32[]{:S(2)}, u32[]{:S(2)}) collective-permute-start(bf16[17,128,128]{2,1,0:T(8,128)(2,1)S(1)} %get-tuple-element.33), channel_id=1, source_target_pairs={{0,2},{1,3},{2,0},{3,1},{4,6},{5,7},{6,4},{7,5},{8,10},{9,11},{10,... | collective-permute-start | bytes 1671176 | tf_op jit(solution)/shard_map/ppermute | solution.py:458
  16.9 1.3 %pack.1 = (bf16[3,4,128,128]{3,2,1,0:T(8,128)(2,1)S(1)}, bf16[3,4,128,128]{3,2,1,0:T(8,128)(2,1)S(1)}, bf16[3,4,128,128]{3,2,1,0:T(8,128)(2,1)S(1)}, bf16[3,4,12...) custom-call(s32[1]{0:T(128)} %bitcast.place_ref, ...), custom_call_target="tpu_custom_call" | custom-call | bytes 6291456 | tf_op jit(solution)/shard_map/pack/pallas_call | solution.py:71
  18.7 1.7 %collective-permute-start.5 = (bf16[3,4,128,128]{3,2,1,0:T(8,128)(2,1)S(1)}, bf16[3,4,128,128]{3,2,1,0:T(8,128)(2,1)S(1)}, u32[]{:S(2)}, u32[]{:S(2)}) collective-permute-start(bf16[3,4,128,128]{3,2,1,0:T(8,128)(2,1)S(1)} %get-tuple-element.43), channel_id=1, source_target_pairs={{0,4},{1,5},{2,6},{3,7},{4,0},{5,1},{6,2},{7,3},{8,12},{9,13},{10,... | collective-permute-start | bytes 1179656 | tf_op jit(solution)/shard_map/ppermute | solution.py:445
  20.4 10.0 %collective-permute-done.1.refs_2_ = bf16[17,128,128]{2,1,0:T(8,128)(2,1)S(1)} collective-permute-done((bf16[17,128,128]{2,1,0:T(8,128)(2,1)S(1)}, bf16[17,128,128]{2,1,0:T(8,128)(2,1)S(1)}, u32[]{:S(2)}, u32[]{:S(2)}) %collective-permute-start.1) | collective-permute-done | bytes 557088 | tf_op jit(solution)/shard_map/ppermute | solution.py:458
  30.7 4.2 %collective-permute-start.2 = (bf16[17,128,128]{2,1,0:T(8,128)(2,1)S(1)}, bf16[17,128,128]{2,1,0:T(8,128)(2,1)S(1)}, u32[]{:S(2)}, u32[]{:S(2)}) collective-permute-start(bf16[17,128,128]{2,1,0:T(8,128)(2,1)S(1)} %get-tuple-element.37), channel_id=1, source_target_pairs={{0,4},{1,5},{2,6},{3,7},{8,12},{9,13},{10,14},{11,15},{16,20},{17,... | collective-permute-start | bytes 1671176 | tf_op jit(solution)/shard_map/ppermute | solution.py:458
  35.3 3.5 %collective-permute-done.4.rest_1_ = bf16[3,4,128,128]{3,2,1,0:T(8,128)(2,1)S(1)} collective-permute-done((bf16[3,4,128,128]{3,2,1,0:T(8,128)(2,1)S(1)}, bf16[3,4,128,128]{3,2,1,0:T(8,128)(2,1)S(1)}, u32[]{:S(2)}, u32[]{:S(2)}) %collective-permute-start.4) | collective-permute-done | bytes 393248 | tf_op jit(solution)/shard_map/ppermute | solution.py:445
  38.8 2.1 %collective-permute-start.11 = (bf16[3,4,128,128]{3,2,1,0:T(8,128)(2,1)S(1)}, bf16[3,4,128,128]{3,2,1,0:T(8,128)(2,1)S(1)}, u32[]{:S(2)}, u32[]{:S(2)}) collective-permute-start(bf16[3,4,128,128]{3,2,1,0:T(8,128)(2,1)S(1)} %get-tuple-element.50), channel_id=1, source_target_pairs={{0,2},{1,3},{2,0},{3,1},{4,6},{5,7},{6,4},{7,5},{8,10},{9,11},{10,... | collective-permute-start | bytes 1179656 | tf_op jit(solution)/shard_map/ppermute | solution.py:445
  40.8 1.5 %collective-permute-start.12 = (bf16[3,4,128,128]{3,2,1,0:T(8,128)(2,1)S(1)}, bf16[3,4,128,128]{3,2,1,0:T(8,128)(2,1)S(1)}, u32[]{:S(2)}, u32[]{:S(2)}) collective-permute-start(bf16[3,4,128,128]{3,2,1,0:T(8,128)(2,1)S(1)} %get-tuple-element.51), channel_id=1, source_target_pairs={{0,4},{1,5},{2,6},{3,7},{4,0},{5,1},{6,2},{7,3},{8,12},{9,13},{10,... | collective-permute-start | bytes 1179656 | tf_op jit(solution)/shard_map/ppermute | solution.py:445
  42.3 6.4 %collective-permute-done.6.rest_3_ = bf16[3,4,128,128]{3,2,1,0:T(8,128)(2,1)S(1)} collective-permute-done((bf16[3,4,128,128]{3,2,1,0:T(8,128)(2,1)S(1)}, bf16[3,4,128,128]{3,2,1,0:T(8,128)(2,1)S(1)}, u32[]{:S(2)}, u32[]{:S(2)}) %collective-permute-start.6) | collective-permute-done | bytes 393248 | tf_op jit(solution)/shard_map/ppermute | solution.py:445
  48.8 1.4 %collective-permute-start.13 = (bf16[3,4,128,128]{3,2,1,0:T(8,128)(2,1)S(1)}, bf16[3,4,128,128]{3,2,1,0:T(8,128)(2,1)S(1)}, u32[]{:S(2)}, u32[]{:S(2)}) collective-permute-start(bf16[3,4,128,128]{3,2,1,0:T(8,128)(2,1)S(1)} %get-tuple-element.52), channel_id=1, source_target_pairs={{0,6},{1,7},{2,4},{3,5},{4,2},{5,3},{6,0},{7,1},{8,14},{9,15},{10,... | collective-permute-start | bytes 1179656 | tf_op jit(solution)/shard_map/ppermute | solution.py:445
  50.2 14.4 %collective-permute-done.2.refs_3_ = bf16[17,128,128]{2,1,0:T(8,128)(2,1)S(1)} collective-permute-done((bf16[17,128,128]{2,1,0:T(8,128)(2,1)S(1)}, bf16[17,128,128]{2,1,0:T(8,128)(2,1)S(1)}, u32[]{:S(2)}, u32[]{:S(2)}) %collective-permute-start.2) | collective-permute-done | bytes 557088 | tf_op jit(solution)/shard_map/ppermute | solution.py:458
  64.9 0.6 collective-permute-start.3
  65.5 5.0 %collective-permute-done.12.rest_2_ = bf16[3,4,128,128]{3,2,1,0:T(8,128)(2,1)S(1)} collective-permute-done((bf16[3,4,128,128]{3,2,1,0:T(8,128)(2,1)S(1)}, bf16[3,4,128,128]{3,2,1,0:T(8,128)(2,1)S(1)}, u32[]{:S(2)}, u32[]{:S(2)}) %collective-permute-start.12) | collective-permute-done | bytes 393248 | tf_op jit(solution)/shard_map/ppermute | solution.py:445
  70.5 0.5 collective-permute-start.14
  71.6 0.7 collective-permute-done.9.rest_6_
  72.4 7.2 %attend.2 = (bf16[4,128,128]{2,1,0:T(8,128)(2,1)S(1)}, bf16[4,128,128]{2,1,0:T(8,128)(2,1)S(1)}, bf16[4,128,128]{2,1,0:T(8,128)(2,1)S(1)}, bf16[4,128,128]{2,1,0:T(8,128)(2,1)S(1)}) custom-call(s32[1]{0:T(128)} %bitcast.place_ref, s32[8,8]{1,0:T(8,128)S(1)} %copy-done.9, s32[8]{0:T(128)S(1)} %copy-done.10, ...), custom_call_target="tpu_custom_call" | custom-call | flops 536870912 | bytes 3670016 | tf_op jit(solution)/shard_map/attend/pallas_call | solution.py:158
  79.7 1.6 %collective-permute-start.18 = (bf16[4,128,128]{2,1,0:T(8,128)(2,1)S(1)}, bf16[4,128,128]{2,1,0:T(8,128)(2,1)S(1)}, u32[]{:S(2)}, u32[]{:S(2)}) collective-permute-start(bf16[4,128,128]{2,1,0:T(8,128)(2,1)S(1)} %get-tuple-element.54), channel_id=1, source_target_pairs={{0,2},{1,3},{2,0},{3,1},{4,6},{5,7},{6,4},{7,5},{8,10},{9,11},{10,... | collective-permute-start | bytes 393224 | tf_op jit(solution)/shard_map/ppermute | solution.py:474
  81.3 2.5 %collective-permute-start.20 = (bf16[4,128,128]{2,1,0:T(8,128)(2,1)S(1)}, bf16[4,128,128]{2,1,0:T(8,128)(2,1)S(1)}, u32[]{:S(2)}, u32[]{:S(2)}) collective-permute-start(bf16[4,128,128]{2,1,0:T(8,128)(2,1)S(1)} %get-tuple-element.56), channel_id=1, source_target_pairs={{0,4},{1,5},{2,6},{3,7},{4,0},{5,1},{6,2},{7,3},{8,12},{9,13},{10,... | collective-permute-start | bytes 393224 | tf_op jit(solution)/shard_map/ppermute | solution.py:474
  83.8 7.2 %attend.3 = (bf16[4,128,128]{2,1,0:T(8,128)(2,1)S(1)}, bf16[4,128,128]{2,1,0:T(8,128)(2,1)S(1)}, bf16[4,128,128]{2,1,0:T(8,128)(2,1)S(1)}, bf16[4,128,128]{2,1,0:T(8,128)(2,1)S(1)}) custom-call(s32[1]{0:T(128)} %bitcast.place_ref, s32[8,8]{1,0:T(8,128)S(1)} %copy-done.9, s32[8]{0:T(128)S(1)} %copy-done.10, ...), custom_call_target="tpu_custom_call" | custom-call | flops 536870912 | bytes 3670016 | tf_op jit(solution)/shard_map/attend/pallas_call | solution.py:158
  91.0 1.6 %collective-permute-start.19 = (bf16[4,128,128]{2,1,0:T(8,128)(2,1)S(1)}, bf16[4,128,128]{2,1,0:T(8,128)(2,1)S(1)}, u32[]{:S(2)}, u32[]{:S(2)}) collective-permute-start(bf16[4,128,128]{2,1,0:T(8,128)(2,1)S(1)} %get-tuple-element.55), channel_id=1, source_target_pairs={{0,2},{1,3},{2,0},{3,1},{4,6},{5,7},{6,4},{7,5},{8,10},{9,11},{10,... | collective-permute-start | bytes 393224 | tf_op jit(solution)/shard_map/ppermute | solution.py:474
  92.6 2.0 %collective-permute-start.21 = (bf16[4,128,128]{2,1,0:T(8,128)(2,1)S(1)}, bf16[4,128,128]{2,1,0:T(8,128)(2,1)S(1)}, u32[]{:S(2)}, u32[]{:S(2)}) collective-permute-start(bf16[4,128,128]{2,1,0:T(8,128)(2,1)S(1)} %get-tuple-element.57), channel_id=1, source_target_pairs={{0,4},{1,5},{2,6},{3,7},{4,0},{5,1},{6,2},{7,3},{8,12},{9,13},{10,... | collective-permute-start | bytes 393224 | tf_op jit(solution)/shard_map/ppermute | solution.py:474
  94.6 5.0 %within.1.inner_ref = f32[32,128,128]{2,1,0:T(8,128)S(1)} custom-call(bf16[128,32,128]{2,1,0:T(8,128)(2,1)S(1)} %copy-done, bf16[128,32,128]{2,1,0:T(8,128)(2,1)S(1)} %copy-done.2, bf16[128,32,128]{2,1,0:T(8,128)(2,1)S(1)} %copy-done.4, bf16[128,32]{1,0:T(8,128)(2,1)S(1)} %copy.14.decay_ref), custom_call_target="tpu_custom_call" | custom-call | flops 268435456 | bytes 5242880 | tf_op jit(solution)/shard_map/within/pallas_call | solution.py:260
  99.7 0.8 collective-permute-done.23.rest_7_
  100.4 1.4 %unpack.1 = bf16[128,32,128]{2,1,0:T(8,128)(2,1)} custom-call(s32[1]{0:T(128)} %bitcast.place_ref, bf16[4,128,128]{2,1,0:T(8,128)(2,1)S(1)} %get-tuple-element.48.rest_0_, bf16[4,128,128]{2,1,0:T(8,128)(2,1)S(1)} %get-tuple-element.53.rest_1_, bf16[4,128,128]{2,1,0:T(8,128)(2,1)S(1)} %collective-permute-done.18.rest_2_, ...), custom_call_target="tpu_custom_call" | custom-call | bytes 2097152 | tf_op jit(solution)/shard_map/unpack/pallas_call | solution.py:196
  101.9 3.4 %finish.1 = bf16[128,32,128]{2,1,0:T(8,128)(2,1)} custom-call(s32[1]{0:T(128)} %bitcast.place_ref, bf16[128,32,128]{2,1,0:T(8,128)(2,1)S(1)} %copy-done, bf16[128,32]{1,0:T(8,128)(2,1)S(1)} %copy.14.decay_ref, f32[32,128]{1,0:T(8,128)S(1)} %bitcast.2, f32[32,128,128]{2,1,0:T(8,128)S(1)} %within.1.inner_ref, ...), custom_call_target="tpu_custom_call" | custom-call | flops 268435456 | bytes 10485760 | tf_op jit(solution)/shard_map/finish/pallas_call | solution.py:408
  (49 shorter events, 2.2 us)
Async XLA Ops:
  7.4 4.5 %collective-permute-start = (f32[33,128,128]{2,1,0:T(8,128)}, f32[33,128,128]{2,1,0:T(8,128)S(1)}, u32[]{:S(2)}, u32[]{:S(2)}) collective-permute-start(f32[33,128,128]{2,1,0:T(8,128)} %block_state.1.own_ref), channel_id=1, source_target_pairs={{0,1},{1,0},{2,3},{3,2},{4,5},{5,4},{6,7},{7,6},{8,9},{9,8},{10,11... | collective-permute-start | bytes 6488072 | tf_op jit(solution)/shard_map/ppermute | solution.py:449
  11.9 5.0 %copy-start.6 = (bf16[128,32,128]{2,1,0:T(8,128)(2,1)S(1)}, bf16[128,32,128]{2,1,0:T(8,128)(2,1)}, u32[]{:S(2)}) copy-start(bf16[128,32,128]{2,1,0:T(8,128)(2,1)} %k_ref.5) | copy-start | bytes 3145732
  11.9 5.0 %copy-start.7 = (bf16[128,32,128]{2,1,0:T(8,128)(2,1)S(1)}, bf16[128,32,128]{2,1,0:T(8,128)(2,1)}, u32[]{:S(2)}) copy-start(bf16[128,32,128]{2,1,0:T(8,128)(2,1)} %v_ref.5) | copy-start | bytes 3145732
  14.0 16.3 %collective-permute-start.1 = (bf16[17,128,128]{2,1,0:T(8,128)(2,1)S(1)}, bf16[17,128,128]{2,1,0:T(8,128)(2,1)S(1)}, u32[]{:S(2)}, u32[]{:S(2)}) collective-permute-start(bf16[17,128,128]{2,1,0:T(8,128)(2,1)S(1)} %get-tuple-element.33), channel_id=1, source_target_pairs={{0,2},{1,3},{2,0},{3,1},{4,6},{5,7},{6,4},{7,5},{8,10},{9,11},{10,... | collective-permute-start | bytes 1671176 | tf_op jit(solution)/shard_map/ppermute | solution.py:458
  18.3 20.5 %collective-permute-start.4 = (bf16[3,4,128,128]{3,2,1,0:T(8,128)(2,1)S(1)}, bf16[3,4,128,128]{3,2,1,0:T(8,128)(2,1)S(1)}, u32[]{:S(2)}, u32[]{:S(2)}) collective-permute-start(bf16[3,4,128,128]{3,2,1,0:T(8,128)(2,1)S(1)} %get-tuple-element.40), channel_id=1, source_target_pairs={{0,2},{1,3},{2,0},{3,1},{4,6},{5,7},{6,4},{7,5},{8,10},{9,11},{10,... | collective-permute-start | bytes 1179656 | tf_op jit(solution)/shard_map/ppermute | solution.py:445
  18.7 22.2 %collective-permute-start.5 = (bf16[3,4,128,128]{3,2,1,0:T(8,128)(2,1)S(1)}, bf16[3,4,128,128]{3,2,1,0:T(8,128)(2,1)S(1)}, u32[]{:S(2)}, u32[]{:S(2)}) collective-permute-start(bf16[3,4,128,128]{3,2,1,0:T(8,128)(2,1)S(1)} %get-tuple-element.43), channel_id=1, source_target_pairs={{0,4},{1,5},{2,6},{3,7},{4,0},{5,1},{6,2},{7,3},{8,12},{9,13},{10,... | collective-permute-start | bytes 1179656 | tf_op jit(solution)/shard_map/ppermute | solution.py:445
  30.7 41.7 %copy-start.9 = (s32[8,8]{1,0:T(8,128)S(1)}, s32[8,8]{1,0:T(8,128)}, u32[]{:S(2)}) copy-start(s32[8,8]{1,0:T(8,128)} %bits_ref.3) | copy-start | bytes 772
  30.7 41.7 %copy-start.10 = (s32[8]{0:T(128)S(1)}, s32[8]{0:T(128)}, u32[]{:S(2)}) copy-start(s32[8]{0:T(128)} %agents_ref.3) | copy-start | bytes 100
  30.7 33.9 %collective-permute-start.2 = (bf16[17,128,128]{2,1,0:T(8,128)(2,1)S(1)}, bf16[17,128,128]{2,1,0:T(8,128)(2,1)S(1)}, u32[]{:S(2)}, u32[]{:S(2)}) collective-permute-start(bf16[17,128,128]{2,1,0:T(8,128)(2,1)S(1)} %get-tuple-element.37), channel_id=1, source_target_pairs={{0,4},{1,5},{2,6},{3,7},{8,12},{9,13},{10,14},{11,15},{16,20},{17,... | collective-permute-start | bytes 1671176 | tf_op jit(solution)/shard_map/ppermute | solution.py:458
  34.9 13.8 %collective-permute-start.6 = (bf16[3,4,128,128]{3,2,1,0:T(8,128)(2,1)S(1)}, bf16[3,4,128,128]{3,2,1,0:T(8,128)(2,1)S(1)}, u32[]{:S(2)}, u32[]{:S(2)}) collective-permute-start(bf16[3,4,128,128]{3,2,1,0:T(8,128)(2,1)S(1)} %get-tuple-element.46), channel_id=1, source_target_pairs={{0,6},{1,7},{2,4},{3,5},{4,2},{5,3},{6,0},{7,1},{8,14},{9,15},{10,... | collective-permute-start | bytes 1179656 | tf_op jit(solution)/shard_map/ppermute | solution.py:445
  35.3 29.6 %collective-permute-start.7 = (bf16[3,4,128,128]{3,2,1,0:T(8,128)(2,1)S(1)}, bf16[3,4,128,128]{3,2,1,0:T(8,128)(2,1)S(1)}, u32[]{:S(2)}, u32[]{:S(2)}) collective-permute-start(bf16[3,4,128,128]{3,2,1,0:T(8,128)(2,1)S(1)} %get-tuple-element.38.rest_0_), channel_id=1, source_target_pairs={{0,1},{1,0},{2,3},{3,2},{4,5},{5,4},{6,7},{7,6},{8,9},{9,8},{10,11... | collective-permute-start | bytes 1179656 | tf_op jit(solution)/shard_map/ppermute | solution.py:471
  38.8 26.7 %collective-permute-start.11 = (bf16[3,4,128,128]{3,2,1,0:T(8,128)(2,1)S(1)}, bf16[3,4,128,128]{3,2,1,0:T(8,128)(2,1)S(1)}, u32[]{:S(2)}, u32[]{:S(2)}) collective-permute-start(bf16[3,4,128,128]{3,2,1,0:T(8,128)(2,1)S(1)} %get-tuple-element.50), channel_id=1, source_target_pairs={{0,2},{1,3},{2,0},{3,1},{4,6},{5,7},{6,4},{7,5},{8,10},{9,11},{10,... | collective-permute-start | bytes 1179656 | tf_op jit(solution)/shard_map/ppermute | solution.py:445
  40.8 29.7 %collective-permute-start.12 = (bf16[3,4,128,128]{3,2,1,0:T(8,128)(2,1)S(1)}, bf16[3,4,128,128]{3,2,1,0:T(8,128)(2,1)S(1)}, u32[]{:S(2)}, u32[]{:S(2)}) collective-permute-start(bf16[3,4,128,128]{3,2,1,0:T(8,128)(2,1)S(1)} %get-tuple-element.51), channel_id=1, source_target_pairs={{0,4},{1,5},{2,6},{3,7},{4,0},{5,1},{6,2},{7,3},{8,12},{9,13},{10,... | collective-permute-start | bytes 1179656 | tf_op jit(solution)/shard_map/ppermute | solution.py:445
  48.8 21.8 %collective-permute-start.13 = (bf16[3,4,128,128]{3,2,1,0:T(8,128)(2,1)S(1)}, bf16[3,4,128,128]{3,2,1,0:T(8,128)(2,1)S(1)}, u32[]{:S(2)}, u32[]{:S(2)}) collective-permute-start(bf16[3,4,128,128]{3,2,1,0:T(8,128)(2,1)S(1)} %get-tuple-element.52), channel_id=1, source_target_pairs={{0,6},{1,7},{2,4},{3,5},{4,2},{5,3},{6,0},{7,1},{8,14},{9,15},{10,... | collective-permute-start | bytes 1179656 | tf_op jit(solution)/shard_map/ppermute | solution.py:445
  64.6 6.4 %collective-permute-start.10 = (bf16[3,4,128,128]{3,2,1,0:T(8,128)(2,1)S(1)}, bf16[3,4,128,128]{3,2,1,0:T(8,128)(2,1)S(1)}, u32[]{:S(2)}, u32[]{:S(2)}) collective-permute-start(bf16[3,4,128,128]{3,2,1,0:T(8,128)(2,1)S(1)} %collective-permute-done.6.rest_3_), channel_id=1, source_target_pairs={{0,1},{1,0},{2,3},{3,2},{4,5},{5,4},{6,7},{7,6},{8,9},{9,8},{10,11... | collective-permute-start | bytes 1179656 | tf_op jit(solution)/shard_map/ppermute | solution.py:471
  64.9 37.0 %collective-permute-start.3 = (f32[16,128,128]{2,1,0:T(8,128)S(1)}, f32[16,128,128]{2,1,0:T(8,128)S(1)}, u32[]{:S(2)}, u32[]{:S(2)}) collective-permute-start(f32[16,128,128]{2,1,0:T(8,128)S(1)} %climb.3.own_ref), channel_id=1, source_target_pairs={{0,1},{1,0},{2,3},{3,2},{4,5},{5,4},{6,7},{7,6},{8,9},{9,8},{10,11... | collective-permute-start | bytes 3145736 | tf_op jit(solution)/shard_map/ppermute | solution.py:463
  65.4 5.7 %collective-permute-start.8 = (bf16[3,4,128,128]{3,2,1,0:T(8,128)(2,1)S(1)}, bf16[3,4,128,128]{3,2,1,0:T(8,128)(2,1)S(1)}, u32[]{:S(2)}, u32[]{:S(2)}) collective-permute-start(bf16[3,4,128,128]{3,2,1,0:T(8,128)(2,1)S(1)} %collective-permute-done.4.rest_1_), channel_id=1, source_target_pairs={{0,1},{1,0},{2,3},{3,2},{4,5},{5,4},{6,7},{7,6},{8,9},{9,8},{10,11... | collective-permute-start | bytes 1179656 | tf_op jit(solution)/shard_map/ppermute | solution.py:471
  70.5 1.7 %collective-permute-start.9 = (bf16[3,4,128,128]{3,2,1,0:T(8,128)(2,1)S(1)}, bf16[3,4,128,128]{3,2,1,0:T(8,128)(2,1)S(1)}, u32[]{:S(2)}, u32[]{:S(2)}) collective-permute-start(bf16[3,4,128,128]{3,2,1,0:T(8,128)(2,1)S(1)} %collective-permute-done.5.rest_2_), channel_id=1, source_target_pairs={{0,1},{1,0},{2,3},{3,2},{4,5},{5,4},{6,7},{7,6},{8,9},{9,8},{10,11... | collective-permute-start | bytes 1179656 | tf_op jit(solution)/shard_map/ppermute | solution.py:471
  70.5 9.1 %collective-permute-start.14 = (bf16[3,4,128,128]{3,2,1,0:T(8,128)(2,1)S(1)}, bf16[3,4,128,128]{3,2,1,0:T(8,128)(2,1)S(1)}, u32[]{:S(2)}, u32[]{:S(2)}) collective-permute-start(bf16[3,4,128,128]{3,2,1,0:T(8,128)(2,1)S(1)} %get-tuple-element.49.rest_0_), channel_id=1, source_target_pairs={{0,1},{1,0},{2,3},{3,2},{4,5},{5,4},{6,7},{7,6},{8,9},{9,8},{10,11... | collective-permute-start | bytes 1179656 | tf_op jit(solution)/shard_map/ppermute | solution.py:471
  71.0 10.2 %collective-permute-start.15 = (bf16[3,4,128,128]{3,2,1,0:T(8,128)(2,1)S(1)}, bf16[3,4,128,128]{3,2,1,0:T(8,128)(2,1)S(1)}, u32[]{:S(2)}, u32[]{:S(2)}) collective-permute-start(bf16[3,4,128,128]{3,2,1,0:T(8,128)(2,1)S(1)} %collective-permute-done.11.rest_1_), channel_id=1, source_target_pairs={{0,1},{1,0},{2,3},{3,2},{4,5},{5,4},{6,7},{7,6},{8,9},{9,8},{10,11... | collective-permute-start | bytes 1179656 | tf_op jit(solution)/shard_map/ppermute | solution.py:471
  71.1 12.6 %collective-permute-start.16 = (bf16[3,4,128,128]{3,2,1,0:T(8,128)(2,1)S(1)}, bf16[3,4,128,128]{3,2,1,0:T(8,128)(2,1)S(1)}, u32[]{:S(2)}, u32[]{:S(2)}) collective-permute-start(bf16[3,4,128,128]{3,2,1,0:T(8,128)(2,1)S(1)} %collective-permute-done.12.rest_2_), channel_id=1, source_target_pairs={{0,1},{1,0},{2,3},{3,2},{4,5},{5,4},{6,7},{7,6},{8,9},{9,8},{10,11... | collective-permute-start | bytes 1179656 | tf_op jit(solution)/shard_map/ppermute | solution.py:471
  72.2 11.5 %collective-permute-start.17 = (bf16[3,4,128,128]{3,2,1,0:T(8,128)(2,1)S(1)}, bf16[3,4,128,128]{3,2,1,0:T(8,128)(2,1)S(1)}, u32[]{:S(2)}, u32[]{:S(2)}) collective-permute-start(bf16[3,4,128,128]{3,2,1,0:T(8,128)(2,1)S(1)} %collective-permute-done.13.rest_3_), channel_id=1, source_target_pairs={{0,1},{1,0},{2,3},{3,2},{4,5},{5,4},{6,7},{7,6},{8,9},{9,8},{10,11... | collective-permute-start | bytes 1179656 | tf_op jit(solution)/shard_map/ppermute | solution.py:471
  79.6 15.0 %copy-start = (bf16[128,32,128]{2,1,0:T(8,128)(2,1)S(1)}, bf16[128,32,128]{2,1,0:T(8,128)(2,1)}, u32[]{:S(2)}) copy-start(bf16[128,32,128]{2,1,0:T(8,128)(2,1)} %q_ref.4) | copy-start | bytes 3145732
  79.7 15.0 %copy-start.2 = (bf16[128,32,128]{2,1,0:T(8,128)(2,1)S(1)}, bf16[128,32,128]{2,1,0:T(8,128)(2,1)}, u32[]{:S(2)}) copy-start(bf16[128,32,128]{2,1,0:T(8,128)(2,1)} %k_ref.4) | copy-start | bytes 3145732
  79.7 15.0 %copy-start.4 = (bf16[128,32,128]{2,1,0:T(8,128)(2,1)S(1)}, bf16[128,32,128]{2,1,0:T(8,128)(2,1)}, u32[]{:S(2)}) copy-start(bf16[128,32,128]{2,1,0:T(8,128)(2,1)} %v_ref.4) | copy-start | bytes 3145732
  79.7 12.9 %collective-permute-start.18 = (bf16[4,128,128]{2,1,0:T(8,128)(2,1)S(1)}, bf16[4,128,128]{2,1,0:T(8,128)(2,1)S(1)}, u32[]{:S(2)}, u32[]{:S(2)}) collective-permute-start(bf16[4,128,128]{2,1,0:T(8,128)(2,1)S(1)} %get-tuple-element.54), channel_id=1, source_target_pairs={{0,2},{1,3},{2,0},{3,1},{4,6},{5,7},{6,4},{7,5},{8,10},{9,11},{10,... | collective-permute-start | bytes 393224 | tf_op jit(solution)/shard_map/ppermute | solution.py:474
  81.3 13.3 %collective-permute-start.20 = (bf16[4,128,128]{2,1,0:T(8,128)(2,1)S(1)}, bf16[4,128,128]{2,1,0:T(8,128)(2,1)S(1)}, u32[]{:S(2)}, u32[]{:S(2)}) collective-permute-start(bf16[4,128,128]{2,1,0:T(8,128)(2,1)S(1)} %get-tuple-element.56), channel_id=1, source_target_pairs={{0,4},{1,5},{2,6},{3,7},{4,0},{5,1},{6,2},{7,3},{8,12},{9,13},{10,... | collective-permute-start | bytes 393224 | tf_op jit(solution)/shard_map/ppermute | solution.py:474
  83.7 15.9 %collective-permute-start.22 = (bf16[4,128,128]{2,1,0:T(8,128)(2,1)S(1)}, bf16[4,128,128]{2,1,0:T(8,128)(2,1)S(1)}, u32[]{:S(2)}, u32[]{:S(2)}) collective-permute-start(bf16[4,128,128]{2,1,0:T(8,128)(2,1)S(1)} %get-tuple-element.58), channel_id=1, source_target_pairs={{0,6},{1,7},{2,4},{3,5},{4,2},{5,3},{6,0},{7,1},{8,14},{9,15},{10,... | collective-permute-start | bytes 393224 | tf_op jit(solution)/shard_map/ppermute | solution.py:474
  91.0 8.6 %collective-permute-start.19 = (bf16[4,128,128]{2,1,0:T(8,128)(2,1)S(1)}, bf16[4,128,128]{2,1,0:T(8,128)(2,1)S(1)}, u32[]{:S(2)}, u32[]{:S(2)}) collective-permute-start(bf16[4,128,128]{2,1,0:T(8,128)(2,1)S(1)} %get-tuple-element.55), channel_id=1, source_target_pairs={{0,2},{1,3},{2,0},{3,1},{4,6},{5,7},{6,4},{7,5},{8,10},{9,11},{10,... | collective-permute-start | bytes 393224 | tf_op jit(solution)/shard_map/ppermute | solution.py:474
  92.6 7.1 %collective-permute-start.21 = (bf16[4,128,128]{2,1,0:T(8,128)(2,1)S(1)}, bf16[4,128,128]{2,1,0:T(8,128)(2,1)S(1)}, u32[]{:S(2)}, u32[]{:S(2)}) collective-permute-start(bf16[4,128,128]{2,1,0:T(8,128)(2,1)S(1)} %get-tuple-element.57), channel_id=1, source_target_pairs={{0,4},{1,5},{2,6},{3,7},{4,0},{5,1},{6,2},{7,3},{8,12},{9,13},{10,... | collective-permute-start | bytes 393224 | tf_op jit(solution)/shard_map/ppermute | solution.py:474
  94.6 7.3 %copy-start.8 = (f32[4096]{0:T(1024)S(1)}, f32[4096]{0:T(1024)}, u32[]{:S(2)}) copy-start(f32[4096]{0:T(1024)} %param.14) | copy-start | bytes 49156
  94.6 5.9 %collective-permute-start.23 = (bf16[4,128,128]{2,1,0:T(8,128)(2,1)S(1)}, bf16[4,128,128]{2,1,0:T(8,128)(2,1)S(1)}, u32[]{:S(2)}, u32[]{:S(2)}) collective-permute-start(bf16[4,128,128]{2,1,0:T(8,128)(2,1)S(1)} %get-tuple-element.59), channel_id=1, source_target_pairs={{0,6},{1,7},{2,4},{3,5},{4,2},{5,3},{6,0},{7,1},{8,14},{9,15},{10,... | collective-permute-start | bytes 393224 | tf_op jit(solution)/shard_map/ppermute | solution.py:474
  (3 other events, 7.5 us)

commit v2 on v1

v2 whole, which is shorter than its diff:
```python
import jax
import jax.numpy as jnp
from jax import lax
from jax.experimental import pallas as pl
from jax.experimental.pallas import tpu as pltpu
from jax.sharding import PartitionSpec as P

EPSILON = 1e-06
PAIR = 2
PARTS = 2
TURN = 8
BUSY = 16
LOG_ROWS = 16
LOG2E = 1.4426950408889634
VMEM = pl.BlockSpec(memory_space=pltpu.VMEM)
SMEM = pl.BlockSpec(memory_space=pltpu.SMEM)
ANY = pl.BlockSpec(memory_space=pl.ANY)


def params(mib):
    return pltpu.CompilerParams(vmem_limit_bytes=mib << 20)


def cost(flops, nbytes, exps=0):
    return pl.CostEstimate(flops=BUSY * flops, bytes_accessed=nbytes, transcendentals=exps)


def shape(dims, dtype):
    return jax.ShapeDtypeStruct(dims, dtype)


def turns(heads):
    step = min(TURN, heads)
    return [(at, step) for at in range(0, heads, step)]


def span_of(index, rows):
    return pl.ds(index * rows, rows)


def nt(a, b):
    return lax.dot_general(a, b, (((1,), (1,)), ((), ())), preferred_element_type=jnp.float32)


def tn(a, b):
    return lax.dot_general(a, b, (((0,), (0,)), ((), ())), preferred_element_type=jnp.float32)


def nn(a, b):
    return lax.dot_general(a, b, (((1,), (0,)), ((), ())), preferred_element_type=jnp.float32)


def triangle(size):
    rows = lax.broadcasted_iota(jnp.int32, (size, size), 0)
    cols = lax.broadcasted_iota(jnp.int32, (size, size), 1)
    return cols <= rows


def pack(place, arrays, chips, hosted, parts, extra):
    rows, heads, width = arrays[0].shape
    each = hosted // parts
    pieces = 2
    cut = rows // pieces

    def kernel(place_ref, q_ref, k_ref, v_ref, *rest):
        outs, (landed, turned, sems) = rest[:-3], rest[-3:]
        copies = [
            pltpu.make_async_copy(
                ref.at[pl.ds(piece * cut, cut)],
                landed.at[which, pl.ds(piece * cut, cut)],
                sems.at[which, piece],
            )
            for which, ref in enumerate((q_ref, k_ref, v_ref))
            for piece in range(pieces)
        ]
        for copy in copies:
            copy.start()
        for which in range(3):
            for piece in range(pieces):
                copies[which * pieces + piece].wait()
                span = slice(piece * cut, (piece + 1) * cut)
                for at, step in turns(heads):
                    turned[which, at : at + step, span, :] = jnp.swapaxes(
                        landed[which, span, at : at + step, :], 0, 1
                    )
        chip = place_ref[0] // PAIR
        for m in range(chips):
            first = (chip ^ m) * hosted
            for part in range(parts):
                out_ref = outs[m * parts + part]
                for which in range(3):
                    for h in range(each):
                        out_ref[span_of(which * each + h, rows)] = turned[which, first + part * each + h]
                if part == parts - 1:
                    out_ref[3 * each * rows :] = jnp.zeros((extra, width), jnp.bfloat16)

    out_shape = [
        shape((3 * each * rows + (extra if part == parts - 1 else 0), width), jnp.bfloat16)
        for m in range(chips)
        for part in range(parts)
    ]
    outs = pl.pallas_call(
        kernel,
        out_shape=out_shape,
        in_specs=[SMEM, ANY, ANY, ANY],
        out_specs=[VMEM] * (chips * parts),
        scratch_shapes=[
            pltpu.VMEM((3, rows, heads, width), jnp.bfloat16),
            pltpu.VMEM((3, heads, rows, width), jnp.bfloat16),
            pltpu.SemaphoreType.DMA((3, pieces)),
        ],
        compiler_params=params(56),
        cost_estimate=cost(0, 12 * rows * heads * width),
        name="pack",
    )(place, *arrays)
    return [outs[m * parts : (m + 1) * parts] for m in range(chips)]


def attend(place, bits, agents, own, other, each, rows, extra):
    chips = len(own)
    width = own[0].shape[-1]
    slots = PAIR * chips
    scale = width**-0.5 * LOG2E
    sent = 3 * each * rows

    def kernel(place_ref, bits_ref, agents_ref, *rest):
        ins, outs = rest[:slots], rest[slots : slots + chips]
        held, scores, top, total, mixed, done, sems = rest[slots + chips :]
        me = place_ref[0]
        chip, core = me // PAIR, me % PAIR
        copies = [
            pltpu.make_async_copy(ins[j].at[pl.ds(0, sent)], held.at[j], sems.at[j]) for j in range(slots)
        ]
        for copy in copies:
            copy.start()
        for copy in copies:
            copy.wait()
        lower = triangle(rows)

        def head(j, which, h):
            return held[j, span_of(which * each + h, rows)]

        def block_of(j):
            return PAIR * (chip ^ (j % chips)) + jnp.where(j < chips, core, PAIR - 1 - core)

        def sees(query_block, j):
            key_block = block_of(j)
            open_ = (bits_ref[query_block, key_block] == 1) | (
                agents_ref[query_block] == agents_ref[key_block]
            )
            return (key_block < query_block) & open_

        def one_query(i, carry):
            query_block = block_of(i)
            for h in range(each):
                s = jnp.where(lower, nt(head(i, 0, h), head(i, 1, h)), -1e30)
                scores[slots, h] = s
                top[h] = s

            def score(j, carry):
                @pl.when(sees(query_block, j))
                def _():
                    for h in range(each):
                        s = nt(head(i, 0, h), head(j, 1, h))
                        scores[j, h] = s
                        top[h] = jnp.maximum(top[h], s)

                return carry

            lax.fori_loop(0, slots, score, 0)
            for h in range(each):
                summit = jnp.max(top[h], axis=1, keepdims=True)
                top[h] = jnp.broadcast_to(summit, (rows, rows))
                p = jnp.exp2((scores[slots, h] - summit) * scale)
                total[h] = p
                mixed[h] = nn(p.astype(jnp.bfloat16), head(i, 2, h))

            def weigh(j, carry):
                @pl.when(sees(query_block, j))
                def _():
                    for h in range(each):
                        p = jnp.exp2((scores[j, h] - top[h]) * scale)
                        total[h] += p
                        mixed[h] += nn(p.astype(jnp.bfloat16), head(j, 2, h))

                return carry

            lax.fori_loop(0, slots, weigh, 0)
            for h in range(each):
                sums = jnp.sum(total[h], axis=1, keepdims=True)
                done[i, h] = (mixed[h] / sums).astype(jnp.bfloat16)
            return carry

        lax.fori_loop(0, chips, one_query, 0)
        for m in range(chips):
            for h in range(each):
                outs[m][span_of(h, rows)] = done[m, h]
            if extra:
                outs[m][each * rows :] = jnp.zeros((extra, width), jnp.bfloat16)

    pairs = chips * slots // 2
    return pl.pallas_call(
        kernel,
        out_shape=[shape((each * rows + extra, width), jnp.bfloat16)] * chips,
        in_specs=[SMEM, SMEM, SMEM] + [ANY] * slots,
        out_specs=[VMEM] * chips,
        scratch_shapes=[
            pltpu.VMEM((slots, sent, width), jnp.bfloat16),
            pltpu.VMEM((slots + 1, each, rows, rows), jnp.float32),
            pltpu.VMEM((each, rows, rows), jnp.float32),
            pltpu.VMEM((each, rows, rows), jnp.float32),
            pltpu.VMEM((each, rows, width), jnp.float32),
            pltpu.VMEM((chips, each, rows, width), jnp.bfloat16),
            pltpu.SemaphoreType.DMA((slots,)),
        ],
        compiler_params=params(24),
        cost_estimate=cost(
            4 * pairs * each * rows * rows * width,
            2 * (3 * slots + chips) * each * rows * width,
            pairs * each * rows * rows,
        ),
        name="attend",
    )(place, bits, agents, *own, *other)


def unpack(place, pieces, heads, rows, each):
    chips, parts = len(pieces), len(pieces[0])
    width = pieces[0][0].shape[-1]

    def kernel(place_ref, *rest):
        ins, out_ref, turned = rest[:-2], rest[-2], rest[-1]
        chip = place_ref[0] // PAIR
        for m in range(chips):
            for part in range(parts):
                first = (chip ^ m) * (each * parts) + part * each
                for h in range(each):
                    turned[first + h] = ins[m * parts + part][span_of(h, rows)]
        for at, step in turns(heads):
            out_ref[:, at : at + step, :] = jnp.swapaxes(turned[at : at + step], 0, 1)

    return pl.pallas_call(
        kernel,
        out_shape=shape((rows, heads, width), jnp.bfloat16),
        in_specs=[SMEM] + [VMEM] * (chips * parts),
        out_specs=VMEM,
        scratch_shapes=[pltpu.VMEM((heads, rows, width), jnp.bfloat16)],
        compiler_params=params(16),
        cost_estimate=cost(0, 4 * rows * heads * width),
        name="unpack",
    )(place, *[piece for row in pieces for piece in row])


def decay_sums(decay_ref):
    decay = decay_ref[...]
    lower = triangle(decay.shape[0]).astype(jnp.bfloat16)
    return nn(lower, decay), lax.dot_general(
        decay, lower, (((0,), (1,)), ((), ())), preferred_element_type=jnp.float32
    )


def block_state(keys, values, decay):
    rows, heads, width = keys.shape

    def kernel(k_ref, v_ref, decay_ref, out_ref):
        cumul, _ = decay_sums(decay_ref)
        last = cumul[rows - 1 : rows, :]
        left = jnp.exp(last - cumul)
        for at, step in turns(heads):
            k = jnp.swapaxes(k_ref[:, at : at + step, :], 0, 1)
            v = jnp.swapaxes(v_ref[:, at : at + step, :], 0, 1)
            for h in range(step):
                kept = k[h].astype(jnp.float32) * left[:, at + h : at + h + 1]
                out_ref[at + h] = tn(kept.astype(jnp.bfloat16), v[h])
        out_ref[heads] = jnp.zeros((width, width), jnp.float32)
        out_ref[heads, 0:1, 0:heads] = last

    return pl.pallas_call(
        kernel,
        out_shape=shape((heads + 1, width, width), jnp.float32),
        in_specs=[VMEM] * 3,
        out_specs=VMEM,
        compiler_params=params(24),
        cost_estimate=cost(2 * heads * rows * width * width, 8 * rows * heads * width),
        name="block_state",
    )(keys, values, decay)


def within(queries, keys, values, decay):
    rows, heads, width = queries.shape

    def kernel(q_ref, k_ref, v_ref, decay_ref, out_ref):
        cumul, cumul_row = decay_sums(decay_ref)
        lower = triangle(rows)
        for at, step in turns(heads):
            q = jnp.swapaxes(q_ref[:, at : at + step, :], 0, 1)
            k = jnp.swapaxes(k_ref[:, at : at + step, :], 0, 1)
            v = jnp.swapaxes(v_ref[:, at : at + step, :], 0, 1)
            for h in range(step):
                i = at + h
                apart = cumul[:, i : i + 1] - cumul_row[i : i + 1, :]
                damping = jnp.where(lower, jnp.exp(jnp.where(lower, apart, 0.0)), 0.0)
                weights = (nt(q[h], k[h]) * damping).astype(jnp.bfloat16)
                out_ref[i] = nn(weights, v[h])

    return pl.pallas_call(
        kernel,
        out_shape=shape((heads, rows, width), jnp.float32),
        in_specs=[VMEM] * 4,
        out_specs=VMEM,
        compiler_params=params(24),
        cost_estimate=cost(4 * heads * rows * rows * width, 10 * rows * heads * width, heads * rows * rows),
        name="within",
    )(queries, keys, values, decay)


def join_cores(place, own, other, payloads, at_row):
    heads, width = own.shape[0] - 1, own.shape[-1]
    chips = len(payloads)
    half = heads // PAIR
    few = half // chips
    extra = few * width + LOG_ROWS

    def kernel(place_ref, own_ref, other_ref, *rest):
        outs, totals, staged, sems = rest[chips : 2 * chips], *rest[2 * chips :]
        core, chip = place_ref[0] % PAIR, place_ref[0] // PAIR
        own_logs, other_logs = own_ref[heads, 0:1, :], other_ref[heads, 0:1, :]
        logs = own_logs + other_logs
        later = jnp.exp(jnp.where(core == 0, other_logs, own_logs))
        own_factor = jnp.where(core == 0, later, 1.0)
        other_factor = jnp.where(core == 0, 1.0, later)
        for h in range(half):
            at = core * half + h
            own_by = jnp.where(core == 0, own_factor[:, h : h + 1], own_factor[:, half + h : half + h + 1])
            other_by = jnp.where(
                core == 0, other_factor[:, h : h + 1], other_factor[:, half + h : half + h + 1]
            )
            totals[h] = (own_ref[at] * own_by + other_ref[at] * other_by).astype(jnp.bfloat16)
        first = logs.astype(jnp.bfloat16).astype(jnp.float32)
        second = (logs - first).astype(jnp.bfloat16).astype(jnp.float32)
        third = logs - first - second
        row = lax.broadcasted_iota(jnp.int32, (LOG_ROWS, width), 0)
        split = jnp.where(row == 0, first, jnp.where(row == 1, second, jnp.where(row == 2, third, 0.0)))
        copies = []
        for m in range(chips):
            for h in range(few):
                staged[m, span_of(h, width)] = totals[(chip ^ m) * few + h]
            staged[m, few * width :] = split.astype(jnp.bfloat16)
            copies.append(
                pltpu.make_async_copy(staged.at[m], outs[m].at[pl.ds(at_row, extra)], sems.at[m])
            )
            copies[-1].start()
        for copy in copies:
            copy.wait()

    return pl.pallas_call(
        kernel,
        out_shape=[shape(payload.shape, payload.dtype) for payload in payloads],
        in_specs=[SMEM, VMEM, VMEM] + [ANY] * chips,
        out_specs=[ANY] * chips,
        scratch_shapes=[
            pltpu.VMEM((half, width, width), jnp.bfloat16),
            pltpu.VMEM((chips, extra, width), jnp.bfloat16),
            pltpu.SemaphoreType.DMA((chips,)),
        ],
        input_output_aliases={3 + m: m for m in range(chips)},
        compiler_params=params(24),
        cost_estimate=cost(3 * half * width * width, 14 * half * width * width),
        name="join_cores",
    )(place, own, other, *payloads)


def scan_chips(place, arrived, from_row, payloads, to_row, few, heads):
    chips = len(arrived)
    width = arrived[0].shape[-1]
    half = heads // PAIR
    extra = few * width + LOG_ROWS

    def kernel(place_ref, *rest):
        ins, outs = rest[:chips], rest[2 * chips : 3 * chips]
        got, given, state, in_sems, out_sems = rest[3 * chips :]
        core, chip = place_ref[0] % PAIR, place_ref[0] // PAIR
        copies = [
            pltpu.make_async_copy(ins[m].at[pl.ds(from_row, extra)], got.at[m], in_sems.at[m])
            for m in range(chips)
        ]
        for copy in copies:
            copy.start()
        for copy in copies:
            copy.wait()
        state[...] = jnp.zeros_like(state)
        column = lax.broadcasted_iota(jnp.int32, (1, width), 1)
        first = core * half + chip * few

        def one_chip(c, carry):
            m = c ^ chip
            logs = jnp.sum(got[m, few * width :].astype(jnp.float32), axis=0, keepdims=True)
            for h in range(few):
                span = span_of(h, width)
                here = state[span]
                given[m, span] = here.astype(jnp.bfloat16)
                log = jnp.sum(jnp.where(column == first + h, logs, 0.0), axis=1, keepdims=True)
                state[span] = here * jnp.exp(log) + got[m, span].astype(jnp.float32)
            return carry

        lax.fori_loop(0, chips, one_chip, 0)
        copies = [
            pltpu.make_async_copy(given.at[m], outs[m].at[pl.ds(to_row, few * width)], out_sems.at[m])
            for m in range(chips)
        ]
        for copy in copies:
            copy.start()
        for copy in copies:
            copy.wait()

    return pl.pallas_call(
        kernel,
        out_shape=[shape(payload.shape, payload.dtype) for payload in payloads],
        in_specs=[SMEM] + [ANY] * (2 * chips),
        out_specs=[ANY] * chips,
        scratch_shapes=[
            pltpu.VMEM((chips, extra, width), jnp.bfloat16),
            pltpu.VMEM((chips, few * width, width), jnp.bfloat16),
            pltpu.VMEM((few * width, width), jnp.float32),
            pltpu.SemaphoreType.DMA((chips,)),
            pltpu.SemaphoreType.DMA((chips,)),
        ],
        input_output_aliases={1 + chips + m: m for m in range(chips)},
        compiler_params=params(24),
        cost_estimate=cost(3 * half * width * width, 8 * half * width * width),
        name="scan_chips",
    )(place, *arrived, *payloads)


def gather_entry(place, arrived, from_row, few):
    chips = len(arrived)
    width = arrived[0].shape[-1]

    def kernel(place_ref, *rest):
        ins, out_ref = rest[:chips], rest[chips]
        chip = place_ref[0] // PAIR
        for m in range(chips):
            for h in range(few):
                out_ref[(chip ^ m) * few + h] = ins[m][pl.ds(from_row + h * width, width)]

    return pl.pallas_call(
        kernel,
        out_shape=shape((chips * few, width, width), jnp.bfloat16),
        in_specs=[SMEM] + [VMEM] * chips,
        out_specs=VMEM,
        compiler_params=params(16),
        cost_estimate=cost(0, 4 * chips * few * width * width),
        name="gather_entry",
    )(place, *arrived)


def finish(place, queries, decay, gain, inner, neighbour, entry_own, entry_other):
    rows, heads, width = queries.shape
    half = heads // PAIR

    def kernel(
        place_ref, q_ref, decay_ref, gain_ref, inner_ref, near_ref, own_ref, other_ref, out_ref, mixed
    ):
        core = place_ref[0] % PAIR
        cumul, _ = decay_sums(decay_ref)
        grown = jnp.exp(cumul)
        near_logs = near_ref[heads, 0:1, :]
        far = jnp.where(core == 0, 1.0, jnp.exp(near_logs))
        near = jnp.where(core == 0, 0.0, 1.0)
        power = jnp.zeros((rows, width), jnp.float32)
        for at, step in turns(heads):
            q = jnp.swapaxes(q_ref[:, at : at + step, :], 0, 1)
            for h in range(step):
                i = at + h
                mine, theirs = own_ref[i % half], other_ref[i % half]
                chip_entry = jnp.where(core == i // half, mine, theirs).astype(jnp.float32)
                entry = chip_entry * far[:, i : i + 1] + near_ref[i] * near
                coarse = entry.astype(jnp.bfloat16)
                fine = (entry - coarse.astype(jnp.float32)).astype(jnp.bfloat16)
                brought = (nn(q[h], coarse) + nn(q[h], fine)) * grown[:, i : i + 1]
                mix = inner_ref[i] + brought
                mixed[i] = mix
                power += mix * mix
        mean = jnp.sum(power, axis=1, keepdims=True) / (heads * width)
        norm = lax.rsqrt(mean + EPSILON)
        for at, step in turns(heads):
            normed = [
                (mixed[at + h] * norm * gain_ref[at + h : at + h + 1, :]).astype(jnp.bfloat16)
                for h in range(step)
            ]
            out_ref[:, at : at + step, :] = jnp.swapaxes(jnp.stack(normed), 0, 1)

    return pl.pallas_call(
        kernel,
        out_shape=shape((rows, heads, width), jnp.bfloat16),
        in_specs=[SMEM] + [VMEM] * 7,
        out_specs=VMEM,
        scratch_shapes=[pltpu.VMEM((heads, rows, width), jnp.float32)],
        compiler_params=params(32),
        cost_estimate=cost(4 * heads * rows * width * width, 20 * rows * heads * width),
        name="finish",
    )(place, queries, decay, gain, inner, neighbour, entry_own, entry_other)


def per_device(
    lin_q, lin_k, lin_v, lin_decay, lin_gain, soft_q, soft_k, soft_v, block_bits, agent_ids
):
    count = lax.axis_size("seq")
    chips = count // PAIR
    rows, heads, width = soft_q.shape
    lin_heads = lin_q.shape[1]
    hosted = heads // chips
    parts = min(PARTS, hosted)
    each = hosted // parts
    few = lin_heads // count
    qkv_rows, out_rows = 3 * each * rows, each * rows
    place = lax.axis_index("seq").astype(jnp.int32).reshape(1)
    masks = range(1, chips)

    def exchange(value, m):
        return lax.ppermute(value, "seq", [(i, i ^ (PAIR * m)) for i in range(count)])

    def swap_cores(value):
        return lax.ppermute(value, "seq", [(i, i ^ 1) for i in range(count)])

    def after(value, *earlier):
        return lax.optimization_barrier((value, *earlier))[0]

    packed = pack(place, (soft_q, soft_k, soft_v), chips, hosted, parts, few * width + LOG_ROWS)
    own = []
    for part in range(parts - 1):
        own.append([packed[0][part]])
        for m in masks:
            outgoing = packed[m][part]
            if part > 0:
                outgoing = after(outgoing, own[part - 1][m])
            own[part].append(exchange(outgoing, m))
        own[part] = list(lax.optimization_barrier(tuple(own[part])))

    lin_decay = after(lin_decay, packed[0][0])
    state = block_state(lin_k, lin_v, lin_decay)
    near = swap_cores(state)
    payloads = join_cores(place, state, near, [packed[m][-1] for m in range(chips)], qkv_rows)
    inner = within(lin_q, lin_k, lin_v, after(lin_decay, own[0][0], payloads[0]))
    own.append([payloads[0]])
    for m in masks:
        own[-1].append(exchange(after(payloads[m], own[parts - 2][m]) if parts > 1 else payloads[m], m))

    back = [[] for _ in range(chips)]

    def give_back(values):
        for m in range(chips):
            back[m].append(exchange(values[m], m) if m else values[m])

    mixed = None
    for part in range(parts):
        if part == parts - 1 and part > 0:
            for m in masks:
                own[part][m] = after(own[part][m], inner, mixed[0])
        other = [swap_cores(block) for block in own[part]]
        if part == parts - 1 and part > 0:
            arrived = lax.optimization_barrier((*own[part], *other[:2]))[:chips]
            give_back(scan_chips(place, arrived, qkv_rows, mixed, out_rows, few, lin_heads))
        mixed = attend(
            place, block_bits, agent_ids, own[part], other, each, rows, few * width if part == 0 else 0
        )
        if parts == 1:
            mixed = scan_chips(place, own[part], qkv_rows, mixed, out_rows, few, lin_heads)
        elif 0 < part < parts - 1:
            give_back(mixed)
    if parts > 1:
        for m in masks:
            back[m][0] = after(back[m][0], mixed[0])
    give_back(mixed)

    entry = gather_entry(place, [back[m][0] for m in range(chips)], out_rows, few)
    gain = lin_gain.reshape(lin_heads, width)
    lin_out = finish(place, lin_q, lin_decay, gain, inner, near, entry, swap_cores(entry))
    back[0][-1] = after(back[0][-1], lin_out)
    soft_out = unpack(place, back, heads, rows, each)
    return (lin_out, soft_out)


def solution(mesh):
    rows = P(("dp", "seq"), None, None)
    return jax.shard_map(
        per_device,
        mesh=mesh,
        in_specs=(rows, rows, rows, P(("dp", "seq"), None), P(), rows, rows, rows, P("dp", None), P("dp")),
        out_specs=(rows, rows),
        check_vma=False,
    )
```

time: 107 us -> 89.6 us (0.84); the launches traced: 105 us -> 89.3 us
  waiting for transfers between devices: 44.9 us -> 27.4 us
  starting transfers between devices: 24.5 us -> 17 us
  Pallas kernels: 31.8 us -> 37.3 us
  local copies, waits for them, and re-layouts: 3.31 us -> 6.77 us
    ppermute x24 -> x22, waiting for transfers between devices: 44.9 us -> 27.4 us  [the longest x12 25.8 us: exchange(): return lax.ppermute(value, 'seq', [(i, i ^ PAIR * m) for i in range(count)])]
    ppermute x24 -> x22, starting transfers between devices: 24.5 us -> 17 us  [the longest x12 14.8 us: exchange(): return lax.ppermute(value, 'seq', [(i, i ^ PAIR * m) for i in range(count)])]
    pallas_call x6, Pallas kernels: 18.4 us -> 25.3 us  [the longest x2 17 us: attend(): pl.pallas_call(kernel, out_shape=[shape((each * rows + extra, width), jnp...]
    unnamed x23 -> x44, local copies, waits for them, and re-layouts: 3.31 us -> 5.84 us
    pallas_call x1, Pallas kernels: 3.47 us -> 2.07 us  [block_state(): pl.pallas_call(kernel, out_shape=shape((heads + 1, width, width), jnp.flo...]
  transfers between devices with their start and end apart: 24 -> 22, of which waited for: 8 -> 6; matrix products, arithmetic and copies ran while one was open for 0% -> 1% of each run, Pallas kernels for 22% -> 33%
where the time goes in v2:
time: 89.6 us; the launch traced here: 89.3 us
  Pallas kernels  37.3 us (42%)
  waiting for transfers between devices  27.4 us (31%)
  starting transfers between devices  17 us (19%)
  local copies, waits for them, and re-layouts  6.77 us (8%)
    ppermute x12, waiting for transfers between devices, exchange(): return lax.ppermute(value, 'seq', [(i, i ^ PAIR * m) for i in range(count)])  25.8 us
    pallas_call x2, Pallas kernels, attend(): pl.pallas_call(kernel, out_shape=[shape((each * rows + extra, width), jnp...  17 us
    ppermute x12, starting transfers between devices, exchange(): return lax.ppermute(value, 'seq', [(i, i ^ PAIR * m) for i in range(count)])  14.8 us
    unnamed x44, local copies, waits for them, and re-layouts  5.84 us
    pallas_call x1, Pallas kernels, within(): pl.pallas_call(kernel, out_shape=shape((heads, rows, width), jnp.float32)...  5.01 us
    pallas_call x1, Pallas kernels, pack(): pl.pallas_call(kernel, out_shape=out_shape, in_specs=[SMEM, ANY, ANY, ANY...  4.18 us
    pallas_call x1, Pallas kernels, finish(): pl.pallas_call(kernel, out_shape=shape((rows, heads, width), jnp.bfloat16...  3.51 us
    pallas_call x1, Pallas kernels, scan_chips(): pl.pallas_call(kernel, out_shape=[shape(payload.shape, payload.dtype) for...  2.46 us
  transfers between devices with their start and end apart: 22, of which 6 were waited for; matrix products, arithmetic and copies ran while one was open for 1% of the time, Pallas kernels for 33%

profile of v2, /device:TPU:0, one launch (start us, length us, event | category | flops | bytes accessed | tf_op | source)
XLA Modules:
  0.0 89.3 jit_solution(5358035192449004823)
XLA Ops:
  0.7 4.2 %pack.1 = (bf16[1536,128]{1,0:T(8,128)(2,1)}, bf16[2064,128]{1,0:T(8,128)(2,1)}, bf16[1536,128]{1,0:T(8,128)(2,1)}, bf16[2064,128]{1,0:T(8,128)(2,1)}, bf16[1536...) custom-call(s32[1]{0:T(128)} %bitcast.place_ref, ...), custom_call_target="tpu_custom_call" | custom-call | bytes 6291456 | tf_op jit(solution)/shard_map/pack/pallas_call | solution.py:102
  5.1 2.1 %block_state.1.own_ref = f32[33,128,128]{2,1,0:T(8,128)S(1)} custom-call(bf16[128,32,128]{2,1,0:T(8,128)(2,1)S(1)} %copy-done.8, bf16[128,32,128]{2,1,0:T(8,128)(2,1)S(1)} %copy-done.10, bf16[128,32]{1,0:T(8,128)(2,1)S(1)} %copy.22.decay_ref), custom_call_target="tpu_custom_call" | custom-call | flops 2147483648 | bytes 4194304 | tf_op jit(solution)/shard_map/block_state/pallas_call | solution.py:277
  7.7 2.6 %collective-permute-start = (bf16[1536,128]{1,0:T(8,128)(2,1)S(1)}, bf16[1536,128]{1,0:T(8,128)(2,1)S(1)}, u32[]{:S(2)}, u32[]{:S(2)}) collective-permute-start(bf16[1536,128]{1,0:T(8,128)(2,1)S(1)} %copy-done.21), channel_id=1, source_target_pairs={{0,2},{1,3},{2,0},{3,1},{4,6},{5,7},{6,4},{7,5},{8,10},{9,11},{10,... | collective-permute-start | bytes 1179656 | tf_op jit(solution)/shard_map/ppermute | solution.py:520
  10.2 1.5 %collective-permute-start.1 = (bf16[1536,128]{1,0:T(8,128)(2,1)S(1)}, bf16[1536,128]{1,0:T(8,128)(2,1)S(1)}, u32[]{:S(2)}, u32[]{:S(2)}) collective-permute-start(bf16[1536,128]{1,0:T(8,128)(2,1)S(1)} %copy-done.20), channel_id=1, source_target_pairs={{0,4},{1,5},{2,6},{3,7},{4,0},{5,1},{6,2},{7,3},{8,12},{9,13},{10,... | collective-permute-start | bytes 1179656 | tf_op jit(solution)/shard_map/ppermute | solution.py:520
  11.8 8.4 %collective-permute-done.rest_1_ = bf16[1536,128]{1,0:T(8,128)(2,1)S(1)} collective-permute-done((bf16[1536,128]{1,0:T(8,128)(2,1)S(1)}, bf16[1536,128]{1,0:T(8,128)(2,1)S(1)}, u32[]{:S(2)}, u32[]{:S(2)}) %collective-permute-start) | collective-permute-done | bytes 393248 | tf_op jit(solution)/shard_map/ppermute | solution.py:520
  20.2 9.6 %collective-permute-done.1.rest_2_ = bf16[1536,128]{1,0:T(8,128)(2,1)S(1)} collective-permute-done((bf16[1536,128]{1,0:T(8,128)(2,1)S(1)}, bf16[1536,128]{1,0:T(8,128)(2,1)S(1)}, u32[]{:S(2)}, u32[]{:S(2)}) %collective-permute-start.1) | collective-permute-done | bytes 393248 | tf_op jit(solution)/shard_map/ppermute | solution.py:520
  30.9 1.7 %join_cores.1 = (bf16[2064,128]{1,0:T(8,128)(2,1)S(1)}, bf16[2064,128]{1,0:T(8,128)(2,1)S(1)}, bf16[2064,128]{1,0:T(8,128)(2,1)}, bf16[2064,128]{1,0:T(8,128)(2,1)}) custom-call(s32[1]{0:T(128)} %bitcast.place_ref, f32[33,128,128]{2,1,0:T(8,128)S(1)} %block_state.1.own_ref, ...), custom_call_target="tpu_custom_call", output_to_operand_aliasing={{0}: (3, {}), {1}: (4, {}), {2}: (5, {}), {3}: (6, {})} | custom-call | flops 12582912 | bytes 3670016 | tf_op jit(solution)/shard_map/join_cores/pallas_call | solution.py:355
  32.6 1.6 %collective-permute-start.10 = (bf16[2064,128]{1,0:T(8,128)(2,1)}, bf16[2064,128]{1,0:T(8,128)(2,1)}, u32[]{:S(2)}, u32[]{:S(2)}) collective-permute-start(bf16[2064,128]{1,0:T(8,128)(2,1)} %get-tuple-element.69), channel_id=1, source_target_pairs={{0,6},{1,7},{2,4},{3,5},{4,2},{5,3},{6,0},{7,1},{8,14},{9,15},{10,... | collective-permute-start | bytes 1585160 | tf_op jit(solution)/shard_map/ppermute | solution.py:520
  34.1 1.2 %collective-permute-start.9 = (bf16[2064,128]{1,0:T(8,128)(2,1)}, bf16[2064,128]{1,0:T(8,128)(2,1)}, u32[]{:S(2)}, u32[]{:S(2)}) collective-permute-start(bf16[2064,128]{1,0:T(8,128)(2,1)} %get-tuple-element.66), channel_id=1, source_target_pairs={{0,4},{1,5},{2,6},{3,7},{4,0},{5,1},{6,2},{7,3},{8,12},{9,13},{10,... | collective-permute-start | bytes 1585160 | tf_op jit(solution)/shard_map/ppermute | solution.py:520
  35.4 0.8 collective-permute-start.4
  36.2 8.5 %attend.2 = (bf16[1024,128]{1,0:T(8,128)(2,1)S(1)}, bf16[1024,128]{1,0:T(8,128)(2,1)S(1)}, bf16[1024,128]{1,0:T(8,128)(2,1)S(1)}, bf16[1024,128]{1,0:T(8,128)(2,1)S(1)}) custom-call(s32[1]{0:T(128)} %bitcast.place_ref, s32[8,8]{1,0:T(8,128)S(1)} %copy-done.16, s32[8]{0:T(128)S(1)} %copy-done.17, bf16[1536,128]{1,0:T(8,128)(2,1)S(1)} %copy-done.14, ...), custom_call_target="tpu_custom_call" | custom-call | flops 8589934592 | bytes 3670016 | tf_op jit(solution)/shard_map/attend/pallas_call | solution.py:202
  44.7 0.7 copy-done.2
  45.4 0.7 copy-done.4
  46.1 0.7 copy-done.6
  46.8 0.8 copy.21.decay_ref
  47.6 1.2 %copy-done.9 = bf16[128,32,128]{2,1,0:T(8,128)(2,1)S(1)} copy-done((bf16[128,32,128]{2,1,0:T(8,128)(2,1)S(1)}, bf16[128,32,128]{2,1,0:T(8,128)(2,1)}, u32[]{:S(2)}) %copy-start.9) | copy-done | bytes 1048600
  48.8 1.2 %copy-done.11 = bf16[128,32,128]{2,1,0:T(8,128)(2,1)S(1)} copy-done((bf16[128,32,128]{2,1,0:T(8,128)(2,1)S(1)}, bf16[128,32,128]{2,1,0:T(8,128)(2,1)}, u32[]{:S(2)}) %copy-start.11) | copy-done | bytes 1048600
  50.0 1.2 %copy-done.12 = bf16[128,32,128]{2,1,0:T(8,128)(2,1)S(1)} copy-done((bf16[128,32,128]{2,1,0:T(8,128)(2,1)S(1)}, bf16[128,32,128]{2,1,0:T(8,128)(2,1)}, u32[]{:S(2)}) %copy-start.12) | copy-done | bytes 1048600
  51.3 5.0 %within.1.inner_ref = f32[32,128,128]{2,1,0:T(8,128)S(1)} custom-call(bf16[128,32,128]{2,1,0:T(8,128)(2,1)S(1)} %copy-done.12, bf16[128,32,128]{2,1,0:T(8,128)(2,1)S(1)} %copy-done.9, bf16[128,32,128]{2,1,0:T(8,128)(2,1)S(1)} %copy-done.11, bf16[128,32]{1,0:T(8,128)(2,1)S(1)} %copy.21.decay_ref), custom_call_target="tpu_custom_call" | custom-call | flops 4294967296 | bytes 5242880 | tf_op jit(solution)/shard_map/within/pallas_call | solution.py:305
  56.3 3.0 %collective-permute-done.4.rest_1_ = bf16[2064,128]{1,0:T(8,128)(2,1)} collective-permute-done((bf16[2064,128]{1,0:T(8,128)(2,1)S(1)}, bf16[2064,128]{1,0:T(8,128)(2,1)}, u32[]{:S(2)}, u32[]{:S(2)}) %collective-permute-start.4) | collective-permute-done | bytes 528416 | tf_op jit(solution)/shard_map/ppermute | solution.py:520
  59.9 1.5 %collective-permute-done.12.rest_5_ = bf16[2064,128]{1,0:T(8,128)(2,1)S(1)} collective-permute-done((bf16[2064,128]{1,0:T(8,128)(2,1)}, bf16[2064,128]{1,0:T(8,128)(2,1)S(1)}, u32[]{:S(2)}, u32[]{:S(2)}) %collective-permute-start.12) | collective-permute-done | bytes 528416 | tf_op jit(solution)/shard_map/ppermute | solution.py:523
  61.4 2.5 %scan_chips.1 = (bf16[1024,128]{1,0:T(8,128)(2,1)S(1)}, bf16[1024,128]{1,0:T(8,128)(2,1)S(1)}, bf16[1024,128]{1,0:T(8,128)(2,1)S(1)}, bf16[1024,128]{1,0:T(8,128)(2,1)S(1)}) custom-call(s32[1]{0:T(128)} %bitcast.place_ref, bf16[2064,128]{1,0:T(8,128)(2,1)S(1)} %get-tuple-element.71.rest_0_, ...), custom_call_target="tpu_custom_call", output_to_operand_aliasing={{0}: (5, {}), {1}: (6, {}), {2}: (7, {}), {3}: (8, {})} | custom-call | flops 12582912 | bytes 2097152 | tf_op jit(solution)/shard_map/scan_chips/pallas_call | solution.py:415
  63.9 1.2 %collective-permute-start.17 = (bf16[1024,128]{1,0:T(8,128)(2,1)S(1)}, bf16[1024,128]{1,0:T(8,128)(2,1)S(1)}, u32[]{:S(2)}, u32[]{:S(2)}) collective-permute-start(bf16[1024,128]{1,0:T(8,128)(2,1)S(1)} %get-tuple-element.84), channel_id=1, source_target_pairs={{0,6},{1,7},{2,4},{3,5},{4,2},{5,3},{6,0},{7,1},{8,14},{9,15},{10,... | collective-permute-start | bytes 786440 | tf_op jit(solution)/shard_map/ppermute | solution.py:520
  65.1 0.9 collective-permute-start.16
  66.0 1.5 %collective-permute-start.13 = (bf16[1024,128]{1,0:T(8,128)(2,1)S(1)}, bf16[1024,128]{1,0:T(8,128)(2,1)S(1)}, u32[]{:S(2)}, u32[]{:S(2)}) collective-permute-start(bf16[1024,128]{1,0:T(8,128)(2,1)S(1)} %get-tuple-element.79), channel_id=1, source_target_pairs={{0,2},{1,3},{2,0},{3,1},{4,6},{5,7},{6,4},{7,5},{8,10},{9,11},{10,... | collective-permute-start | bytes 786440 | tf_op jit(solution)/shard_map/ppermute | solution.py:520
  67.5 8.5 %attend.3 = (bf16[512,128]{1,0:T(8,128)(2,1)S(1)}, bf16[512,128]{1,0:T(8,128)(2,1)S(1)}, bf16[512,128]{1,0:T(8,128)(2,1)S(1)}, bf16[512,128]{1,0:T(8,128)(2,1)S(1)}) custom-call(s32[1]{0:T(128)} %bitcast.place_ref, s32[8,8]{1,0:T(8,128)S(1)} %copy-done.16, s32[8]{0:T(128)S(1)} %copy-done.17, bf16[2064,128]{1,0:T(8,128)(2,1)S(1)} %get-tuple-element.71.rest_0_, ...), custom_call_target="tpu_custom_call" | custom-call | flops 8589934592 | bytes 3670016 | tf_op jit(solution)/shard_map/attend/pallas_call | solution.py:202
  76.0 2.8 %collective-permute-done.16.rest_2_.rest_4_ = bf16[1024,128]{1,0:T(8,128)(2,1)S(1)} collective-permute-done((bf16[1024,128]{1,0:T(8,128)(2,1)S(1)}, bf16[1024,128]{1,0:T(8,128)(2,1)S(1)}, u32[]{:S(2)}, u32[]{:S(2)}) %collective-permute-start.16) | collective-permute-done | bytes 262176 | tf_op jit(solution)/shard_map/ppermute | solution.py:520
  79.5 1.1 %collective-permute-start.20 = (bf16[512,128]{1,0:T(8,128)(2,1)S(1)}, bf16[512,128]{1,0:T(8,128)(2,1)S(1)}, u32[]{:S(2)}, u32[]{:S(2)}) collective-permute-start(bf16[512,128]{1,0:T(8,128)(2,1)S(1)} %get-tuple-element.88), channel_id=1, source_target_pairs={{0,4},{1,5},{2,6},{3,7},{4,0},{5,1},{6,2},{7,3},{8,12},{9,13},{10,... | collective-permute-start | bytes 393224 | tf_op jit(solution)/shard_map/ppermute | solution.py:520
  80.7 1.7 %collective-permute-start.21 = (bf16[512,128]{1,0:T(8,128)(2,1)S(1)}, bf16[512,128]{1,0:T(8,128)(2,1)S(1)}, u32[]{:S(2)}, u32[]{:S(2)}) collective-permute-start(bf16[512,128]{1,0:T(8,128)(2,1)S(1)} %get-tuple-element.89), channel_id=1, source_target_pairs={{0,6},{1,7},{2,4},{3,5},{4,2},{5,3},{6,0},{7,1},{8,14},{9,15},{10,... | collective-permute-start | bytes 393224 | tf_op jit(solution)/shard_map/ppermute | solution.py:520
  82.4 3.5 %finish.1 = bf16[128,32,128]{2,1,0:T(8,128)(2,1)} custom-call(s32[1]{0:T(128)} %bitcast.place_ref, bf16[128,32,128]{2,1,0:T(8,128)(2,1)S(1)} %copy-done.13, bf16[128,32]{1,0:T(8,128)(2,1)S(1)} %copy.22.decay_ref, f32[32,128]{1,0:T(8,128)S(1)} %bitcast.2, f32[32,128,128]{2,1,0:T(8,128)S(1)} %within.1.inner_ref, ...), custom_call_target="tpu_custom_call" | custom-call | flops 4294967296 | bytes 10485760 | tf_op jit(solution)/shard_map/finish/pallas_call | solution.py:492
  85.9 2.0 %collective-permute-done.20.rest_5_ = bf16[512,128]{1,0:T(8,128)(2,1)S(1)} collective-permute-done((bf16[512,128]{1,0:T(8,128)(2,1)S(1)}, bf16[512,128]{1,0:T(8,128)(2,1)S(1)}, u32[]{:S(2)}, u32[]{:S(2)}) %collective-permute-start.20) | collective-permute-done | bytes 131104 | tf_op jit(solution)/shard_map/ppermute | solution.py:520
  87.9 1.4 %unpack.1 = bf16[128,32,128]{2,1,0:T(8,128)(2,1)} custom-call(s32[1]{0:T(128)} %bitcast.place_ref, bf16[1024,128]{1,0:T(8,128)(2,1)S(1)} %get-tuple-element.78.rest_0_, bf16[512,128]{1,0:T(8,128)(2,1)S(1)} %get-tuple-element.86.rest_1_, bf16[1024,128]{1,0:T(8,128)(2,1)S(1)} %collective-permute-done.13.rest_1_.rest_2_, ...), custom_call_target="tpu_custom_call" | custom-call | bytes 2097152 | tf_op jit(solution)/shard_map/unpack/pallas_call | solution.py:241
  (68 shorter events, 3.2 us)
Async XLA Ops:
  5.0 6.7 %copy-start.19 = (bf16[1536,128]{1,0:T(8,128)(2,1)S(1)}, bf16[1536,128]{1,0:T(8,128)(2,1)}, u32[]{:S(2)}) copy-start(bf16[1536,128]{1,0:T(8,128)(2,1)} %get-tuple-element.50) | copy-start | bytes 1179652
  5.0 24.8 %copy-start.14 = (bf16[1536,128]{1,0:T(8,128)(2,1)S(1)}, bf16[1536,128]{1,0:T(8,128)(2,1)}, u32[]{:S(2)}) copy-start(bf16[1536,128]{1,0:T(8,128)(2,1)} %get-tuple-element.51.rest_0_) | copy-start | bytes 1179652
  5.0 25.8 %copy-start = (bf16[2064,128]{1,0:T(8,128)(2,1)S(1)}, bf16[2064,128]{1,0:T(8,128)(2,1)}, u32[]{:S(2)}) copy-start(bf16[2064,128]{1,0:T(8,128)(2,1)} %get-tuple-element.52.rest_0_) | copy-start | bytes 1585156
  5.1 25.8 %copy-start.1 = (bf16[2064,128]{1,0:T(8,128)(2,1)S(1)}, bf16[2064,128]{1,0:T(8,128)(2,1)}, u32[]{:S(2)}) copy-start(bf16[2064,128]{1,0:T(8,128)(2,1)} %get-tuple-element.53.rest_1_) | copy-start | bytes 1585156
  7.1 23.7 %collective-permute-start.3 = (f32[33,128,128]{2,1,0:T(8,128)S(1)}, f32[33,128,128]{2,1,0:T(8,128)S(1)}, u32[]{:S(2)}, u32[]{:S(2)}) collective-permute-start(f32[33,128,128]{2,1,0:T(8,128)S(1)} %block_state.1.own_ref), channel_id=1, source_target_pairs={{0,1},{1,0},{2,3},{3,2},{4,5},{5,4},{6,7},{7,6},{8,9},{9,8},{10,11... | collective-permute-start | bytes 6488072 | tf_op jit(solution)/shard_map/ppermute | solution.py:523
  7.7 12.5 %collective-permute-start = (bf16[1536,128]{1,0:T(8,128)(2,1)S(1)}, bf16[1536,128]{1,0:T(8,128)(2,1)S(1)}, u32[]{:S(2)}, u32[]{:S(2)}) collective-permute-start(bf16[1536,128]{1,0:T(8,128)(2,1)S(1)} %copy-done.21), channel_id=1, source_target_pairs={{0,2},{1,3},{2,0},{3,1},{4,6},{5,7},{6,4},{7,5},{8,10},{9,11},{10,... | collective-permute-start | bytes 1179656 | tf_op jit(solution)/shard_map/ppermute | solution.py:520
  10.2 19.6 %collective-permute-start.1 = (bf16[1536,128]{1,0:T(8,128)(2,1)S(1)}, bf16[1536,128]{1,0:T(8,128)(2,1)S(1)}, u32[]{:S(2)}, u32[]{:S(2)}) collective-permute-start(bf16[1536,128]{1,0:T(8,128)(2,1)S(1)} %copy-done.20), channel_id=1, source_target_pairs={{0,4},{1,5},{2,6},{3,7},{4,0},{5,1},{6,2},{7,3},{8,12},{9,13},{10,... | collective-permute-start | bytes 1179656 | tf_op jit(solution)/shard_map/ppermute | solution.py:520
  11.8 18.1 %collective-permute-start.2 = (bf16[1536,128]{1,0:T(8,128)(2,1)S(1)}, bf16[1536,128]{1,0:T(8,128)(2,1)S(1)}, u32[]{:S(2)}, u32[]{:S(2)}) collective-permute-start(bf16[1536,128]{1,0:T(8,128)(2,1)S(1)} %copy-done.19), channel_id=1, source_target_pairs={{0,6},{1,7},{2,4},{3,5},{4,2},{5,3},{6,0},{7,1},{8,14},{9,15},{10,... | collective-permute-start | bytes 1179656 | tf_op jit(solution)/shard_map/ppermute | solution.py:520
  29.9 4.3 %collective-permute-start.5 = (bf16[1536,128]{1,0:T(8,128)(2,1)S(1)}, bf16[1536,128]{1,0:T(8,128)(2,1)S(1)}, u32[]{:S(2)}, u32[]{:S(2)}) collective-permute-start(bf16[1536,128]{1,0:T(8,128)(2,1)S(1)} %copy-done.14), channel_id=1, source_target_pairs={{0,1},{1,0},{2,3},{3,2},{4,5},{5,4},{6,7},{7,6},{8,9},{9,8},{10,11... | collective-permute-start | bytes 1179656 | tf_op jit(solution)/shard_map/ppermute | solution.py:523
  29.9 5.5 %collective-permute-start.6 = (bf16[1536,128]{1,0:T(8,128)(2,1)S(1)}, bf16[1536,128]{1,0:T(8,128)(2,1)S(1)}, u32[]{:S(2)}, u32[]{:S(2)}) collective-permute-start(bf16[1536,128]{1,0:T(8,128)(2,1)S(1)} %collective-permute-done.rest_1_), channel_id=1, source_target_pairs={{0,1},{1,0},{2,3},{3,2},{4,5},{5,4},{6,7},{7,6},{8,9},{9,8},{10,11... | collective-permute-start | bytes 1179656 | tf_op jit(solution)/shard_map/ppermute | solution.py:523
  30.4 5.8 %collective-permute-start.7 = (bf16[1536,128]{1,0:T(8,128)(2,1)S(1)}, bf16[1536,128]{1,0:T(8,128)(2,1)S(1)}, u32[]{:S(2)}, u32[]{:S(2)}) collective-permute-start(bf16[1536,128]{1,0:T(8,128)(2,1)S(1)} %collective-permute-done.1.rest_2_), channel_id=1, source_target_pairs={{0,1},{1,0},{2,3},{3,2},{4,5},{5,4},{6,7},{7,6},{8,9},{9,8},{10,11... | collective-permute-start | bytes 1179656 | tf_op jit(solution)/shard_map/ppermute | solution.py:523
  30.4 5.7 %collective-permute-start.8 = (bf16[1536,128]{1,0:T(8,128)(2,1)S(1)}, bf16[1536,128]{1,0:T(8,128)(2,1)S(1)}, u32[]{:S(2)}, u32[]{:S(2)}) collective-permute-start(bf16[1536,128]{1,0:T(8,128)(2,1)S(1)} %collective-permute-done.2.rest_3_), channel_id=1, source_target_pairs={{0,1},{1,0},{2,3},{3,2},{4,5},{5,4},{6,7},{7,6},{8,9},{9,8},{10,11... | collective-permute-start | bytes 1179656 | tf_op jit(solution)/shard_map/ppermute | solution.py:523
  30.9 5.3 %copy-start.16 = (s32[8,8]{1,0:T(8,128)S(1)}, s32[8,8]{1,0:T(8,128)}, u32[]{:S(2)}) copy-start(s32[8,8]{1,0:T(8,128)} %bits_ref.3) | copy-start | bytes 772
  32.6 26.7 %collective-permute-start.10 = (bf16[2064,128]{1,0:T(8,128)(2,1)}, bf16[2064,128]{1,0:T(8,128)(2,1)}, u32[]{:S(2)}, u32[]{:S(2)}) collective-permute-start(bf16[2064,128]{1,0:T(8,128)(2,1)} %get-tuple-element.69), channel_id=1, source_target_pairs={{0,6},{1,7},{2,4},{3,5},{4,2},{5,3},{6,0},{7,1},{8,14},{9,15},{10,... | collective-permute-start | bytes 1585160 | tf_op jit(solution)/shard_map/ppermute | solution.py:520
  34.1 25.7 %collective-permute-start.9 = (bf16[2064,128]{1,0:T(8,128)(2,1)}, bf16[2064,128]{1,0:T(8,128)(2,1)}, u32[]{:S(2)}, u32[]{:S(2)}) collective-permute-start(bf16[2064,128]{1,0:T(8,128)(2,1)} %get-tuple-element.66), channel_id=1, source_target_pairs={{0,4},{1,5},{2,6},{3,7},{4,0},{5,1},{6,2},{7,3},{8,12},{9,13},{10,... | collective-permute-start | bytes 1585160 | tf_op jit(solution)/shard_map/ppermute | solution.py:520
  35.4 23.9 %collective-permute-start.4 = (bf16[2064,128]{1,0:T(8,128)(2,1)S(1)}, bf16[2064,128]{1,0:T(8,128)(2,1)}, u32[]{:S(2)}, u32[]{:S(2)}) collective-permute-start(bf16[2064,128]{1,0:T(8,128)(2,1)S(1)} %get-tuple-element.60), channel_id=1, source_target_pairs={{0,2},{1,3},{2,0},{3,1},{4,6},{5,7},{6,4},{7,5},{8,10},{9,11},{10,... | collective-permute-start | bytes 1585160 | tf_op jit(solution)/shard_map/ppermute | solution.py:520
  46.8 13.1 %collective-permute-start.11 = (bf16[2064,128]{1,0:T(8,128)(2,1)S(1)}, bf16[2064,128]{1,0:T(8,128)(2,1)}, u32[]{:S(2)}, u32[]{:S(2)}) collective-permute-start(bf16[2064,128]{1,0:T(8,128)(2,1)S(1)} %get-tuple-element.71.rest_0_), channel_id=1, source_target_pairs={{0,1},{1,0},{2,3},{3,2},{4,5},{5,4},{6,7},{7,6},{8,9},{9,8},{10,11... | collective-permute-start | bytes 1585160 | tf_op jit(solution)/shard_map/ppermute | solution.py:523
  51.2 10.2 %copy-start.3 = (bf16[1024,128]{1,0:T(8,128)(2,1)S(1)}, bf16[1024,128]{1,0:T(8,128)(2,1)}, u32[]{:S(2)}) copy-start(bf16[1024,128]{1,0:T(8,128)(2,1)} %copy-done.2) | copy-start | bytes 786436
  51.2 10.2 %copy-start.5 = (bf16[1024,128]{1,0:T(8,128)(2,1)S(1)}, bf16[1024,128]{1,0:T(8,128)(2,1)}, u32[]{:S(2)}) copy-start(bf16[1024,128]{1,0:T(8,128)(2,1)} %copy-done.4) | copy-start | bytes 786436
  51.2 10.2 %copy-start.7 = (bf16[1024,128]{1,0:T(8,128)(2,1)S(1)}, bf16[1024,128]{1,0:T(8,128)(2,1)}, u32[]{:S(2)}) copy-start(bf16[1024,128]{1,0:T(8,128)(2,1)} %copy-done.6) | copy-start | bytes 786436
  59.3 2.1 %collective-permute-start.12 = (bf16[2064,128]{1,0:T(8,128)(2,1)}, bf16[2064,128]{1,0:T(8,128)(2,1)S(1)}, u32[]{:S(2)}, u32[]{:S(2)}) collective-permute-start(bf16[2064,128]{1,0:T(8,128)(2,1)} %collective-permute-done.4.rest_1_), channel_id=1, source_target_pairs={{0,1},{1,0},{2,3},{3,2},{4,5},{5,4},{6,7},{7,6},{8,9},{9,8},{10,11... | collective-permute-start | bytes 1585160 | tf_op jit(solution)/shard_map/ppermute | solution.py:523
  59.3 8.2 %collective-permute-start.15 = (bf16[2064,128]{1,0:T(8,128)(2,1)}, bf16[2064,128]{1,0:T(8,128)(2,1)S(1)}, u32[]{:S(2)}, u32[]{:S(2)}) collective-permute-start(bf16[2064,128]{1,0:T(8,128)(2,1)} %collective-permute-done.10.rest_3_), channel_id=1, source_target_pairs={{0,1},{1,0},{2,3},{3,2},{4,5},{5,4},{6,7},{7,6},{8,9},{9,8},{10,11... | collective-permute-start | bytes 1585160 | tf_op jit(solution)/shard_map/ppermute | solution.py:523
  59.8 7.7 %collective-permute-start.14 = (bf16[2064,128]{1,0:T(8,128)(2,1)}, bf16[2064,128]{1,0:T(8,128)(2,1)S(1)}, u32[]{:S(2)}, u32[]{:S(2)}) collective-permute-start(bf16[2064,128]{1,0:T(8,128)(2,1)} %collective-permute-done.9.rest_2_), channel_id=1, source_target_pairs={{0,1},{1,0},{2,3},{3,2},{4,5},{5,4},{6,7},{7,6},{8,9},{9,8},{10,11... | collective-permute-start | bytes 1585160 | tf_op jit(solution)/shard_map/ppermute | solution.py:523
  63.9 12.1 %collective-permute-start.17 = (bf16[1024,128]{1,0:T(8,128)(2,1)S(1)}, bf16[1024,128]{1,0:T(8,128)(2,1)S(1)}, u32[]{:S(2)}, u32[]{:S(2)}) collective-permute-start(bf16[1024,128]{1,0:T(8,128)(2,1)S(1)} %get-tuple-element.84), channel_id=1, source_target_pairs={{0,6},{1,7},{2,4},{3,5},{4,2},{5,3},{6,0},{7,1},{8,14},{9,15},{10,... | collective-permute-start | bytes 786440 | tf_op jit(solution)/shard_map/ppermute | solution.py:520
  65.1 13.7 %collective-permute-start.16 = (bf16[1024,128]{1,0:T(8,128)(2,1)S(1)}, bf16[1024,128]{1,0:T(8,128)(2,1)S(1)}, u32[]{:S(2)}, u32[]{:S(2)}) collective-permute-start(bf16[1024,128]{1,0:T(8,128)(2,1)S(1)} %get-tuple-element.82), channel_id=1, source_target_pairs={{0,4},{1,5},{2,6},{3,7},{4,0},{5,1},{6,2},{7,3},{8,12},{9,13},{10,... | collective-permute-start | bytes 786440 | tf_op jit(solution)/shard_map/ppermute | solution.py:520
  65.9 16.5 %copy-start.13 = (bf16[128,32,128]{2,1,0:T(8,128)(2,1)S(1)}, bf16[128,32,128]{2,1,0:T(8,128)(2,1)}, u32[]{:S(2)}) copy-start(bf16[128,32,128]{2,1,0:T(8,128)(2,1)} %q_ref.5) | copy-start | bytes 3145732
  65.9 16.5 %copy-start.15 = (f32[4096]{0:T(1024)S(1)}, f32[4096]{0:T(1024)}, u32[]{:S(2)}) copy-start(f32[4096]{0:T(1024)} %param.14) | copy-start | bytes 49156
  66.0 12.8 %collective-permute-start.13 = (bf16[1024,128]{1,0:T(8,128)(2,1)S(1)}, bf16[1024,128]{1,0:T(8,128)(2,1)S(1)}, u32[]{:S(2)}, u32[]{:S(2)}) collective-permute-start(bf16[1024,128]{1,0:T(8,128)(2,1)S(1)} %get-tuple-element.79), channel_id=1, source_target_pairs={{0,2},{1,3},{2,0},{3,1},{4,6},{5,7},{6,4},{7,5},{8,10},{9,11},{10,... | collective-permute-start | bytes 786440 | tf_op jit(solution)/shard_map/ppermute | solution.py:520
  78.8 3.6 %collective-permute-start.18 = (bf16[16,128,128]{2,1,0:T(8,128)(2,1)S(1)}, bf16[16,128,128]{2,1,0:T(8,128)(2,1)S(1)}, u32[]{:S(2)}, u32[]{:S(2)}) collective-permute-start(bf16[16,128,128]{2,1,0:T(8,128)(2,1)S(1)} %gather_entry.1.own_ref), channel_id=1, source_target_pairs={{0,1},{1,0},{2,3},{3,2},{4,5},{5,4},{6,7},{7,6},{8,9},{9,8},{10,11... | collective-permute-start | bytes 1572872 | tf_op jit(solution)/shard_map/ppermute | solution.py:523
  78.9 7.1 %collective-permute-start.19 = (bf16[512,128]{1,0:T(8,128)(2,1)S(1)}, bf16[512,128]{1,0:T(8,128)(2,1)S(1)}, u32[]{:S(2)}, u32[]{:S(2)}) collective-permute-start(bf16[512,128]{1,0:T(8,128)(2,1)S(1)} %get-tuple-element.87), channel_id=1, source_target_pairs={{0,2},{1,3},{2,0},{3,1},{4,6},{5,7},{6,4},{7,5},{8,10},{9,11},{10,... | collective-permute-start | bytes 393224 | tf_op jit(solution)/shard_map/ppermute | solution.py:520
  79.5 8.4 %collective-permute-start.20 = (bf16[512,128]{1,0:T(8,128)(2,1)S(1)}, bf16[512,128]{1,0:T(8,128)(2,1)S(1)}, u32[]{:S(2)}, u32[]{:S(2)}) collective-permute-start(bf16[512,128]{1,0:T(8,128)(2,1)S(1)} %get-tuple-element.88), channel_id=1, source_target_pairs={{0,4},{1,5},{2,6},{3,7},{4,0},{5,1},{6,2},{7,3},{8,12},{9,13},{10,... | collective-permute-start | bytes 393224 | tf_op jit(solution)/shard_map/ppermute | solution.py:520
  80.7 7.2 %collective-permute-start.21 = (bf16[512,128]{1,0:T(8,128)(2,1)S(1)}, bf16[512,128]{1,0:T(8,128)(2,1)S(1)}, u32[]{:S(2)}, u32[]{:S(2)}) collective-permute-start(bf16[512,128]{1,0:T(8,128)(2,1)S(1)} %get-tuple-element.89), channel_id=1, source_target_pairs={{0,6},{1,7},{2,4},{3,5},{4,2},{5,3},{6,0},{7,1},{8,14},{9,15},{10,... | collective-permute-start | bytes 393224 | tf_op jit(solution)/shard_map/ppermute | solution.py:520
  (12 other events, 31.9 us)

commit v3 on v2

v3 whole, which is shorter than its diff:
```python
import jax
import jax.numpy as jnp
from jax import lax
from jax.experimental import pallas as pl
from jax.experimental.pallas import tpu as pltpu
from jax.sharding import PartitionSpec as P

EPSILON = 1e-06
PAIR = 2
ABREAST = 2
EARLY = 2
PACK_MIB = 56
WEIGHT = 1 << 29
PARTS = 1
TURN = 8
LOG_ROWS = 16
LOG2E = 1.4426950408889634
VMEM = pl.BlockSpec(memory_space=pltpu.VMEM)
SMEM = pl.BlockSpec(memory_space=pltpu.SMEM)
ANY = pl.BlockSpec(memory_space=pl.ANY)


def params(mib):
    return pltpu.CompilerParams(vmem_limit_bytes=mib << 20)


def cost(weight=1):
    return pl.CostEstimate(flops=WEIGHT * weight, bytes_accessed=1, transcendentals=0)


def shape(dims, dtype):
    return jax.ShapeDtypeStruct(dims, dtype)


def turns(heads):
    step = min(TURN, heads)
    return [(at, step) for at in range(0, heads, step)]


def span_of(index, rows):
    return pl.ds(index * rows, rows)


def nt(a, b):
    return lax.dot_general(a, b, (((1,), (1,)), ((), ())), preferred_element_type=jnp.float32)


def tn(a, b):
    return lax.dot_general(a, b, (((0,), (0,)), ((), ())), preferred_element_type=jnp.float32)


def nn(a, b):
    return lax.dot_general(a, b, (((1,), (0,)), ((), ())), preferred_element_type=jnp.float32)


def triangle(size):
    rows = lax.broadcasted_iota(jnp.int32, (size, size), 0)
    cols = lax.broadcasted_iota(jnp.int32, (size, size), 1)
    return cols <= rows


def pack(place, arrays, chips, sizes):
    rows, heads, width = arrays[0].shape
    hosted = sum(sizes)
    pieces = 2
    cut = rows // pieces

    def kernel(place_ref, q_ref, k_ref, v_ref, *rest):
        outs, (landed, turned, in_sems, out_sems) = rest[:-4], rest[-4:]
        chip = place_ref[0] // PAIR
        arriving = [
            pltpu.make_async_copy(
                ref.at[pl.ds(piece * cut, cut)],
                landed.at[which, pl.ds(piece * cut, cut)],
                in_sems.at[which, piece],
            )
            for which, ref in enumerate((q_ref, k_ref, v_ref))
            for piece in range(pieces)
        ]
        for copy in arriving:
            copy.start()
        leaving = []
        for which in range(3):
            for piece in range(pieces):
                arriving[which * pieces + piece].wait()
            for at, step in turns(heads):
                block = jnp.swapaxes(landed[which, :, at : at + step, :], 0, 1)
                for h in range(step):
                    turned[which, at + h] = block[h].T if which == 1 else block[h]
            for part, each in enumerate(sizes):
                for m in range(chips):
                    first = (chip ^ m) * hosted + sum(sizes[:part])
                    leaving.append(
                        pltpu.make_async_copy(
                            turned.at[which, pl.ds(first, each)],
                            outs[part * chips + m].at[pl.ds(which * each, each)],
                            out_sems.at[len(leaving)],
                        )
                    )
                    leaving[-1].start()
        for copy in leaving:
            copy.wait()

    outs = pl.pallas_call(
        kernel,
        out_shape=[shape((3 * each, rows, width), jnp.bfloat16) for each in sizes for _ in range(chips)],
        in_specs=[SMEM, ANY, ANY, ANY],
        out_specs=[ANY] * (chips * len(sizes)),
        scratch_shapes=[
            pltpu.VMEM((3, rows, heads, width), jnp.bfloat16),
            pltpu.VMEM((3, heads, rows, width), jnp.bfloat16),
            pltpu.SemaphoreType.DMA((3, pieces)),
            pltpu.SemaphoreType.DMA((3 * chips * len(sizes),)),
        ],
        compiler_params=params(PACK_MIB),
        cost_estimate=cost(4),
        name="pack",
    )(place, *arrays)
    return [list(outs[part * chips : (part + 1) * chips]) for part in range(len(sizes))]


def attend(place, bits, agents, own, other, each):
    chips = len(own)
    _, rows, width = own[0].shape
    slots = PAIR * chips
    scale = width**-0.5 * LOG2E
    most = sum(PAIR * chip + PAIR - 1 for chip in range(chips)) + ABREAST - 1

    def kernel(place_ref, bits_ref, agents_ref, *rest):
        ins, outs = rest[:slots], rest[slots : slots + chips]
        held, scores, top, total, mixed, probs, query_of, key_of, sems = rest[slots + chips :]
        me = place_ref[0]
        chip, core = me // PAIR, me % PAIR
        spans = [(0, 3 * each)] * chips + [(each, 2 * each)] * chips
        copies = [
            pltpu.make_async_copy(ins[j].at[pl.ds(at, size)], held.at[j, pl.ds(at, size)], sems.at[j])
            for j, (at, size) in enumerate(spans)
        ]
        for copy in copies:
            copy.start()

        found = jnp.int32(0)
        for i in range(chips):
            query_block = PAIR * (chip ^ i) + core

            def list_pair(key_block, found, i=i, query_block=query_block):
                seen = (bits_ref[query_block, key_block] == 1) | (
                    agents_ref[query_block] == agents_ref[key_block]
                )
                query_of[found] = i
                key_of[found] = (chip ^ (key_block // PAIR)) + chips * ((core + key_block) & (PAIR - 1))
                return found + seen.astype(jnp.int32)

            found = lax.fori_loop(0, query_block, list_pair, found)
        for spare in range(ABREAST - 1):
            query_of[found + spare] = 0
            key_of[found + spare] = 0
        rounds = (found + ABREAST - 1) // ABREAST

        def head(j, which, h):
            return held[j, which * each + h]

        lower = triangle(rows)
        for copy in copies[:chips]:
            copy.wait()
        for i in range(chips):
            for h in range(each):
                top[i, h] = jnp.where(lower, nn(head(i, 0, h), head(i, 1, h)), -1e30)
        for i in range(chips):
            for h in range(each):
                total[i, h] = top[i, h]
        for copy in copies[chips:]:
            copy.wait()

        def score(turn, carry):
            for lane in range(ABREAST):
                at = ABREAST * turn + lane
                i, j = query_of[at], key_of[at]
                for h in range(each):
                    s = jnp.where(at < found, nn(head(i, 0, h), head(j, 1, h)), -1e30)
                    scores[at, h] = s
                    top[i, h] = jnp.maximum(top[i, h], s)
            return carry

        lax.fori_loop(0, rounds, score, 0)
        for i in range(chips):
            for h in range(each):
                top[i, h] = jnp.broadcast_to(jnp.max(top[i, h], axis=1, keepdims=True), (rows, rows))
        for i in range(chips):
            for h in range(each):
                p = jnp.exp2((total[i, h] - top[i, h]) * scale)
                total[i, h] = p
                probs[i, h] = p.astype(jnp.bfloat16)
        for i in range(chips):
            for h in range(each):
                mixed[i, h] = nn(probs[i, h], head(i, 2, h))

        def weigh(turn, carry):
            for lane in range(ABREAST):
                at = ABREAST * turn + lane
                i = query_of[at]
                for h in range(each):
                    p = jnp.exp2((scores[at, h] - top[i, h]) * scale)
                    total[i, h] += p
                    probs[lane, h] = p.astype(jnp.bfloat16)
            for lane in range(ABREAST):
                at = ABREAST * turn + lane
                i, j = query_of[at], key_of[at]
                for h in range(each):
                    mixed[i, h] += nn(probs[lane, h], head(j, 2, h))
            return carry

        lax.fori_loop(0, rounds, weigh, 0)
        for i in range(chips):
            for h in range(each):
                sums = jnp.sum(total[i, h], axis=1, keepdims=True)
                outs[i][span_of(h, rows)] = (mixed[i, h] / sums).astype(jnp.bfloat16)

    block = (chips, each, rows, rows)
    held_bytes = 2 * each * rows * (3 * slots * width + (chips + max(chips, ABREAST)) * rows)
    score_bytes = 4 * each * rows * ((most + 2 * chips) * rows + chips * width)
    return pl.pallas_call(
        kernel,
        out_shape=[shape((each * rows, width), jnp.bfloat16)] * chips,
        in_specs=[SMEM, SMEM, SMEM] + [ANY] * slots,
        out_specs=[VMEM] * chips,
        scratch_shapes=[
            pltpu.VMEM((slots, 3 * each, rows, width), jnp.bfloat16),
            pltpu.VMEM((most, each, rows, rows), jnp.float32),
            pltpu.VMEM(block, jnp.float32),
            pltpu.VMEM(block, jnp.float32),
            pltpu.VMEM((chips, each, rows, width), jnp.float32),
            pltpu.VMEM((max(chips, ABREAST), each, rows, rows), jnp.bfloat16),
            pltpu.SMEM((most,), jnp.int32),
            pltpu.SMEM((most,), jnp.int32),
            pltpu.SemaphoreType.DMA((slots,)),
        ],
        compiler_params=params(8 + (held_bytes + score_bytes >> 20)),
        cost_estimate=cost(14),
        name="attend",
    )(place, bits, agents, *own, *other)


def unpack(place, pieces, heads, rows, sizes):
    chips, width = len(pieces[0]), pieces[0][0].shape[-1]

    def kernel(place_ref, *rest):
        ins, out_ref, turned = rest[:-2], rest[-2], rest[-1]
        chip = place_ref[0] // PAIR
        for part, each in enumerate(sizes):
            for m in range(chips):
                first = (chip ^ m) * sum(sizes) + sum(sizes[:part])
                for h in range(each):
                    turned[first + h] = ins[part * chips + m][span_of(h, rows)]
        for at, step in turns(heads):
            out_ref[:, at : at + step, :] = jnp.swapaxes(turned[at : at + step], 0, 1)

    return pl.pallas_call(
        kernel,
        out_shape=shape((rows, heads, width), jnp.bfloat16),
        in_specs=[SMEM] + [VMEM] * (chips * len(sizes)),
        out_specs=VMEM,
        scratch_shapes=[pltpu.VMEM((heads, rows, width), jnp.bfloat16)],
        compiler_params=params(16),
        cost_estimate=cost(4),
        name="unpack",
    )(place, *[piece for part in pieces for piece in part])


def decay_sums(decay_ref):
    decay = decay_ref[...]
    lower = triangle(decay.shape[0]).astype(jnp.bfloat16)
    return nn(lower, decay), lax.dot_general(
        decay, lower, (((0,), (1,)), ((), ())), preferred_element_type=jnp.float32
    )


def block_state(keys, values, decay):
    rows, heads, width = keys.shape

    def kernel(k_ref, v_ref, decay_ref, out_ref):
        cumul, _ = decay_sums(decay_ref)
        last = cumul[rows - 1 : rows, :]
        left = jnp.exp(last - cumul)
        for at, step in turns(heads):
            k = jnp.swapaxes(k_ref[:, at : at + step, :], 0, 1)
            v = jnp.swapaxes(v_ref[:, at : at + step, :], 0, 1)
            for h in range(step):
                kept = k[h].astype(jnp.float32) * left[:, at + h : at + h + 1]
                out_ref[at + h] = tn(kept.astype(jnp.bfloat16), v[h])
        out_ref[heads] = jnp.zeros((width, width), jnp.float32)
        out_ref[heads, 0:1, 0:heads] = last

    return pl.pallas_call(
        kernel,
        out_shape=shape((heads + 1, width, width), jnp.float32),
        in_specs=[VMEM] * 3,
        out_specs=VMEM,
        compiler_params=params(24),
        cost_estimate=cost(4),
        name="block_state",
    )(keys, values, decay)


def within(queries, keys, values, decay):
    rows, heads, width = queries.shape

    def kernel(q_ref, k_ref, v_ref, decay_ref, out_ref):
        cumul, cumul_row = decay_sums(decay_ref)
        lower = triangle(rows)
        for at, step in turns(heads):
            q = jnp.swapaxes(q_ref[:, at : at + step, :], 0, 1)
            k = jnp.swapaxes(k_ref[:, at : at + step, :], 0, 1)
            v = jnp.swapaxes(v_ref[:, at : at + step, :], 0, 1)
            for h in range(step):
                i = at + h
                apart = cumul[:, i : i + 1] - cumul_row[i : i + 1, :]
                damping = jnp.where(lower, jnp.exp(jnp.where(lower, apart, 0.0)), 0.0)
                weights = (nt(q[h], k[h]) * damping).astype(jnp.bfloat16)
                out_ref[i] = nn(weights, v[h])

    return pl.pallas_call(
        kernel,
        out_shape=shape((heads, rows, width), jnp.float32),
        in_specs=[VMEM] * 4,
        out_specs=VMEM,
        compiler_params=params(24),
        cost_estimate=cost(10),
        name="within",
    )(queries, keys, values, decay)


def join_cores(place, own, other, chips):
    heads, width = own.shape[0] - 1, own.shape[-1]
    half = heads // PAIR
    few = half // chips

    def kernel(place_ref, own_ref, other_ref, *rest):
        outs, totals = rest[:-1], rest[-1]
        core, chip = place_ref[0] % PAIR, place_ref[0] // PAIR
        own_logs, other_logs = own_ref[heads, 0:1, :], other_ref[heads, 0:1, :]
        logs = own_logs + other_logs
        later = jnp.exp(jnp.where(core == 0, other_logs, own_logs))
        own_factor = jnp.where(core == 0, later, 1.0)
        other_factor = jnp.where(core == 0, 1.0, later)
        for h in range(half):
            at = core * half + h
            own_by = jnp.where(core == 0, own_factor[:, h : h + 1], own_factor[:, half + h : half + h + 1])
            other_by = jnp.where(
                core == 0, other_factor[:, h : h + 1], other_factor[:, half + h : half + h + 1]
            )
            totals[h] = (own_ref[at] * own_by + other_ref[at] * other_by).astype(jnp.bfloat16)
        first = logs.astype(jnp.bfloat16).astype(jnp.float32)
        second = (logs - first).astype(jnp.bfloat16).astype(jnp.float32)
        third = logs - first - second
        row = lax.broadcasted_iota(jnp.int32, (LOG_ROWS, width), 0)
        split = jnp.where(row == 0, first, jnp.where(row == 1, second, jnp.where(row == 2, third, 0.0)))
        for m in range(chips):
            for h in range(few):
                outs[m][span_of(h, width)] = totals[(chip ^ m) * few + h]
            outs[m][few * width :] = split.astype(jnp.bfloat16)

    return pl.pallas_call(
        kernel,
        out_shape=[shape((few * width + LOG_ROWS, width), jnp.bfloat16)] * chips,
        in_specs=[SMEM, VMEM, VMEM],
        out_specs=[VMEM] * chips,
        scratch_shapes=[pltpu.VMEM((half, width, width), jnp.bfloat16)],
        compiler_params=params(24),
        cost_estimate=cost(3),
        name="join_cores",
    )(place, own, other)


def scan_chips(place, arrived, heads):
    chips = len(arrived)
    width = arrived[0].shape[-1]
    half = heads // PAIR
    few = half // chips

    def kernel(place_ref, *rest):
        ins, outs = rest[:chips], rest[chips : 2 * chips]
        got, given, state = rest[2 * chips :]
        core, chip = place_ref[0] % PAIR, place_ref[0] // PAIR
        for m in range(chips):
            got[m] = ins[m][...]
        state[...] = jnp.zeros_like(state)
        column = lax.broadcasted_iota(jnp.int32, (1, width), 1)
        first = core * half + chip * few

        def one_chip(c, carry):
            m = c ^ chip
            logs = jnp.sum(got[m, few * width :].astype(jnp.float32), axis=0, keepdims=True)
            for h in range(few):
                span = span_of(h, width)
                here = state[span]
                given[m, span] = here.astype(jnp.bfloat16)
                log = jnp.sum(jnp.where(column == first + h, logs, 0.0), axis=1, keepdims=True)
                state[span] = here * jnp.exp(log) + got[m, span].astype(jnp.float32)
            return carry

        lax.fori_loop(0, chips, one_chip, 0)
        for m in range(chips):
            outs[m][...] = given[m]

    return pl.pallas_call(
        kernel,
        out_shape=[shape((few * width, width), jnp.bfloat16)] * chips,
        in_specs=[SMEM] + [VMEM] * chips,
        out_specs=[VMEM] * chips,
        scratch_shapes=[
            pltpu.VMEM((chips, few * width + LOG_ROWS, width), jnp.bfloat16),
            pltpu.VMEM((chips, few * width, width), jnp.bfloat16),
            pltpu.VMEM((few * width, width), jnp.float32),
        ],
        compiler_params=params(24),
        cost_estimate=cost(2),
        name="scan_chips",
    )(place, *arrived)


def gather_entry(place, arrived):
    chips = len(arrived)
    width = arrived[0].shape[-1]
    few = arrived[0].shape[0] // width

    def kernel(place_ref, *rest):
        ins, out_ref = rest[:chips], rest[chips]
        chip = place_ref[0] // PAIR
        for m in range(chips):
            for h in range(few):
                out_ref[(chip ^ m) * few + h] = ins[m][span_of(h, width)]

    return pl.pallas_call(
        kernel,
        out_shape=shape((chips * few, width, width), jnp.bfloat16),
        in_specs=[SMEM] + [VMEM] * chips,
        out_specs=VMEM,
        compiler_params=params(16),
        cost_estimate=cost(1),
        name="gather_entry",
    )(place, *arrived)


def finish(place, queries, decay, gain, inner, neighbour, entry_own, entry_other):
    rows, heads, width = queries.shape
    half = heads // PAIR

    def kernel(
        place_ref, q_ref, decay_ref, gain_ref, inner_ref, near_ref, own_ref, other_ref, out_ref, mixed
    ):
        core = place_ref[0] % PAIR
        cumul, _ = decay_sums(decay_ref)
        grown = jnp.exp(cumul)
        near_logs = near_ref[heads, 0:1, :]
        far = jnp.where(core == 0, 1.0, jnp.exp(near_logs))
        near = jnp.where(core == 0, 0.0, 1.0)
        power = jnp.zeros((rows, width), jnp.float32)
        for at, step in turns(heads):
            q = jnp.swapaxes(q_ref[:, at : at + step, :], 0, 1)
            for h in range(step):
                i = at + h
                mine, theirs = own_ref[i % half], other_ref[i % half]
                chip_entry = jnp.where(core == i // half, mine, theirs).astype(jnp.float32)
                entry = chip_entry * far[:, i : i + 1] + near_ref[i] * near
                coarse = entry.astype(jnp.bfloat16)
                fine = (entry - coarse.astype(jnp.float32)).astype(jnp.bfloat16)
                brought = (nn(q[h], coarse) + nn(q[h], fine)) * grown[:, i : i + 1]
                mix = inner_ref[i] + brought
                mixed[i] = mix
                power += mix * mix
        mean = jnp.sum(power, axis=1, keepdims=True) / (heads * width)
        norm = lax.rsqrt(mean + EPSILON)
        for at, step in turns(heads):
            normed = [
                (mixed[at + h] * norm * gain_ref[at + h : at + h + 1, :]).astype(jnp.bfloat16)
                for h in range(step)
            ]
            out_ref[:, at : at + step, :] = jnp.swapaxes(jnp.stack(normed), 0, 1)

    return pl.pallas_call(
        kernel,
        out_shape=shape((rows, heads, width), jnp.bfloat16),
        in_specs=[SMEM] + [VMEM] * 7,
        out_specs=VMEM,
        scratch_shapes=[pltpu.VMEM((heads, rows, width), jnp.float32)],
        compiler_params=params(32),
        cost_estimate=cost(8),
        name="finish",
    )(place, queries, decay, gain, inner, neighbour, entry_own, entry_other)


def per_device(
    lin_q, lin_k, lin_v, lin_decay, lin_gain, soft_q, soft_k, soft_v, block_bits, agent_ids
):
    count = lax.axis_size("seq")
    chips = count // PAIR
    rows, heads, width = soft_q.shape
    lin_heads = lin_q.shape[1]
    hosted = heads // chips
    parts = min(PARTS, hosted)
    sizes = [hosted // parts] * parts
    place = lax.axis_index("seq").astype(jnp.int32).reshape(1)
    masks = range(1, chips)

    def exchange(value, m):
        return lax.ppermute(value, "seq", [(i, i ^ (PAIR * m)) for i in range(count)])

    def exchange_all(values):
        return [values[0]] + [exchange(values[m], m) for m in masks]

    def swap_cores(value):
        return lax.ppermute(value, "seq", [(i, i ^ 1) for i in range(count)])

    def after(value, *earlier):
        return lax.optimization_barrier((value, *earlier))[0]

    def together(values):
        return list(lax.optimization_barrier(tuple(values)))

    (packed,) = pack(place, (soft_q, soft_k, soft_v), chips, sizes)
    own = exchange_all(packed)
    across = swap_cores(own[0])
    decay = after(lin_decay, packed[0])
    state = block_state(lin_k, lin_v, decay)
    near = swap_cores(state)
    inner = within(lin_q, lin_k, lin_v, after(decay, state))
    totals = exchange_all(join_cores(place, state, after(near, inner, across), chips))
    arrived = together([*own, *totals])
    own, totals = arrived[:chips], arrived[chips:]
    other = [across] + [swap_cores(block) for block in own[1:]]
    starts = scan_chips(place, totals, lin_heads)

    entries = exchange_all(starts)
    mixed = attend(place, block_bits, agent_ids, own, other, hosted)
    back = [exchange_all(mixed)]
    entry = gather_entry(place, [after(block, mixed[0]) for block in entries])
    gain = lin_gain.reshape(lin_heads, width)
    lin_out = finish(place, lin_q, lin_decay, gain, inner, near, entry, swap_cores(entry))
    back[-1][0] = after(back[-1][0], lin_out)
    soft_out = unpack(place, back, heads, rows, sizes)
    return (lin_out, soft_out)


def solution(mesh):
    rows = P(("dp", "seq"), None, None)
    return jax.shard_map(
        per_device,
        mesh=mesh,
        in_specs=(rows, rows, rows, P(("dp", "seq"), None), P(), rows, rows, rows, P("dp", None), P("dp")),
        out_specs=(rows, rows),
        check_vma=False,
    )
```

time: 89.6 us -> 83.6 us (0.933)
  Pallas kernels: 37.3 us -> 27.9 us
  starting transfers between devices: 17 us -> 20.1 us
  waiting for transfers between devices: 27.4 us -> 28.4 us
    pallas_call x5 -> x4, Pallas kernels: 25.3 us -> 12.4 us  [the longest x1 6.3 us: attend(): pl.pallas_call(kernel, out_shape=[shape((each * rows, width), jnp.bfloat1...]
    ppermute x12, starting transfers between devices: 14.8 us -> 18.1 us  [exchange(): return lax.ppermute(value, 'seq', [(i, i ^ PAIR * m) for i in range(count)])]
    ppermute x12, waiting for transfers between devices: 25.8 us -> 28.3 us  [exchange(): return lax.ppermute(value, 'seq', [(i, i ^ PAIR * m) for i in range(count)])]
    ppermute x10 -> x6, waiting for transfers between devices: 1.56 us -> 0.12 us  [swap_cores(): return lax.ppermute(value, 'seq', [(i, i ^ 1) for i in range(count)])]
    pallas_call x1, Pallas kernels: 2.07 us -> 3.47 us  [block_state(): pl.pallas_call(kernel, out_shape=shape((heads + 1, width, width), jnp.flo...]
    pallas_call x1, Pallas kernels: 3.51 us -> 4.64 us  [finish(): pl.pallas_call(kernel, out_shape=shape((rows, heads, width), jnp.bfloat16...]
    ppermute x10 -> x6, starting transfers between devices: 2.19 us -> 1.95 us  [swap_cores(): return lax.ppermute(value, 'seq', [(i, i ^ 1) for i in range(count)])]
    unnamed x44 -> x31, local copies, waits for them, and re-layouts: 5.84 us -> 5.64 us
  transfers between devices with their start and end apart: 22 -> 18, of which waited for: 6 -> 7; matrix products, arithmetic and copies ran while one was open for 1% -> 0% of each run, Pallas kernels for 33% -> 22%
where the time goes in v3:
time: 83.6 us; the launch traced here: 83.1 us
  waiting for transfers between devices  28.4 us (34%)
  Pallas kernels  27.9 us (33%)
  starting transfers between devices  20.1 us (24%)
  local copies, waits for them, and re-layouts  5.88 us (7%)
    ppermute x12, waiting for transfers between devices, exchange(): return lax.ppermute(value, 'seq', [(i, i ^ PAIR * m) for i in range(count)])  28.3 us
    ppermute x12, starting transfers between devices, exchange(): return lax.ppermute(value, 'seq', [(i, i ^ PAIR * m) for i in range(count)])  18.1 us
    pallas_call x1, Pallas kernels, attend(): pl.pallas_call(kernel, out_shape=[shape((each * rows, width), jnp.bfloat1...  6.3 us
    unnamed x31, local copies, waits for them, and re-layouts  5.64 us
    pallas_call x1, Pallas kernels, within(): pl.pallas_call(kernel, out_shape=shape((heads, rows, width), jnp.float32)...  5.01 us
    pallas_call x1, Pallas kernels, finish(): pl.pallas_call(kernel, out_shape=shape((rows, heads, width), jnp.bfloat16...  4.64 us
    pallas_call x1, Pallas kernels, pack(): pl.pallas_call(kernel, out_shape=[shape((3 * each, rows, width), jnp.bflo...  3.63 us
    pallas_call x1, Pallas kernels, block_state(): pl.pallas_call(kernel, out_shape=shape((heads + 1, width, width), jnp.flo...  3.47 us
  transfers between devices with their start and end apart: 18, of which 7 were waited for; matrix products, arithmetic and copies ran while one was open for 0% of the time, Pallas kernels for 22%

profile of v3, /device:TPU:0, one launch (start us, length us, event | category | flops | bytes accessed | tf_op | source)
XLA Modules:
  0.0 83.1 jit_solution(3309318077209399484)
XLA Ops:
  0.7 3.6 %pack.1 = (bf16[24,128,128]{2,1,0:T(8,128)(2,1)}, bf16[24,128,128]{2,1,0:T(8,128)(2,1)}, bf16[24,128,128]{2,1,0:T(8,128)(2,1)}, bf16[24,128,128]{2,1,0:T(8,128)(2,1)}) custom-call(s32[1]{0:T(128)} %bitcast.place_ref, bf16[128,32,128]{2,1,0:T(8,128)(2,1)} %q_ref.3, bf16[128,32,128]{2,1,0:T(8,128)(2,1)} %k_ref.3, bf16[128,32,128]{2,1,0:T(8,128)(2,1)} %v_ref.3), custom_call_target="tpu_custom_call" | custom-call | flops 2147483648 | bytes 1 | tf_op jit(solution)/shard_map/pack/pallas_call | solution.py:104
  4.5 3.5 %block_state.1.own_ref = f32[33,128,128]{2,1,0:T(8,128)} custom-call(bf16[128,32,128]{2,1,0:T(8,128)(2,1)S(1)} %copy-done, bf16[128,32,128]{2,1,0:T(8,128)(2,1)S(1)} %copy-done.1, bf16[128,32]{1,0:T(8,128)(2,1)S(1)} %copy.12.decay_ref), custom_call_target="tpu_custom_call" | custom-call | flops 2147483648 | bytes 1 | tf_op jit(solution)/shard_map/block_state/pallas_call | solution.py:294
  8.4 2.9 %collective-permute-start.1 = (bf16[24,128,128]{2,1,0:T(8,128)(2,1)}, bf16[24,128,128]{2,1,0:T(8,128)(2,1)}, u32[]{:S(2)}, u32[]{:S(2)}) collective-permute-start(bf16[24,128,128]{2,1,0:T(8,128)(2,1)} %get-tuple-element.37), channel_id=1, source_target_pairs={{0,2},{1,3},{2,0},{3,1},{4,6},{5,7},{6,4},{7,5},{8,10},{9,11},{10,... | collective-permute-start | bytes 2359304 | tf_op jit(solution)/shard_map/ppermute | solution.py:507
  11.4 1.5 %collective-permute-start.2 = (bf16[24,128,128]{2,1,0:T(8,128)(2,1)}, bf16[24,128,128]{2,1,0:T(8,128)(2,1)}, u32[]{:S(2)}, u32[]{:S(2)}) collective-permute-start(bf16[24,128,128]{2,1,0:T(8,128)(2,1)} %get-tuple-element.38), channel_id=1, source_target_pairs={{0,4},{1,5},{2,6},{3,7},{4,0},{5,1},{6,2},{7,3},{8,12},{9,13},{10,... | collective-permute-start | bytes 2359304 | tf_op jit(solution)/shard_map/ppermute | solution.py:507
  13.0 1.2 %copy-done.2 = bf16[128,32,128]{2,1,0:T(8,128)(2,1)S(1)} copy-done((bf16[128,32,128]{2,1,0:T(8,128)(2,1)S(1)}, bf16[128,32,128]{2,1,0:T(8,128)(2,1)}, u32[]{:S(2)}) %copy-start.2) | copy-done | bytes 1048600
  14.3 1.2 %copy-done.3 = bf16[128,32,128]{2,1,0:T(8,128)(2,1)S(1)} copy-done((bf16[128,32,128]{2,1,0:T(8,128)(2,1)S(1)}, bf16[128,32,128]{2,1,0:T(8,128)(2,1)}, u32[]{:S(2)}) %copy-start.3) | copy-done | bytes 1048600
  15.5 5.0 %within.1.inner_ref = f32[32,128,128]{2,1,0:T(8,128)S(1)} custom-call(bf16[128,32,128]{2,1,0:T(8,128)(2,1)S(1)} %copy-done.3, bf16[128,32,128]{2,1,0:T(8,128)(2,1)S(1)} %copy-done, bf16[128,32,128]{2,1,0:T(8,128)(2,1)S(1)} %copy-done.2, bf16[128,32]{1,0:T(8,128)(2,1)S(1)} %copy.13.decay_ref), custom_call_target="tpu_custom_call" | custom-call | flops 5368709120 | bytes 1 | tf_op jit(solution)/shard_map/within/pallas_call | solution.py:322
  20.5 1.3 %copy-done.10 = f32[32,128,128]{2,1,0:T(8,128)} copy-done((f32[32,128,128]{2,1,0:T(8,128)}, f32[32,128,128]{2,1,0:T(8,128)S(1)}, u32[]{:S(2)}) %copy-start.10) | copy-done | bytes 2097176
  21.8 2.0 %join_cores.1 = (bf16[528,128]{1,0:T(8,128)(2,1)S(1)}, bf16[528,128]{1,0:T(8,128)(2,1)S(1)}, bf16[528,128]{1,0:T(8,128)(2,1)S(1)}, bf16[528,128]{1,0:T(8,128)(2,1)S(1)}) custom-call(s32[1]{0:T(128)} %bitcast.place_ref, f32[33,128,128]{2,1,0:T(8,128)} %block_state.1.own_ref, f32[33,128,128]{2,1,0:T(8,128)S(1)} %collective-permute-done.other_ref.near_ref), custom_call_target="tpu_custom_call" | custom-call | flops 1610612736 | bytes 1 | tf_op jit(solution)/shard_map/join_cores/pallas_call | solution.py:363
  23.8 2.0 %collective-permute-start.5 = (bf16[528,128]{1,0:T(8,128)(2,1)S(1)}, bf16[528,128]{1,0:T(8,128)(2,1)S(1)}, u32[]{:S(2)}, u32[]{:S(2)}) collective-permute-start(bf16[528,128]{1,0:T(8,128)(2,1)S(1)} %get-tuple-element.42), channel_id=1, source_target_pairs={{0,2},{1,3},{2,0},{3,1},{4,6},{5,7},{6,4},{7,5},{8,10},{9,11},{10,... | collective-permute-start | bytes 405512 | tf_op jit(solution)/shard_map/ppermute | solution.py:507
  25.9 1.5 %collective-permute-start.6 = (bf16[528,128]{1,0:T(8,128)(2,1)S(1)}, bf16[528,128]{1,0:T(8,128)(2,1)S(1)}, u32[]{:S(2)}, u32[]{:S(2)}) collective-permute-start(bf16[528,128]{1,0:T(8,128)(2,1)S(1)} %get-tuple-element.43), channel_id=1, source_target_pairs={{0,4},{1,5},{2,6},{3,7},{4,0},{5,1},{6,2},{7,3},{8,12},{9,13},{10,... | collective-permute-start | bytes 405512 | tf_op jit(solution)/shard_map/ppermute | solution.py:507
  27.4 2.7 %collective-permute-done.1.rest_1_ = bf16[24,128,128]{2,1,0:T(8,128)(2,1)} collective-permute-done((bf16[24,128,128]{2,1,0:T(8,128)(2,1)}, bf16[24,128,128]{2,1,0:T(8,128)(2,1)}, u32[]{:S(2)}, u32[]{:S(2)}) %collective-permute-start.1) | collective-permute-done | bytes 786464 | tf_op jit(solution)/shard_map/ppermute | solution.py:507
  30.0 3.0 %collective-permute-start.7 = (bf16[528,128]{1,0:T(8,128)(2,1)S(1)}, bf16[528,128]{1,0:T(8,128)(2,1)S(1)}, u32[]{:S(2)}, u32[]{:S(2)}) collective-permute-start(bf16[528,128]{1,0:T(8,128)(2,1)S(1)} %get-tuple-element.44), channel_id=1, source_target_pairs={{0,6},{1,7},{2,4},{3,5},{4,2},{5,3},{6,0},{7,1},{8,14},{9,15},{10,... | collective-permute-start | bytes 405512 | tf_op jit(solution)/shard_map/ppermute | solution.py:507
  33.1 15.9 %collective-permute-done.2.rest_2_ = bf16[24,128,128]{2,1,0:T(8,128)(2,1)} collective-permute-done((bf16[24,128,128]{2,1,0:T(8,128)(2,1)}, bf16[24,128,128]{2,1,0:T(8,128)(2,1)}, u32[]{:S(2)}, u32[]{:S(2)}) %collective-permute-start.2) | collective-permute-done | bytes 786464 | tf_op jit(solution)/shard_map/ppermute | solution.py:507
  49.0 0.7 collective-permute-done.5.rest_1_
  49.7 3.7 %collective-permute-done.6.rest_2_ = bf16[528,128]{1,0:T(8,128)(2,1)S(1)} collective-permute-done((bf16[528,128]{1,0:T(8,128)(2,1)S(1)}, bf16[528,128]{1,0:T(8,128)(2,1)S(1)}, u32[]{:S(2)}, u32[]{:S(2)}) %collective-permute-start.6) | collective-permute-done | bytes 135200 | tf_op jit(solution)/shard_map/ppermute | solution.py:507
  53.4 0.5 collective-permute-start.8
  53.9 0.6 scan_chips.1
  54.5 1.6 %collective-permute-start.13 = (bf16[512,128]{1,0:T(8,128)(2,1)S(1)}, bf16[512,128]{1,0:T(8,128)(2,1)S(1)}, u32[]{:S(2)}, u32[]{:S(2)}) collective-permute-start(bf16[512,128]{1,0:T(8,128)(2,1)S(1)} %get-tuple-element.60), channel_id=1, source_target_pairs={{0,6},{1,7},{2,4},{3,5},{4,2},{5,3},{6,0},{7,1},{8,14},{9,15},{10,... | collective-permute-start | bytes 393224 | tf_op jit(solution)/shard_map/ppermute | solution.py:507
  56.0 1.3 %collective-permute-start.12 = (bf16[512,128]{1,0:T(8,128)(2,1)S(1)}, bf16[512,128]{1,0:T(8,128)(2,1)S(1)}, u32[]{:S(2)}, u32[]{:S(2)}) collective-permute-start(bf16[512,128]{1,0:T(8,128)(2,1)S(1)} %get-tuple-element.58), channel_id=1, source_target_pairs={{0,4},{1,5},{2,6},{3,7},{4,0},{5,1},{6,2},{7,3},{8,12},{9,13},{10,... | collective-permute-start | bytes 393224 | tf_op jit(solution)/shard_map/ppermute | solution.py:507
  57.3 0.7 collective-permute-start.11
  58.2 6.3 %attend.1 = (bf16[1024,128]{1,0:T(8,128)(2,1)S(1)}, bf16[1024,128]{1,0:T(8,128)(2,1)S(1)}, bf16[1024,128]{1,0:T(8,128)(2,1)S(1)}, bf16[1024,128]{1,0:T(8,128)(2,1)S(1)}) custom-call(s32[1]{0:T(128)} %bitcast.place_ref, s32[8,8]{1,0:T(8,128)S(1)} %copy-done.8, s32[8]{0:T(128)S(1)} %copy-done.9, bf16[24,128,128]{2,1,0:T(8,128)(2,1)} %get-tuple-element.50.rest_0_, ...), custom_call_target="tpu_custom_call" | custom-call | flops 7516192768 | bytes 1 | tf_op jit(solution)/shard_map/attend/pallas_call | solution.py:222
  64.5 0.9 %gather_entry.1.own_ref = bf16[16,128,128]{2,1,0:T(8,128)(2,1)} custom-call(s32[1]{0:T(128)} %bitcast.place_ref, bf16[512,128]{1,0:T(8,128)(2,1)S(1)} %get-tuple-element.55.rest_0_, bf16[512,128]{1,0:T(8,128)(2,1)S(1)} %collective-permute-done.11.rest_1_, bf16[512,128]{1,0:T(8,128)(2,1)S(1)} %collective-permute-done.12.rest_2_, ...), custom_call_target="tpu_custom_call" | custom-call | flops 536870912 | bytes 1 | tf_op jit(solution)/shard_map/gather_entry/pallas_call | solution.py:434
  65.6 0.9 %collective-permute-start.14 = (bf16[16,128,128]{2,1,0:T(8,128)(2,1)}, bf16[16,128,128]{2,1,0:T(8,128)(2,1)}, u32[]{:S(2)}, u32[]{:S(2)}) collective-permute-start(bf16[16,128,128]{2,1,0:T(8,128)(2,1)} %gather_entry.1.own_ref), channel_id=1, source_target_pairs={{0,1},{1,0},{2,3},{3,2},{4,5},{5,4},{6,7},{7,6},{8,9},{9,8},{10,11... | collective-permute-start | bytes 1572872 | tf_op jit(solution)/shard_map/ppermute | solution.py:513
  66.6 1.3 %collective-permute-start.15 = (bf16[1024,128]{1,0:T(8,128)(2,1)}, bf16[1024,128]{1,0:T(8,128)(2,1)S(1)}, u32[]{:S(2)}, u32[]{:S(2)}) collective-permute-start(bf16[1024,128]{1,0:T(8,128)(2,1)} %copy-done.6), channel_id=1, source_target_pairs={{0,2},{1,3},{2,0},{3,1},{4,6},{5,7},{6,4},{7,5},{8,10},{9,11},{10,... | collective-permute-start | bytes 786440 | tf_op jit(solution)/shard_map/ppermute | solution.py:507
  67.9 0.8 collective-permute-start.16
  68.7 1.4 %collective-permute-start.17 = (bf16[1024,128]{1,0:T(8,128)(2,1)S(1)}, bf16[1024,128]{1,0:T(8,128)(2,1)S(1)}, u32[]{:S(2)}, u32[]{:S(2)}) collective-permute-start(bf16[1024,128]{1,0:T(8,128)(2,1)S(1)} %get-tuple-element.65), channel_id=1, source_target_pairs={{0,6},{1,7},{2,4},{3,5},{4,2},{5,3},{6,0},{7,1},{8,14},{9,15},{10,... | collective-permute-start | bytes 786440 | tf_op jit(solution)/shard_map/ppermute | solution.py:507
  70.2 1.6 %copy-done.11 = f32[32,128,128]{2,1,0:T(8,128)S(1)} copy-done((f32[32,128,128]{2,1,0:T(8,128)S(1)}, f32[32,128,128]{2,1,0:T(8,128)}, u32[]{:S(2)}) %copy-start.11) | copy-done | bytes 2097176
  71.8 4.6 %finish.1 = bf16[128,32,128]{2,1,0:T(8,128)(2,1)} custom-call(s32[1]{0:T(128)} %bitcast.place_ref, bf16[128,32,128]{2,1,0:T(8,128)(2,1)S(1)} %copy-done.4, bf16[128,32]{1,0:T(8,128)(2,1)S(1)} %copy.14.decay_ref, f32[32,128]{1,0:T(8,128)S(1)} %bitcast.2, f32[32,128,128]{2,1,0:T(8,128)S(1)} %copy-done.11, ...), custom_call_target="tpu_custom_call" | custom-call | flops 4294967296 | bytes 1 | tf_op jit(solution)/shard_map/finish/pallas_call | solution.py:481
  76.4 3.7 %collective-permute-done.16.rest_2_ = bf16[1024,128]{1,0:T(8,128)(2,1)S(1)} collective-permute-done((bf16[1024,128]{1,0:T(8,128)(2,1)}, bf16[1024,128]{1,0:T(8,128)(2,1)S(1)}, u32[]{:S(2)}, u32[]{:S(2)}) %collective-permute-start.16) | collective-permute-done | bytes 262176 | tf_op jit(solution)/shard_map/ppermute | solution.py:507
  80.1 1.6 %collective-permute-done.17.rest_3_ = bf16[1024,128]{1,0:T(8,128)(2,1)S(1)} collective-permute-done((bf16[1024,128]{1,0:T(8,128)(2,1)S(1)}, bf16[1024,128]{1,0:T(8,128)(2,1)S(1)}, u32[]{:S(2)}, u32[]{:S(2)}) %collective-permute-start.17) | collective-permute-done | bytes 262176 | tf_op jit(solution)/shard_map/ppermute | solution.py:507
  81.7 1.4 %unpack.1 = bf16[128,32,128]{2,1,0:T(8,128)(2,1)} custom-call(s32[1]{0:T(128)} %bitcast.place_ref, bf16[1024,128]{1,0:T(8,128)(2,1)S(1)} %copy-done.13, bf16[1024,128]{1,0:T(8,128)(2,1)S(1)} %collective-permute-done.15.rest_1_, bf16[1024,128]{1,0:T(8,128)(2,1)S(1)} %collective-permute-done.16.rest_2_, bf16[1024,128]{1,0:T(8,128)(2,1)S(1)} %collective-permute-done.17.rest_3_), custom_call_target="tpu_custom_call" | custom-call | flops 2147483648 | bytes 1 | tf_op jit(solution)/shard_map/unpack/pallas_call | solution.py:258
  (46 shorter events, 1.2 us)
Async XLA Ops:
  0.6 3.7 %copy-start.14 = (bf16[128,32]{0,1:T(8,128)(2,1)S(1)}, bf16[128,32]{0,1:T(8,128)(2,1)}, u32[]{:S(2)}) copy-start(bf16[128,32]{0,1:T(8,128)(2,1)} %param.13) | copy-start | bytes 24580
  0.6 3.8 %copy-start = (bf16[128,32,128]{2,1,0:T(8,128)(2,1)S(1)}, bf16[128,32,128]{2,1,0:T(8,128)(2,1)}, u32[]{:S(2)}) copy-start(bf16[128,32,128]{2,1,0:T(8,128)(2,1)} %k_ref.5) | copy-start | bytes 3145732
  0.7 3.8 %copy-start.1 = (bf16[128,32,128]{2,1,0:T(8,128)(2,1)S(1)}, bf16[128,32,128]{2,1,0:T(8,128)(2,1)}, u32[]{:S(2)}) copy-start(bf16[128,32,128]{2,1,0:T(8,128)(2,1)} %v_ref.5) | copy-start | bytes 3145732
  7.9 13.9 %collective-permute-start = (f32[33,128,128]{2,1,0:T(8,128)}, f32[33,128,128]{2,1,0:T(8,128)S(1)}, u32[]{:S(2)}, u32[]{:S(2)}) collective-permute-start(f32[33,128,128]{2,1,0:T(8,128)} %block_state.1.own_ref), channel_id=1, source_target_pairs={{0,1},{1,0},{2,3},{3,2},{4,5},{5,4},{6,7},{7,6},{8,9},{9,8},{10,11... | collective-permute-start | bytes 6488072 | tf_op jit(solution)/shard_map/ppermute | solution.py:513
  8.4 13.5 %collective-permute-start.4 = (bf16[24,128,128]{2,1,0:T(8,128)(2,1)}, bf16[24,128,128]{2,1,0:T(8,128)(2,1)}, u32[]{:S(2)}, u32[]{:S(2)}) collective-permute-start(bf16[24,128,128]{2,1,0:T(8,128)(2,1)} %get-tuple-element.50.rest_0_), channel_id=1, source_target_pairs={{0,1},{1,0},{2,3},{3,2},{4,5},{5,4},{6,7},{7,6},{8,9},{9,8},{10,11... | collective-permute-start | bytes 2359304 | tf_op jit(solution)/shard_map/ppermute | solution.py:513
  8.4 21.6 %collective-permute-start.1 = (bf16[24,128,128]{2,1,0:T(8,128)(2,1)}, bf16[24,128,128]{2,1,0:T(8,128)(2,1)}, u32[]{:S(2)}, u32[]{:S(2)}) collective-permute-start(bf16[24,128,128]{2,1,0:T(8,128)(2,1)} %get-tuple-element.37), channel_id=1, source_target_pairs={{0,2},{1,3},{2,0},{3,1},{4,6},{5,7},{6,4},{7,5},{8,10},{9,11},{10,... | collective-permute-start | bytes 2359304 | tf_op jit(solution)/shard_map/ppermute | solution.py:507
  11.4 37.6 %collective-permute-start.2 = (bf16[24,128,128]{2,1,0:T(8,128)(2,1)}, bf16[24,128,128]{2,1,0:T(8,128)(2,1)}, u32[]{:S(2)}, u32[]{:S(2)}) collective-permute-start(bf16[24,128,128]{2,1,0:T(8,128)(2,1)} %get-tuple-element.38), channel_id=1, source_target_pairs={{0,4},{1,5},{2,6},{3,7},{4,0},{5,1},{6,2},{7,3},{8,12},{9,13},{10,... | collective-permute-start | bytes 2359304 | tf_op jit(solution)/shard_map/ppermute | solution.py:507
  12.9 36.1 %collective-permute-start.3 = (bf16[24,128,128]{2,1,0:T(8,128)(2,1)}, bf16[24,128,128]{2,1,0:T(8,128)(2,1)}, u32[]{:S(2)}, u32[]{:S(2)}) collective-permute-start(bf16[24,128,128]{2,1,0:T(8,128)(2,1)} %get-tuple-element.39), channel_id=1, source_target_pairs={{0,6},{1,7},{2,4},{3,5},{4,2},{5,3},{6,0},{7,1},{8,14},{9,15},{10,... | collective-permute-start | bytes 2359304 | tf_op jit(solution)/shard_map/ppermute | solution.py:507
  13.0 1.2 %copy-start.2 = (bf16[128,32,128]{2,1,0:T(8,128)(2,1)S(1)}, bf16[128,32,128]{2,1,0:T(8,128)(2,1)}, u32[]{:S(2)}) copy-start(bf16[128,32,128]{2,1,0:T(8,128)(2,1)} %v_ref.5) | copy-start | bytes 3145732
  14.3 1.2 %copy-start.3 = (bf16[128,32,128]{2,1,0:T(8,128)(2,1)S(1)}, bf16[128,32,128]{2,1,0:T(8,128)(2,1)}, u32[]{:S(2)}) copy-start(bf16[128,32,128]{2,1,0:T(8,128)(2,1)} %q_ref.5) | copy-start | bytes 3145732
  20.5 1.3 %copy-start.10 = (f32[32,128,128]{2,1,0:T(8,128)}, f32[32,128,128]{2,1,0:T(8,128)S(1)}, u32[]{:S(2)}) copy-start(f32[32,128,128]{2,1,0:T(8,128)S(1)} %within.1.inner_ref) | copy-start | bytes 6291460
  23.8 34.3 %copy-start.8 = (s32[8,8]{1,0:T(8,128)S(1)}, s32[8,8]{1,0:T(8,128)}, u32[]{:S(2)}) copy-start(s32[8,8]{1,0:T(8,128)} %bits_ref.1) | copy-start | bytes 772
  23.8 34.3 %copy-start.9 = (s32[8]{0:T(128)S(1)}, s32[8]{0:T(128)}, u32[]{:S(2)}) copy-start(s32[8]{0:T(128)} %agents_ref.1) | copy-start | bytes 100
  23.8 25.9 %collective-permute-start.5 = (bf16[528,128]{1,0:T(8,128)(2,1)S(1)}, bf16[528,128]{1,0:T(8,128)(2,1)S(1)}, u32[]{:S(2)}, u32[]{:S(2)}) collective-permute-start(bf16[528,128]{1,0:T(8,128)(2,1)S(1)} %get-tuple-element.42), channel_id=1, source_target_pairs={{0,2},{1,3},{2,0},{3,1},{4,6},{5,7},{6,4},{7,5},{8,10},{9,11},{10,... | collective-permute-start | bytes 405512 | tf_op jit(solution)/shard_map/ppermute | solution.py:507
  25.9 27.5 %collective-permute-start.6 = (bf16[528,128]{1,0:T(8,128)(2,1)S(1)}, bf16[528,128]{1,0:T(8,128)(2,1)S(1)}, u32[]{:S(2)}, u32[]{:S(2)}) collective-permute-start(bf16[528,128]{1,0:T(8,128)(2,1)S(1)} %get-tuple-element.43), channel_id=1, source_target_pairs={{0,4},{1,5},{2,6},{3,7},{4,0},{5,1},{6,2},{7,3},{8,12},{9,13},{10,... | collective-permute-start | bytes 405512 | tf_op jit(solution)/shard_map/ppermute | solution.py:507
  30.0 23.4 %collective-permute-start.7 = (bf16[528,128]{1,0:T(8,128)(2,1)S(1)}, bf16[528,128]{1,0:T(8,128)(2,1)S(1)}, u32[]{:S(2)}, u32[]{:S(2)}) collective-permute-start(bf16[528,128]{1,0:T(8,128)(2,1)S(1)} %get-tuple-element.44), channel_id=1, source_target_pairs={{0,6},{1,7},{2,4},{3,5},{4,2},{5,3},{6,0},{7,1},{8,14},{9,15},{10,... | collective-permute-start | bytes 405512 | tf_op jit(solution)/shard_map/ppermute | solution.py:507
  53.4 3.9 %collective-permute-start.10 = (bf16[24,128,128]{2,1,0:T(8,128)(2,1)}, bf16[24,128,128]{2,1,0:T(8,128)(2,1)S(1)}, u32[]{:S(2)}, u32[]{:S(2)}) collective-permute-start(bf16[24,128,128]{2,1,0:T(8,128)(2,1)} %collective-permute-done.3.rest_3_), channel_id=1, source_target_pairs={{0,1},{1,0},{2,3},{3,2},{4,5},{5,4},{6,7},{7,6},{8,9},{9,8},{10,11... | collective-permute-start | bytes 2359304 | tf_op jit(solution)/shard_map/ppermute | solution.py:513
  53.4 4.6 %collective-permute-start.8 = (bf16[24,128,128]{2,1,0:T(8,128)(2,1)}, bf16[24,128,128]{2,1,0:T(8,128)(2,1)S(1)}, u32[]{:S(2)}, u32[]{:S(2)}) collective-permute-start(bf16[24,128,128]{2,1,0:T(8,128)(2,1)} %collective-permute-done.1.rest_1_), channel_id=1, source_target_pairs={{0,1},{1,0},{2,3},{3,2},{4,5},{5,4},{6,7},{7,6},{8,9},{9,8},{10,11... | collective-permute-start | bytes 2359304 | tf_op jit(solution)/shard_map/ppermute | solution.py:513
  53.9 4.2 %collective-permute-start.9 = (bf16[24,128,128]{2,1,0:T(8,128)(2,1)}, bf16[24,128,128]{2,1,0:T(8,128)(2,1)S(1)}, u32[]{:S(2)}, u32[]{:S(2)}) collective-permute-start(bf16[24,128,128]{2,1,0:T(8,128)(2,1)} %collective-permute-done.2.rest_2_), channel_id=1, source_target_pairs={{0,1},{1,0},{2,3},{3,2},{4,5},{5,4},{6,7},{7,6},{8,9},{9,8},{10,11... | collective-permute-start | bytes 2359304 | tf_op jit(solution)/shard_map/ppermute | solution.py:513
  54.5 10.0 %collective-permute-start.13 = (bf16[512,128]{1,0:T(8,128)(2,1)S(1)}, bf16[512,128]{1,0:T(8,128)(2,1)S(1)}, u32[]{:S(2)}, u32[]{:S(2)}) collective-permute-start(bf16[512,128]{1,0:T(8,128)(2,1)S(1)} %get-tuple-element.60), channel_id=1, source_target_pairs={{0,6},{1,7},{2,4},{3,5},{4,2},{5,3},{6,0},{7,1},{8,14},{9,15},{10,... | collective-permute-start | bytes 393224 | tf_op jit(solution)/shard_map/ppermute | solution.py:507
  56.0 8.5 %collective-permute-start.12 = (bf16[512,128]{1,0:T(8,128)(2,1)S(1)}, bf16[512,128]{1,0:T(8,128)(2,1)S(1)}, u32[]{:S(2)}, u32[]{:S(2)}) collective-permute-start(bf16[512,128]{1,0:T(8,128)(2,1)S(1)} %get-tuple-element.58), channel_id=1, source_target_pairs={{0,4},{1,5},{2,6},{3,7},{4,0},{5,1},{6,2},{7,3},{8,12},{9,13},{10,... | collective-permute-start | bytes 393224 | tf_op jit(solution)/shard_map/ppermute | solution.py:507
  57.3 12.9 %copy-start.4 = (bf16[128,32,128]{2,1,0:T(8,128)(2,1)S(1)}, bf16[128,32,128]{2,1,0:T(8,128)(2,1)}, u32[]{:S(2)}) copy-start(bf16[128,32,128]{2,1,0:T(8,128)(2,1)} %q_ref.5) | copy-start | bytes 3145732
  57.3 12.9 %copy-start.7 = (f32[4096]{0:T(1024)S(1)}, f32[4096]{0:T(1024)}, u32[]{:S(2)}) copy-start(f32[4096]{0:T(1024)} %param.14) | copy-start | bytes 49156
  57.3 7.2 %collective-permute-start.11 = (bf16[512,128]{1,0:T(8,128)(2,1)S(1)}, bf16[512,128]{1,0:T(8,128)(2,1)S(1)}, u32[]{:S(2)}, u32[]{:S(2)}) collective-permute-start(bf16[512,128]{1,0:T(8,128)(2,1)S(1)} %get-tuple-element.56), channel_id=1, source_target_pairs={{0,2},{1,3},{2,0},{3,1},{4,6},{5,7},{6,4},{7,5},{8,10},{9,11},{10,... | collective-permute-start | bytes 393224 | tf_op jit(solution)/shard_map/ppermute | solution.py:507
  64.5 1.0 %copy-start.5 = (bf16[1024,128]{1,0:T(8,128)(2,1)}, bf16[1024,128]{1,0:T(8,128)(2,1)S(1)}, u32[]{:S(2)}) copy-start(bf16[1024,128]{1,0:T(8,128)(2,1)S(1)} %get-tuple-element.64) | copy-start | bytes 786436
  64.5 1.1 %copy-start.12 = (bf16[1024,128]{1,0:T(8,128)(2,1)}, bf16[1024,128]{1,0:T(8,128)(2,1)S(1)}, u32[]{:S(2)}) copy-start(bf16[1024,128]{1,0:T(8,128)(2,1)S(1)} %get-tuple-element.62.rest_0_) | copy-start | bytes 786436
  65.6 4.6 %collective-permute-start.14 = (bf16[16,128,128]{2,1,0:T(8,128)(2,1)}, bf16[16,128,128]{2,1,0:T(8,128)(2,1)}, u32[]{:S(2)}, u32[]{:S(2)}) collective-permute-start(bf16[16,128,128]{2,1,0:T(8,128)(2,1)} %gather_entry.1.own_ref), channel_id=1, source_target_pairs={{0,1},{1,0},{2,3},{3,2},{4,5},{5,4},{6,7},{7,6},{8,9},{9,8},{10,11... | collective-permute-start | bytes 1572872 | tf_op jit(solution)/shard_map/ppermute | solution.py:513
  66.6 9.8 %collective-permute-start.15 = (bf16[1024,128]{1,0:T(8,128)(2,1)}, bf16[1024,128]{1,0:T(8,128)(2,1)S(1)}, u32[]{:S(2)}, u32[]{:S(2)}) collective-permute-start(bf16[1024,128]{1,0:T(8,128)(2,1)} %copy-done.6), channel_id=1, source_target_pairs={{0,2},{1,3},{2,0},{3,1},{4,6},{5,7},{6,4},{7,5},{8,10},{9,11},{10,... | collective-permute-start | bytes 786440 | tf_op jit(solution)/shard_map/ppermute | solution.py:507
  67.9 12.2 %collective-permute-start.16 = (bf16[1024,128]{1,0:T(8,128)(2,1)}, bf16[1024,128]{1,0:T(8,128)(2,1)S(1)}, u32[]{:S(2)}, u32[]{:S(2)}) collective-permute-start(bf16[1024,128]{1,0:T(8,128)(2,1)} %copy-done.5), channel_id=1, source_target_pairs={{0,4},{1,5},{2,6},{3,7},{4,0},{5,1},{6,2},{7,3},{8,12},{9,13},{10,... | collective-permute-start | bytes 786440 | tf_op jit(solution)/shard_map/ppermute | solution.py:507
  68.7 13.0 %collective-permute-start.17 = (bf16[1024,128]{1,0:T(8,128)(2,1)S(1)}, bf16[1024,128]{1,0:T(8,128)(2,1)S(1)}, u32[]{:S(2)}, u32[]{:S(2)}) collective-permute-start(bf16[1024,128]{1,0:T(8,128)(2,1)S(1)} %get-tuple-element.65), channel_id=1, source_target_pairs={{0,6},{1,7},{2,4},{3,5},{4,2},{5,3},{6,0},{7,1},{8,14},{9,15},{10,... | collective-permute-start | bytes 786440 | tf_op jit(solution)/shard_map/ppermute | solution.py:507
  70.2 1.6 %copy-start.11 = (f32[32,128,128]{2,1,0:T(8,128)S(1)}, f32[32,128,128]{2,1,0:T(8,128)}, u32[]{:S(2)}) copy-start(f32[32,128,128]{2,1,0:T(8,128)} %copy-done.10) | copy-start | bytes 6291460
  71.8 10.0 %copy-start.13 = (bf16[1024,128]{1,0:T(8,128)(2,1)S(1)}, bf16[1024,128]{1,0:T(8,128)(2,1)}, u32[]{:S(2)}) copy-start(bf16[1024,128]{1,0:T(8,128)(2,1)} %copy-done.12) | copy-start | bytes 786436
  (1 other events, 1.0 us)

commit v4 on v3

--- a/solution.py
+++ b/solution.py
@@ -8,16 +8,14 @@
 EPSILON = 1e-06
 PAIR = 2
 ABREAST = 2
-EARLY = 2
-PACK_MIB = 56
 WEIGHT = 1 << 29
-PARTS = 1
 TURN = 8
 LOG_ROWS = 16
 LOG2E = 1.4426950408889634
 VMEM = pl.BlockSpec(memory_space=pltpu.VMEM)
 SMEM = pl.BlockSpec(memory_space=pltpu.SMEM)
 ANY = pl.BlockSpec(memory_space=pl.ANY)
+HBM = pl.BlockSpec(memory_space=pltpu.HBM)
 
 
 def params(mib):
@@ -59,14 +57,14 @@
     return cols <= rows
 
 
-def pack(place, arrays, chips, sizes):
+def pack(place, arrays, decay, chips):
     rows, heads, width = arrays[0].shape
-    hosted = sum(sizes)
+    hosted, lin_heads = heads // chips, decay.shape[0]
     pieces = 2
     cut = rows // pieces
 
-    def kernel(place_ref, q_ref, k_ref, v_ref, *rest):
-        outs, (landed, turned, in_sems, out_sems) = rest[:-4], rest[-4:]
+    def kernel(place_ref, decay_ref, q_ref, k_ref, v_ref, *rest):
+        outs, (landed, turned, padded, in_sems, out_sems) = rest[:-5], rest[-5:]
         chip = place_ref[0] // PAIR
         arriving = [
             pltpu.make_async_copy(
@@ -79,7 +77,12 @@
         ]
         for copy in arriving:
             copy.start()
-        leaving = []
+        padded[...] = jnp.zeros_like(padded)
+        padded[0, 0:lin_heads, :] = decay_ref[...]
+        leaving = [
+            pltpu.make_async_copy(padded, outs[0].at[pl.ds(3 * hosted, 1)], out_sems.at[3 * chips])
+        ]
+        leaving[-1].start()
         for which in range(3):
             for piece in range(pieces):
                 arriving[which * pieces + piece].wait()
@@ -87,36 +90,34 @@
                 block = jnp.swapaxes(landed[which, :, at : at + step, :], 0, 1)
                 for h in range(step):
                     turned[which, at + h] = block[h].T if which == 1 else block[h]
-            for part, each in enumerate(sizes):
-                for m in range(chips):
-                    first = (chip ^ m) * hosted + sum(sizes[:part])
-                    leaving.append(
-                        pltpu.make_async_copy(
-                            turned.at[which, pl.ds(first, each)],
-                            outs[part * chips + m].at[pl.ds(which * each, each)],
-                            out_sems.at[len(leaving)],
-                        )
+            for m in range(chips):
+                leaving.append(
+                    pltpu.make_async_copy(
+                        turned.at[which, pl.ds((chip ^ m) * hosted, hosted)],
+                        outs[m].at[pl.ds(which * hosted, hosted)],
+                        out_sems.at[which * chips + m],
                     )
-                    leaving[-1].start()
+                )
+                leaving[-1].start()
         for copy in leaving:
             copy.wait()
 
-    outs = pl.pallas_call(
-        kernel,
-        out_shape=[shape((3 * each, rows, width), jnp.bfloat16) for each in sizes for _ in range(chips)],
-        in_specs=[SMEM, ANY, ANY, ANY],
-        out_specs=[ANY] * (chips * len(sizes)),
+    return pl.pallas_call(
+        kernel,
+        out_shape=[shape((3 * hosted + (m == 0), rows, width), jnp.bfloat16) for m in range(chips)],
+        in_specs=[SMEM, VMEM, ANY, ANY, ANY],
+        out_specs=[ANY] * chips,
         scratch_shapes=[
             pltpu.VMEM((3, rows, heads, width), jnp.bfloat16),
             pltpu.VMEM((3, heads, rows, width), jnp.bfloat16),
+            pltpu.VMEM((1, rows, width), jnp.bfloat16),
             pltpu.SemaphoreType.DMA((3, pieces)),
-            pltpu.SemaphoreType.DMA((3 * chips * len(sizes),)),
+            pltpu.SemaphoreType.DMA((3 * chips + 1,)),
         ],
-        compiler_params=params(PACK_MIB),
+        compiler_params=params(56),
         cost_estimate=cost(4),
         name="pack",
-    )(place, *arrays)
-    return [list(outs[part * chips : (part + 1) * chips]) for part in range(len(sizes))]
+    )(place, decay, *arrays)
 
 
 def attend(place, bits, agents, own, other, each):
@@ -136,7 +137,7 @@
             pltpu.make_async_copy(ins[j].at[pl.ds(at, size)], held.at[j, pl.ds(at, size)], sems.at[j])
             for j, (at, size) in enumerate(spans)
         ]
-        for copy in copies:
+        for copy in copies[:chips]:
             copy.start()
 
         found = jnp.int32(0)
@@ -163,6 +164,8 @@
         lower = triangle(rows)
         for copy in copies[:chips]:
             copy.wait()
+        for copy in copies[chips:]:
+            copy.start()
         for i in range(chips):
             for h in range(each):
                 top[i, h] = jnp.where(lower, nn(head(i, 0, h), head(i, 1, h)), -1e30)
@@ -241,72 +244,111 @@
     )(place, bits, agents, *own, *other)
 
 
-def unpack(place, pieces, heads, rows, sizes):
-    chips, width = len(pieces[0]), pieces[0][0].shape[-1]
+def unpack(place, pieces, heads, rows):
+    chips, width = len(pieces), pieces[0].shape[-1]
+    hosted = heads // chips
 
     def kernel(place_ref, *rest):
         ins, out_ref, turned = rest[:-2], rest[-2], rest[-1]
         chip = place_ref[0] // PAIR
-        for part, each in enumerate(sizes):
-            for m in range(chips):
-                first = (chip ^ m) * sum(sizes) + sum(sizes[:part])
-                for h in range(each):
-                    turned[first + h] = ins[part * chips + m][span_of(h, rows)]
+        for m in range(chips):
+            for h in range(hosted):
+                turned[(chip ^ m) * hosted + h] = ins[m][span_of(h, rows)]
         for at, step in turns(heads):
             out_ref[:, at : at + step, :] = jnp.swapaxes(turned[at : at + step], 0, 1)
 
     return pl.pallas_call(
         kernel,
         out_shape=shape((rows, heads, width), jnp.bfloat16),
-        in_specs=[SMEM] + [VMEM] * (chips * len(sizes)),
+        in_specs=[SMEM] + [VMEM] * chips,
         out_specs=VMEM,
         scratch_shapes=[pltpu.VMEM((heads, rows, width), jnp.bfloat16)],
         compiler_params=params(16),
         cost_estimate=cost(4),
         name="unpack",
-    )(place, *[piece for part in pieces for piece in part])
-
-
-def decay_sums(decay_ref):
-    decay = decay_ref[...]
-    lower = triangle(decay.shape[0]).astype(jnp.bfloat16)
-    return nn(lower, decay), lax.dot_general(
-        decay, lower, (((0,), (1,)), ((), ())), preferred_element_type=jnp.float32
-    )
-
-
-def block_state(keys, values, decay):
+    )(place, *pieces)
+
+
+def decay_sums(decay):
+    lower = triangle(decay.shape[1]).astype(jnp.bfloat16)
+    return nt(lower, decay), nt(decay, lower)
+
+
+def block_state(key, value, left):
+    return tn((key.astype(jnp.float32) * left).astype(jnp.bfloat16), value)
+
+
+def totals_of(place, keys, values, decay, near_keys, near_values, across, chips):
     rows, heads, width = keys.shape
-
-    def kernel(k_ref, v_ref, decay_ref, out_ref):
-        cumul, _ = decay_sums(decay_ref)
-        last = cumul[rows - 1 : rows, :]
-        left = jnp.exp(last - cumul)
-        for at, step in turns(heads):
-            k = jnp.swapaxes(k_ref[:, at : at + step, :], 0, 1)
-            v = jnp.swapaxes(v_ref[:, at : at + step, :], 0, 1)
-            for h in range(step):
-                kept = k[h].astype(jnp.float32) * left[:, at + h : at + h + 1]
-                out_ref[at + h] = tn(kept.astype(jnp.bfloat16), v[h])
-        out_ref[heads] = jnp.zeros((width, width), jnp.float32)
-        out_ref[heads, 0:1, 0:heads] = last
-
-    return pl.pallas_call(
-        kernel,
-        out_shape=shape((heads + 1, width, width), jnp.float32),
-        in_specs=[VMEM] * 3,
-        out_specs=VMEM,
+    half = heads // PAIR
+    few = half // chips
+    slot = across.shape[0] - 1
+
+    def kernel(place_ref, k_ref, v_ref, decay_ref, near_k_ref, near_v_ref, across_ref, *rest):
+        outs, (turned, near_decay, totals, sem) = rest[:chips], rest[chips:]
+        core, chip = place_ref[0] % PAIR, place_ref[0] // PAIR
+        copy = pltpu.make_async_copy(across_ref.at[pl.ds(slot, 1)], near_decay, sem)
+        copy.start()
+        for which, ref in enumerate((k_ref, v_ref, near_k_ref, near_v_ref)):
+            for at, step in turns(heads):
+                turned[which, at : at + step] = jnp.swapaxes(ref[:, at : at + step, :], 0, 1)
+        copy.wait()
+        own_sums, _ = decay_sums(decay_ref[...])
+        near_sums, _ = decay_sums(near_decay[0, 0:heads, :])
+        own_last, near_last = own_sums[rows - 1 : rows, :], near_sums[rows - 1 : rows, :]
+        own_left = jnp.exp(own_last - own_sums)
+        near_left = jnp.exp(near_last - near_sums)
+        own_then = jnp.where(core == 0, jnp.exp(near_last), 1.0)
+        near_then = jnp.where(core == 0, 1.0, jnp.exp(own_last))
+
+        def half_of(sums):
+            return jnp.where(core == 0, sums[:, 0:half], sums[:, half:heads])
+
+        own_left, near_left, own_then, near_then = map(half_of, (own_left, near_left, own_then, near_then))
+        for h in range(half):
+            at = core * half + h
+            own = block_state(turned[0, at], turned[1, at], own_left[:, h : h + 1])
+            near = block_state(turned[2, at], turned[3, at], near_left[:, h : h + 1])
+            total = own * own_then[:, h : h + 1] + near * near_then[:, h : h + 1]
+            totals[h] = total.astype(jnp.bfloat16)
+        logs = jnp.concatenate([own_last + near_last, jnp.zeros((1, width - heads), jnp.float32)], axis=1)
+        first = logs.astype(jnp.bfloat16).astype(jnp.float32)
+        second = (logs - first).astype(jnp.bfloat16).astype(jnp.float32)
+        third = logs - first - second
+        row = lax.broadcasted_iota(jnp.int32, (LOG_ROWS, width), 0)
+        split = jnp.where(row == 0, first, jnp.where(row == 1, second, jnp.where(row == 2, third, 0.0)))
+        for m in range(chips):
+            for h in range(few):
+                outs[m][span_of(h, width)] = totals[(chip ^ m) * few + h]
+            outs[m][few * width :] = split.astype(jnp.bfloat16)
+
+    return pl.pallas_call(
+        kernel,
+        out_shape=[shape((few * width + LOG_ROWS, width), jnp.bfloat16)] * chips,
+        in_specs=[SMEM] + [VMEM] * 5 + [ANY],
+        out_specs=[VMEM] * chips,
+        scratch_shapes=[
+            pltpu.VMEM((4, heads, rows, width), jnp.bfloat16),
+            pltpu.VMEM((1, rows, width), jnp.bfloat16),
+            pltpu.VMEM((half, width, width), jnp.bfloat16),
+            pltpu.SemaphoreType.DMA,
+        ],
         compiler_params=params(24),
-        cost_estimate=cost(4),
-        name="block_state",
-    )(keys, values, decay)
-
-
-def within(queries, keys, values, decay):
+        cost_estimate=cost(6),
+        name="totals_of",
+    )(place, keys, values, decay, near_keys, near_values, across)
+
+
+def within(place, queries, keys, values, decay, near_keys, near_values, across):
     rows, heads, width = queries.shape
-
-    def kernel(q_ref, k_ref, v_ref, decay_ref, out_ref):
-        cumul, cumul_row = decay_sums(decay_ref)
+    slot = across.shape[0] - 1
+
+    def kernel(place_ref, q_ref, k_ref, v_ref, decay_ref, near_k_ref, near_v_ref, across_ref, out_ref, near_decay, sem):
+        core = place_ref[0] % PAIR
+        copy = pltpu.make_async_copy(across_ref.at[pl.ds(slot, 1)], near_decay, sem)
+        copy.start()
+        cumul, cumul_row = decay_sums(decay_ref[...])
+        grown = jnp.exp(cumul)
         lower = triangle(rows)
         for at, step in turns(heads):
             q = jnp.swapaxes(q_ref[:, at : at + step, :], 0, 1)
@@ -318,58 +360,37 @@
                 damping = jnp.where(lower, jnp.exp(jnp.where(lower, apart, 0.0)), 0.0)
                 weights = (nt(q[h], k[h]) * damping).astype(jnp.bfloat16)
                 out_ref[i] = nn(weights, v[h])
+        copy.wait()
+
+        @pl.when(core > 0)
+        def _():
+            near_sums, _ = decay_sums(near_decay[0, 0:heads, :])
+            left = jnp.exp(near_sums[rows - 1 : rows, :] - near_sums)
+            for at, step in turns(heads):
+                q = jnp.swapaxes(q_ref[:, at : at + step, :], 0, 1)
+                k = jnp.swapaxes(near_k_ref[:, at : at + step, :], 0, 1)
+                v = jnp.swapaxes(near_v_ref[:, at : at + step, :], 0, 1)
+                for h in range(step):
+                    i = at + h
+                    state = block_state(k[h], v[h], left[:, i : i + 1])
+                    out_ref[i] += precisely(q[h], state) * grown[:, i : i + 1]
 
     return pl.pallas_call(
         kernel,
         out_shape=shape((heads, rows, width), jnp.float32),
-        in_specs=[VMEM] * 4,
+        in_specs=[SMEM] + [VMEM] * 6 + [ANY],
         out_specs=VMEM,
+        scratch_shapes=[pltpu.VMEM((1, rows, width), jnp.bfloat16), pltpu.SemaphoreType.DMA],
         compiler_params=params(24),
-        cost_estimate=cost(10),
+        cost_estimate=cost(14),
         name="within",
-    )(queries, keys, values, decay)
-
-
-def join_cores(place, own, other, chips):
-    heads, width = own.shape[0] - 1, own.shape[-1]
-    half = heads // PAIR
-    few = half // chips
-
-    def kernel(place_ref, own_ref, other_ref, *rest):
-        outs, totals = rest[:-1], rest[-1]
-        core, chip = place_ref[0] % PAIR, place_ref[0] // PAIR
-        own_logs, other_logs = own_ref[heads, 0:1, :], other_ref[heads, 0:1, :]
-        logs = own_logs + other_logs
-        later = jnp.exp(jnp.where(core == 0, other_logs, own_logs))
-        own_factor = jnp.where(core == 0, later, 1.0)
-        other_factor = jnp.where(core == 0, 1.0, later)
-        for h in range(half):
-            at = core * half + h
-            own_by = jnp.where(core == 0, own_factor[:, h : h + 1], own_factor[:, half + h : half + h + 1])
-            other_by = jnp.where(
-                core == 0, other_factor[:, h : h + 1], other_factor[:, half + h : half + h + 1]
-            )
-            totals[h] = (own_ref[at] * own_by + other_ref[at] * other_by).astype(jnp.bfloat16)
-        first = logs.astype(jnp.bfloat16).astype(jnp.float32)
-        second = (logs - first).astype(jnp.bfloat16).astype(jnp.float32)
-        third = logs - first - second
-        row = lax.broadcasted_iota(jnp.int32, (LOG_ROWS, width), 0)
-        split = jnp.where(row == 0, first, jnp.where(row == 1, second, jnp.where(row == 2, third, 0.0)))
-        for m in range(chips):
-            for h in range(few):
-                outs[m][span_of(h, width)] = totals[(chip ^ m) * few + h]
-            outs[m][few * width :] = split.astype(jnp.bfloat16)
-
-    return pl.pallas_call(
-        kernel,
-        out_shape=[shape((few * width + LOG_ROWS, width), jnp.bfloat16)] * chips,
-        in_specs=[SMEM, VMEM, VMEM],
-        out_specs=[VMEM] * chips,
-        scratch_shapes=[pltpu.VMEM((half, width, width), jnp.bfloat16)],
-        compiler_params=params(24),
-        cost_estimate=cost(3),
-        name="join_cores",
-    )(place, own, other)
+    )(place, queries, keys, values, decay, near_keys, near_values, across)
+
+
+def precisely(q, state):
+    coarse = state.astype(jnp.bfloat16)
+    fine = (state - coarse.astype(jnp.float32)).astype(jnp.bfloat16)
+    return nn(q, coarse) + nn(q, fine)
 
 
 def scan_chips(place, arrived, heads):
@@ -442,31 +463,28 @@
     )(place, *arrived)
 
 
-def finish(place, queries, decay, gain, inner, neighbour, entry_own, entry_other):
+def finish(place, queries, decay, across, gain, inner, entry_own, entry_other):
     rows, heads, width = queries.shape
     half = heads // PAIR
+    slot = across.shape[0] - 1
 
     def kernel(
-        place_ref, q_ref, decay_ref, gain_ref, inner_ref, near_ref, own_ref, other_ref, out_ref, mixed
+        place_ref, q_ref, decay_ref, gain_ref, inner_ref, own_ref, other_ref, across_ref, out_ref, mixed, near_decay, sem
     ):
         core = place_ref[0] % PAIR
-        cumul, _ = decay_sums(decay_ref)
-        grown = jnp.exp(cumul)
-        near_logs = near_ref[heads, 0:1, :]
-        far = jnp.where(core == 0, 1.0, jnp.exp(near_logs))
-        near = jnp.where(core == 0, 0.0, 1.0)
+        copy = pltpu.make_async_copy(across_ref.at[pl.ds(slot, 1)], near_decay, sem)
+        copy.start()
+        cumul, _ = decay_sums(decay_ref[...])
+        copy.wait()
+        near_sums, _ = decay_sums(near_decay[0, 0:heads, :])
+        grown = jnp.exp(cumul + jnp.where(core == 0, 0.0, near_sums[rows - 1 : rows, :]))
         power = jnp.zeros((rows, width), jnp.float32)
         for at, step in turns(heads):
             q = jnp.swapaxes(q_ref[:, at : at + step, :], 0, 1)
             for h in range(step):
                 i = at + h
-                mine, theirs = own_ref[i % half], other_ref[i % half]
-                chip_entry = jnp.where(core == i // half, mine, theirs).astype(jnp.float32)
-                entry = chip_entry * far[:, i : i + 1] + near_ref[i] * near
-                coarse = entry.astype(jnp.bfloat16)
-                fine = (entry - coarse.astype(jnp.float32)).astype(jnp.bfloat16)
-                brought = (nn(q[h], coarse) + nn(q[h], fine)) * grown[:, i : i + 1]
-                mix = inner_ref[i] + brought
+                entry = jnp.where(core == i // half, own_ref[i % half], other_ref[i % half])
+                mix = inner_ref[i] + nn(q[h], entry) * grown[:, i : i + 1]
                 mixed[i] = mix
                 power += mix * mix
         mean = jnp.sum(power, axis=1, keepdims=True) / (heads * width)
@@ -481,13 +499,17 @@
     return pl.pallas_call(
         kernel,
         out_shape=shape((rows, heads, width), jnp.bfloat16),
-        in_specs=[SMEM] + [VMEM] * 7,
+        in_specs=[SMEM] + [VMEM] * 6 + [ANY],
         out_specs=VMEM,
-        scratch_shapes=[pltpu.VMEM((heads, rows, width), jnp.float32)],
+        scratch_shapes=[
+            pltpu.VMEM((heads, rows, width), jnp.float32),
+            pltpu.VMEM((1, rows, width), jnp.bfloat16),
+            pltpu.SemaphoreType.DMA,
+        ],
         compiler_params=params(32),
         cost_estimate=cost(8),
         name="finish",
-    )(place, queries, decay, gain, inner, neighbour, entry_own, entry_other)
+    )(place, queries, decay, gain, inner, entry_own, entry_other, across)
 
 
 def per_device(
@@ -498,8 +520,6 @@
     rows, heads, width = soft_q.shape
     lin_heads = lin_q.shape[1]
     hosted = heads // chips
-    parts = min(PARTS, hosted)
-    sizes = [hosted // parts] * parts
     place = lax.axis_index("seq").astype(jnp.int32).reshape(1)
     masks = range(1, chips)
 
@@ -518,27 +538,26 @@
     def together(values):
         return list(lax.optimization_barrier(tuple(values)))
 
-    (packed,) = pack(place, (soft_q, soft_k, soft_v), chips, sizes)
+    lin_decay = lin_decay.T
+    near_k, near_v = swap_cores(lin_k), swap_cores(lin_v)
+    packed = pack(place, (soft_q, soft_k, soft_v), lin_decay, chips)
     own = exchange_all(packed)
     across = swap_cores(own[0])
-    decay = after(lin_decay, packed[0])
-    state = block_state(lin_k, lin_v, decay)
-    near = swap_cores(state)
-    inner = within(lin_q, lin_k, lin_v, after(decay, state))
-    totals = exchange_all(join_cores(place, state, after(near, inner, across), chips))
-    arrived = together([*own, *totals])
-    own, totals = arrived[:chips], arrived[chips:]
+    totals = exchange_all(totals_of(place, lin_k, lin_v, lin_decay, near_k, near_v, across, chips))
+    inner = within(place, lin_q, lin_k, lin_v, lin_decay, near_k, near_v, after(across, totals[0]))
+    arrived = together([*own, *totals, inner])
+    own, totals, inner = arrived[:chips], arrived[chips:-1], arrived[-1]
     other = [across] + [swap_cores(block) for block in own[1:]]
     starts = scan_chips(place, totals, lin_heads)
 
     entries = exchange_all(starts)
     mixed = attend(place, block_bits, agent_ids, own, other, hosted)
-    back = [exchange_all(mixed)]
+    back = exchange_all(mixed)
     entry = gather_entry(place, [after(block, mixed[0]) for block in entries])
     gain = lin_gain.reshape(lin_heads, width)
-    lin_out = finish(place, lin_q, lin_decay, gain, inner, near, entry, swap_cores(entry))
-    back[-1][0] = after(back[-1][0], lin_out)
-    soft_out = unpack(place, back, heads, rows, sizes)
+    lin_out = finish(place, lin_q, lin_decay, across, gain, inner, entry, swap_cores(entry))
+    back[0] = after(back[0], lin_out)
+    soft_out = unpack(place, back, heads, rows)
     return (lin_out, soft_out)
 
 

time: 83.6 us -> 78.5 us (0.939)
  waiting for transfers between devices: 28.4 us -> 35.5 us
  local copies, waits for them, and re-layouts: 5.88 us -> 0.04 us
  Pallas kernels: 27.9 us -> 22.7 us
    ppermute x12, waiting for transfers between devices: 28.3 us -> 35.5 us  [exchange(): return lax.ppermute(value, 'seq', [(i, i ^ PAIR * m) for i in range(count)])]
    unnamed x31 -> x16, local copies, waits for them, and re-layouts: 5.64 us -> 0.04 us
    pallas_call x1, Pallas kernels: 4.64 us -> 2.88 us  [finish(): pl.pallas_call(kernel, out_shape=shape((rows, heads, width), jnp.bfloat16...]
    pallas_call x3 -> x2, Pallas kernels: 9.06 us -> 7.75 us  [the longest x1 4.37 us: pack(): pl.pallas_call(kernel, out_shape=[shape((3 * hosted + (m == 0), rows, wid...]
    pallas_call x1, Pallas kernels: 6.3 us -> 5.04 us  [attend(): pl.pallas_call(kernel, out_shape=[shape((each * rows, width), jnp.bfloat1...]
    pallas_call x1, Pallas kernels: 0.92 us -> 0.04 us  [gather_entry(): pl.pallas_call(kernel, out_shape=shape((chips * few, width, width), jnp.b...]
    ppermute x6 -> x7, starting transfers between devices: 1.95 us -> 1.68 us  [swap_cores(): return lax.ppermute(value, 'seq', [(i, i ^ 1) for i in range(count)])]
  transfers between devices with their start and end apart: 18 -> 19, of which waited for: 7 -> 7; matrix products, arithmetic and copies ran while one was open for 0% -> 0% of each run, Pallas kernels for 22% -> 27%
where the time goes in v4:
time: 78.5 us; the launch traced here: 78.3 us
  waiting for transfers between devices  35.5 us (45%)
  Pallas kernels  22.7 us (29%)
  starting transfers between devices  19.3 us (25%)
    ppermute x12, waiting for transfers between devices, exchange(): return lax.ppermute(value, 'seq', [(i, i ^ PAIR * m) for i in range(count)])  35.5 us
    ppermute x12, starting transfers between devices, exchange(): return lax.ppermute(value, 'seq', [(i, i ^ PAIR * m) for i in range(count)])  17.7 us
    pallas_call x1, Pallas kernels, attend(): pl.pallas_call(kernel, out_shape=[shape((each * rows, width), jnp.bfloat1...  5.04 us
    pallas_call x1, Pallas kernels, within(): pl.pallas_call(kernel, out_shape=shape((heads, rows, width), jnp.float32)...  5.03 us
    pallas_call x1, Pallas kernels, pack(): pl.pallas_call(kernel, out_shape=[shape((3 * hosted + (m == 0), rows, wid...  4.37 us
    pallas_call x1, Pallas kernels, totals_of(): pl.pallas_call(kernel, out_shape=[shape((few * width + LOG_ROWS, width),...  3.38 us
    pallas_call x1, Pallas kernels, finish(): pl.pallas_call(kernel, out_shape=shape((rows, heads, width), jnp.bfloat16...  2.88 us
    ppermute x7, starting transfers between devices, swap_cores(): return lax.ppermute(value, 'seq', [(i, i ^ 1) for i in range(count)])  1.68 us
  transfers between devices with their start and end apart: 19, of which 7 were waited for; matrix products, arithmetic and copies ran while one was open for 0% of the time, Pallas kernels for 27%

profile of v4, /device:TPU:0, one launch (start us, length us, event | category | flops | bytes accessed | tf_op | source)
XLA Modules:
  0.0 78.3 jit_solution(882672872432175491)
XLA Ops:
  0.6 0.5 collective-permute-start.3
  1.1 0.1 collective-permute-start.4
  1.2 4.4 %pack.1 = (bf16[25,128,128]{2,1,0:T(8,128)(2,1)}, bf16[24,128,128]{2,1,0:T(8,128)(2,1)}, bf16[24,128,128]{2,1,0:T(8,128)(2,1)}, bf16[24,128,128]{2,1,0:T(8,128)(2,1)}) custom-call(s32[1]{0:T(128)} %bitcast.place_ref, bf16[32,128]{1,0:T(8,128)(2,1)} %bitcast.4, bf16[128,32,128]{2,1,0:T(8,128)(2,1)} %q_ref.3, bf16[128,32,128]{2,1,0:T(8,128)(2,1)} %k_ref.3, ...), custom_call_target="tpu_custom_call" | custom-call | flops 2147483648 | bytes 1 | tf_op jit(solution)/shard_map/pack/pallas_call | solution.py:105
  5.6 0.5 collective-permute-start.5
  6.1 2.6 %collective-permute-start = (bf16[24,128,128]{2,1,0:T(8,128)(2,1)}, bf16[24,128,128]{2,1,0:T(8,128)(2,1)S(1)}, u32[]{:S(2)}, u32[]{:S(2)}) collective-permute-start(bf16[24,128,128]{2,1,0:T(8,128)(2,1)} %get-tuple-element.34), channel_id=1, source_target_pairs={{0,2},{1,3},{2,0},{3,1},{4,6},{5,7},{6,4},{7,5},{8,10},{9,11},{10,... | collective-permute-start | bytes 2359304 | tf_op jit(solution)/shard_map/ppermute | solution.py:527
  8.7 1.5 %collective-permute-start.1 = (bf16[24,128,128]{2,1,0:T(8,128)(2,1)}, bf16[24,128,128]{2,1,0:T(8,128)(2,1)S(1)}, u32[]{:S(2)}, u32[]{:S(2)}) collective-permute-start(bf16[24,128,128]{2,1,0:T(8,128)(2,1)} %get-tuple-element.35), channel_id=1, source_target_pairs={{0,4},{1,5},{2,6},{3,7},{4,0},{5,1},{6,2},{7,3},{8,12},{9,13},{10,... | collective-permute-start | bytes 2359304 | tf_op jit(solution)/shard_map/ppermute | solution.py:527
  10.2 1.9 %collective-permute-start.2 = (bf16[24,128,128]{2,1,0:T(8,128)(2,1)}, bf16[24,128,128]{2,1,0:T(8,128)(2,1)S(1)}, u32[]{:S(2)}, u32[]{:S(2)}) collective-permute-start(bf16[24,128,128]{2,1,0:T(8,128)(2,1)} %get-tuple-element.36), channel_id=1, source_target_pairs={{0,6},{1,7},{2,4},{3,5},{4,2},{5,3},{6,0},{7,1},{8,14},{9,15},{10,... | collective-permute-start | bytes 2359304 | tf_op jit(solution)/shard_map/ppermute | solution.py:527
  12.1 3.4 %totals_of.1 = (bf16[528,128]{1,0:T(8,128)(2,1)S(1)}, bf16[528,128]{1,0:T(8,128)(2,1)S(1)}, bf16[528,128]{1,0:T(8,128)(2,1)S(1)}, bf16[528,128]{1,0:T(8,128)(2,1)S(1)}) custom-call(s32[1]{0:T(128)} %bitcast.place_ref, bf16[128,32,128]{2,1,0:T(8,128)(2,1)S(1)} %copy-done, bf16[128,32,128]{2,1,0:T(8,128)(2,1)S(1)} %copy-done.1, bf16[32,128]{1,0:T(8,128)(2,1)S(1)} %bitcast.5, ...), custom_call_target="tpu_custom_call" | custom-call | flops 3221225472 | bytes 1 | tf_op jit(solution)/shard_map/totals_of/pallas_call | solution.py:325
  15.5 0.6 collective-permute-start.6
  16.1 1.1 %collective-permute-start.7 = (bf16[528,128]{1,0:T(8,128)(2,1)S(1)}, bf16[528,128]{1,0:T(8,128)(2,1)S(1)}, u32[]{:S(2)}, u32[]{:S(2)}) collective-permute-start(bf16[528,128]{1,0:T(8,128)(2,1)S(1)} %get-tuple-element.39), channel_id=1, source_target_pairs={{0,4},{1,5},{2,6},{3,7},{4,0},{5,1},{6,2},{7,3},{8,12},{9,13},{10,... | collective-permute-start | bytes 405512 | tf_op jit(solution)/shard_map/ppermute | solution.py:527
  17.2 10.1 %collective-permute-done.rest_1_ = bf16[24,128,128]{2,1,0:T(8,128)(2,1)S(1)} collective-permute-done((bf16[24,128,128]{2,1,0:T(8,128)(2,1)}, bf16[24,128,128]{2,1,0:T(8,128)(2,1)S(1)}, u32[]{:S(2)}, u32[]{:S(2)}) %collective-permute-start) | collective-permute-done | bytes 786464 | tf_op jit(solution)/shard_map/ppermute | solution.py:527
  27.3 2.9 %collective-permute-start.8 = (bf16[528,128]{1,0:T(8,128)(2,1)S(1)}, bf16[528,128]{1,0:T(8,128)(2,1)S(1)}, u32[]{:S(2)}, u32[]{:S(2)}) collective-permute-start(bf16[528,128]{1,0:T(8,128)(2,1)S(1)} %get-tuple-element.40), channel_id=1, source_target_pairs={{0,6},{1,7},{2,4},{3,5},{4,2},{5,3},{6,0},{7,1},{8,14},{9,15},{10,... | collective-permute-start | bytes 405512 | tf_op jit(solution)/shard_map/ppermute | solution.py:527
  30.2 5.0 %within.1.inner_ref = f32[32,128,128]{2,1,0:T(8,128)S(1)} custom-call(s32[1]{0:T(128)} %bitcast.place_ref, bf16[128,32,128]{2,1,0:T(8,128)(2,1)S(1)} %copy-done.2, bf16[128,32,128]{2,1,0:T(8,128)(2,1)S(1)} %copy-done, bf16[128,32,128]{2,1,0:T(8,128)(2,1)S(1)} %copy-done.1, bf16[32,128]{1,0:T(8,128)(2,1)S(1)} %bitcast.6, ...), custom_call_target="tpu_custom_call" | custom-call | flops 7516192768 | bytes 1 | tf_op jit(solution)/shard_map/within/pallas_call | solution.py:378
  35.2 0.0 copy-start.3
  35.3 10.9 %collective-permute-done.1.rest_2_ = bf16[24,128,128]{2,1,0:T(8,128)(2,1)S(1)} collective-permute-done((bf16[24,128,128]{2,1,0:T(8,128)(2,1)}, bf16[24,128,128]{2,1,0:T(8,128)(2,1)S(1)}, u32[]{:S(2)}, u32[]{:S(2)}) %collective-permute-start.1) | collective-permute-done | bytes 786464 | tf_op jit(solution)/shard_map/ppermute | solution.py:527
  46.1 0.9 %collective-permute-done.6.rest_1_ = bf16[528,128]{1,0:T(8,128)(2,1)S(1)} collective-permute-done((bf16[528,128]{1,0:T(8,128)(2,1)S(1)}, bf16[528,128]{1,0:T(8,128)(2,1)S(1)}, u32[]{:S(2)}, u32[]{:S(2)}) %collective-permute-start.6) | collective-permute-done | bytes 135200 | tf_op jit(solution)/shard_map/ppermute | solution.py:527
  47.1 4.1 %collective-permute-done.7.rest_2_ = bf16[528,128]{1,0:T(8,128)(2,1)S(1)} collective-permute-done((bf16[528,128]{1,0:T(8,128)(2,1)S(1)}, bf16[528,128]{1,0:T(8,128)(2,1)S(1)}, u32[]{:S(2)}, u32[]{:S(2)}) %collective-permute-start.7) | collective-permute-done | bytes 135200 | tf_op jit(solution)/shard_map/ppermute | solution.py:527
  51.1 0.5 collective-permute-start.10
  51.7 0.6 scan_chips.1
  52.2 1.3 %collective-permute-start.12 = (bf16[512,128]{1,0:T(8,128)(2,1)S(1)}, bf16[512,128]{1,0:T(8,128)(2,1)S(1)}, u32[]{:S(2)}, u32[]{:S(2)}) collective-permute-start(bf16[512,128]{1,0:T(8,128)(2,1)S(1)} %get-tuple-element.54), channel_id=1, source_target_pairs={{0,2},{1,3},{2,0},{3,1},{4,6},{5,7},{6,4},{7,5},{8,10},{9,11},{10,... | collective-permute-start | bytes 393224 | tf_op jit(solution)/shard_map/ppermute | solution.py:527
  53.6 0.8 collective-permute-start.13
  54.4 1.4 %collective-permute-start.14 = (bf16[512,128]{1,0:T(8,128)(2,1)S(1)}, bf16[512,128]{1,0:T(8,128)(2,1)S(1)}, u32[]{:S(2)}, u32[]{:S(2)}) collective-permute-start(bf16[512,128]{1,0:T(8,128)(2,1)S(1)} %get-tuple-element.58), channel_id=1, source_target_pairs={{0,6},{1,7},{2,4},{3,5},{4,2},{5,3},{6,0},{7,1},{8,14},{9,15},{10,... | collective-permute-start | bytes 393224 | tf_op jit(solution)/shard_map/ppermute | solution.py:527
  55.8 5.0 %attend.1 = (bf16[1024,128]{1,0:T(8,128)(2,1)S(1)}, bf16[1024,128]{1,0:T(8,128)(2,1)S(1)}, bf16[1024,128]{1,0:T(8,128)(2,1)S(1)}, bf16[1024,128]{1,0:T(8,128)(2,1)S(1)}) custom-call(s32[1]{0:T(128)} %bitcast.place_ref, s32[8,8]{1,0:T(8,128)S(1)} %copy-done.6, s32[8]{0:T(128)S(1)} %copy-done.7, bf16[25,128,128]{2,1,0:T(8,128)(2,1)S(1)} %copy-done.3, ...), custom_call_target="tpu_custom_call" | custom-call | flops 7516192768 | bytes 1 | tf_op jit(solution)/shard_map/attend/pallas_call | solution.py:225
  60.9 1.1 %collective-permute-done.14.rest_3_ = bf16[512,128]{1,0:T(8,128)(2,1)S(1)} collective-permute-done((bf16[512,128]{1,0:T(8,128)(2,1)S(1)}, bf16[512,128]{1,0:T(8,128)(2,1)S(1)}, u32[]{:S(2)}, u32[]{:S(2)}) %collective-permute-start.14) | collective-permute-done | bytes 131104 | tf_op jit(solution)/shard_map/ppermute | solution.py:527
  62.1 0.1 collective-permute-start.15
  62.1 1.0 %collective-permute-start.16 = (bf16[1024,128]{1,0:T(8,128)(2,1)S(1)}, bf16[1024,128]{1,0:T(8,128)(2,1)S(1)}, u32[]{:S(2)}, u32[]{:S(2)}) collective-permute-start(bf16[1024,128]{1,0:T(8,128)(2,1)S(1)} %get-tuple-element.61), channel_id=1, source_target_pairs={{0,2},{1,3},{2,0},{3,1},{4,6},{5,7},{6,4},{7,5},{8,10},{9,11},{10,... | collective-permute-start | bytes 786440 | tf_op jit(solution)/shard_map/ppermute | solution.py:527
  63.2 1.3 %collective-permute-start.17 = (bf16[1024,128]{1,0:T(8,128)(2,1)S(1)}, bf16[1024,128]{1,0:T(8,128)(2,1)S(1)}, u32[]{:S(2)}, u32[]{:S(2)}) collective-permute-start(bf16[1024,128]{1,0:T(8,128)(2,1)S(1)} %get-tuple-element.62), channel_id=1, source_target_pairs={{0,4},{1,5},{2,6},{3,7},{4,0},{5,1},{6,2},{7,3},{8,12},{9,13},{10,... | collective-permute-start | bytes 786440 | tf_op jit(solution)/shard_map/ppermute | solution.py:527
  64.5 1.2 %collective-permute-start.18 = (bf16[1024,128]{1,0:T(8,128)(2,1)S(1)}, bf16[1024,128]{1,0:T(8,128)(2,1)S(1)}, u32[]{:S(2)}, u32[]{:S(2)}) collective-permute-start(bf16[1024,128]{1,0:T(8,128)(2,1)S(1)} %get-tuple-element.63), channel_id=1, source_target_pairs={{0,6},{1,7},{2,4},{3,5},{4,2},{5,3},{6,0},{7,1},{8,14},{9,15},{10,... | collective-permute-start | bytes 786440 | tf_op jit(solution)/shard_map/ppermute | solution.py:527
  65.7 2.9 %finish.1 = bf16[128,32,128]{2,1,0:T(8,128)(2,1)} custom-call(s32[1]{0:T(128)} %bitcast.place_ref, bf16[128,32,128]{2,1,0:T(8,128)(2,1)S(1)} %copy-done.2, bf16[32,128]{1,0:T(8,128)(2,1)S(1)} %bitcast.7, f32[32,128]{1,0:T(8,128)S(1)} %bitcast.3, f32[32,128,128]{2,1,0:T(8,128)S(1)} %within.1.inner_ref, bf16[16,128,128]{2,1,0:T(8,128)(2,1)S(1)} %gather_entry.1.own_ref, ...), custom_call_target="tpu_custom_call" | custom-call | flops 4294967296 | bytes 1 | tf_op jit(solution)/shard_map/finish/pallas_call | solution.py:499
  68.6 2.7 %collective-permute-done.16.rest_1_ = bf16[1024,128]{1,0:T(8,128)(2,1)S(1)} collective-permute-done((bf16[1024,128]{1,0:T(8,128)(2,1)S(1)}, bf16[1024,128]{1,0:T(8,128)(2,1)S(1)}, u32[]{:S(2)}, u32[]{:S(2)}) %collective-permute-start.16) | collective-permute-done | bytes 262176 | tf_op jit(solution)/shard_map/ppermute | solution.py:527
  71.3 5.6 %collective-permute-done.17.rest_2_ = bf16[1024,128]{1,0:T(8,128)(2,1)S(1)} collective-permute-done((bf16[1024,128]{1,0:T(8,128)(2,1)S(1)}, bf16[1024,128]{1,0:T(8,128)(2,1)S(1)}, u32[]{:S(2)}, u32[]{:S(2)}) %collective-permute-start.17) | collective-permute-done | bytes 262176 | tf_op jit(solution)/shard_map/ppermute | solution.py:527
  76.9 1.4 %unpack.1 = bf16[128,32,128]{2,1,0:T(8,128)(2,1)} custom-call(s32[1]{0:T(128)} %bitcast.place_ref, bf16[1024,128]{1,0:T(8,128)(2,1)S(1)} %get-tuple-element.60.rest_0_, bf16[1024,128]{1,0:T(8,128)(2,1)S(1)} %collective-permute-done.16.rest_1_, bf16[1024,128]{1,0:T(8,128)(2,1)S(1)} %collective-permute-done.17.rest_2_, ...), custom_call_target="tpu_custom_call" | custom-call | flops 2147483648 | bytes 1 | tf_op jit(solution)/shard_map/unpack/pallas_call | solution.py:260
  (30 shorter events, 0.1 us)
Async XLA Ops:
  0.6 11.5 %collective-permute-start.3 = (bf16[128,32,128]{2,1,0:T(8,128)(2,1)}, bf16[128,32,128]{2,1,0:T(8,128)(2,1)S(1)}, u32[]{:S(2)}, u32[]{:S(2)}) collective-permute-start(bf16[128,32,128]{2,1,0:T(8,128)(2,1)} %k_ref.5), channel_id=1, source_target_pairs={{0,1},{1,0},{2,3},{3,2},{4,5},{5,4},{6,7},{7,6},{8,9},{9,8},{10,11... | collective-permute-start | bytes 3145736 | tf_op jit(solution)/shard_map/ppermute | solution.py:533
  1.1 11.0 %collective-permute-start.4 = (bf16[128,32,128]{2,1,0:T(8,128)(2,1)}, bf16[128,32,128]{2,1,0:T(8,128)(2,1)S(1)}, u32[]{:S(2)}, u32[]{:S(2)}) collective-permute-start(bf16[128,32,128]{2,1,0:T(8,128)(2,1)} %v_ref.5), channel_id=1, source_target_pairs={{0,1},{1,0},{2,3},{3,2},{4,5},{5,4},{6,7},{7,6},{8,9},{9,8},{10,11... | collective-permute-start | bytes 3145736 | tf_op jit(solution)/shard_map/ppermute | solution.py:533
  1.2 10.9 %copy-start = (bf16[128,32,128]{2,1,0:T(8,128)(2,1)S(1)}, bf16[128,32,128]{2,1,0:T(8,128)(2,1)}, u32[]{:S(2)}) copy-start(bf16[128,32,128]{2,1,0:T(8,128)(2,1)} %k_ref.5) | copy-start | bytes 3145732
  1.2 10.9 %copy-start.1 = (bf16[128,32,128]{2,1,0:T(8,128)(2,1)S(1)}, bf16[128,32,128]{2,1,0:T(8,128)(2,1)}, u32[]{:S(2)}) copy-start(bf16[128,32,128]{2,1,0:T(8,128)(2,1)} %v_ref.5) | copy-start | bytes 3145732
  1.2 10.9 %copy-start.5 = (bf16[128,32]{0,1:T(8,128)(2,1)S(1)}, bf16[128,32]{0,1:T(8,128)(2,1)}, u32[]{:S(2)}) copy-start(bf16[128,32]{0,1:T(8,128)(2,1)} %param.13) | copy-start | bytes 24580
  5.6 4.6 %collective-permute-start.5 = (bf16[25,128,128]{2,1,0:T(8,128)(2,1)}, bf16[25,128,128]{2,1,0:T(8,128)(2,1)S(1)}, u32[]{:S(2)}, u32[]{:S(2)}) collective-permute-start(bf16[25,128,128]{2,1,0:T(8,128)(2,1)} %get-tuple-element.48.rest_0_), channel_id=1, source_target_pairs={{0,1},{1,0},{2,3},{3,2},{4,5},{5,4},{6,7},{7,6},{8,9},{9,8},{10,11... | collective-permute-start | bytes 2457608 | tf_op jit(solution)/shard_map/ppermute | solution.py:533
  6.1 21.2 %collective-permute-start = (bf16[24,128,128]{2,1,0:T(8,128)(2,1)}, bf16[24,128,128]{2,1,0:T(8,128)(2,1)S(1)}, u32[]{:S(2)}, u32[]{:S(2)}) collective-permute-start(bf16[24,128,128]{2,1,0:T(8,128)(2,1)} %get-tuple-element.34), channel_id=1, source_target_pairs={{0,2},{1,3},{2,0},{3,1},{4,6},{5,7},{6,4},{7,5},{8,10},{9,11},{10,... | collective-permute-start | bytes 2359304 | tf_op jit(solution)/shard_map/ppermute | solution.py:527
  8.7 37.5 %collective-permute-start.1 = (bf16[24,128,128]{2,1,0:T(8,128)(2,1)}, bf16[24,128,128]{2,1,0:T(8,128)(2,1)S(1)}, u32[]{:S(2)}, u32[]{:S(2)}) collective-permute-start(bf16[24,128,128]{2,1,0:T(8,128)(2,1)} %get-tuple-element.35), channel_id=1, source_target_pairs={{0,4},{1,5},{2,6},{3,7},{4,0},{5,1},{6,2},{7,3},{8,12},{9,13},{10,... | collective-permute-start | bytes 2359304 | tf_op jit(solution)/shard_map/ppermute | solution.py:527
  10.2 20.0 %copy-start.2 = (bf16[128,32,128]{2,1,0:T(8,128)(2,1)S(1)}, bf16[128,32,128]{2,1,0:T(8,128)(2,1)}, u32[]{:S(2)}) copy-start(bf16[128,32,128]{2,1,0:T(8,128)(2,1)} %q_ref.5) | copy-start | bytes 3145732
  10.2 35.9 %collective-permute-start.2 = (bf16[24,128,128]{2,1,0:T(8,128)(2,1)}, bf16[24,128,128]{2,1,0:T(8,128)(2,1)S(1)}, u32[]{:S(2)}, u32[]{:S(2)}) collective-permute-start(bf16[24,128,128]{2,1,0:T(8,128)(2,1)} %get-tuple-element.36), channel_id=1, source_target_pairs={{0,6},{1,7},{2,4},{3,5},{4,2},{5,3},{6,0},{7,1},{8,14},{9,15},{10,... | collective-permute-start | bytes 2359304 | tf_op jit(solution)/shard_map/ppermute | solution.py:527
  15.5 31.6 %collective-permute-start.6 = (bf16[528,128]{1,0:T(8,128)(2,1)S(1)}, bf16[528,128]{1,0:T(8,128)(2,1)S(1)}, u32[]{:S(2)}, u32[]{:S(2)}) collective-permute-start(bf16[528,128]{1,0:T(8,128)(2,1)S(1)} %get-tuple-element.38), channel_id=1, source_target_pairs={{0,2},{1,3},{2,0},{3,1},{4,6},{5,7},{6,4},{7,5},{8,10},{9,11},{10,... | collective-permute-start | bytes 405512 | tf_op jit(solution)/shard_map/ppermute | solution.py:527
  16.1 35.0 %collective-permute-start.7 = (bf16[528,128]{1,0:T(8,128)(2,1)S(1)}, bf16[528,128]{1,0:T(8,128)(2,1)S(1)}, u32[]{:S(2)}, u32[]{:S(2)}) collective-permute-start(bf16[528,128]{1,0:T(8,128)(2,1)S(1)} %get-tuple-element.39), channel_id=1, source_target_pairs={{0,4},{1,5},{2,6},{3,7},{4,0},{5,1},{6,2},{7,3},{8,12},{9,13},{10,... | collective-permute-start | bytes 405512 | tf_op jit(solution)/shard_map/ppermute | solution.py:527
  27.3 23.9 %collective-permute-start.8 = (bf16[528,128]{1,0:T(8,128)(2,1)S(1)}, bf16[528,128]{1,0:T(8,128)(2,1)S(1)}, u32[]{:S(2)}, u32[]{:S(2)}) collective-permute-start(bf16[528,128]{1,0:T(8,128)(2,1)S(1)} %get-tuple-element.40), channel_id=1, source_target_pairs={{0,6},{1,7},{2,4},{3,5},{4,2},{5,3},{6,0},{7,1},{8,14},{9,15},{10,... | collective-permute-start | bytes 405512 | tf_op jit(solution)/shard_map/ppermute | solution.py:527
  35.2 20.6 %copy-start.3 = (bf16[25,128,128]{2,1,0:T(8,128)(2,1)S(1)}, bf16[25,128,128]{2,1,0:T(8,128)(2,1)}, u32[]{:S(2)}) copy-start(bf16[25,128,128]{2,1,0:T(8,128)(2,1)} %get-tuple-element.48.rest_0_) | copy-start | bytes 2457604
  35.2 20.6 %copy-start.6 = (s32[8,8]{1,0:T(8,128)S(1)}, s32[8,8]{1,0:T(8,128)}, u32[]{:S(2)}) copy-start(s32[8,8]{1,0:T(8,128)} %bits_ref.1) | copy-start | bytes 772
  35.2 20.6 %copy-start.7 = (s32[8]{0:T(128)S(1)}, s32[8]{0:T(128)}, u32[]{:S(2)}) copy-start(s32[8]{0:T(128)} %agents_ref.1) | copy-start | bytes 100
  51.1 3.2 %collective-permute-start.9 = (bf16[24,128,128]{2,1,0:T(8,128)(2,1)S(1)}, bf16[24,128,128]{2,1,0:T(8,128)(2,1)S(1)}, u32[]{:S(2)}, u32[]{:S(2)}) collective-permute-start(bf16[24,128,128]{2,1,0:T(8,128)(2,1)S(1)} %collective-permute-done.rest_1_), channel_id=1, source_target_pairs={{0,1},{1,0},{2,3},{3,2},{4,5},{5,4},{6,7},{7,6},{8,9},{9,8},{10,11... | collective-permute-start | bytes 2359304 | tf_op jit(solution)/shard_map/ppermute | solution.py:533
  51.1 4.6 %collective-permute-start.10 = (bf16[24,128,128]{2,1,0:T(8,128)(2,1)S(1)}, bf16[24,128,128]{2,1,0:T(8,128)(2,1)S(1)}, u32[]{:S(2)}, u32[]{:S(2)}) collective-permute-start(bf16[24,128,128]{2,1,0:T(8,128)(2,1)S(1)} %collective-permute-done.1.rest_2_), channel_id=1, source_target_pairs={{0,1},{1,0},{2,3},{3,2},{4,5},{5,4},{6,7},{7,6},{8,9},{9,8},{10,11... | collective-permute-start | bytes 2359304 | tf_op jit(solution)/shard_map/ppermute | solution.py:533
  51.7 4.1 %collective-permute-start.11 = (bf16[24,128,128]{2,1,0:T(8,128)(2,1)S(1)}, bf16[24,128,128]{2,1,0:T(8,128)(2,1)S(1)}, u32[]{:S(2)}, u32[]{:S(2)}) collective-permute-start(bf16[24,128,128]{2,1,0:T(8,128)(2,1)S(1)} %collective-permute-done.2.rest_3_), channel_id=1, source_target_pairs={{0,1},{1,0},{2,3},{3,2},{4,5},{5,4},{6,7},{7,6},{8,9},{9,8},{10,11... | collective-permute-start | bytes 2359304 | tf_op jit(solution)/shard_map/ppermute | solution.py:533
  52.2 9.8 %collective-permute-start.12 = (bf16[512,128]{1,0:T(8,128)(2,1)S(1)}, bf16[512,128]{1,0:T(8,128)(2,1)S(1)}, u32[]{:S(2)}, u32[]{:S(2)}) collective-permute-start(bf16[512,128]{1,0:T(8,128)(2,1)S(1)} %get-tuple-element.54), channel_id=1, source_target_pairs={{0,2},{1,3},{2,0},{3,1},{4,6},{5,7},{6,4},{7,5},{8,10},{9,11},{10,... | collective-permute-start | bytes 393224 | tf_op jit(solution)/shard_map/ppermute | solution.py:527
  53.6 8.4 %collective-permute-start.13 = (bf16[512,128]{1,0:T(8,128)(2,1)S(1)}, bf16[512,128]{1,0:T(8,128)(2,1)S(1)}, u32[]{:S(2)}, u32[]{:S(2)}) collective-permute-start(bf16[512,128]{1,0:T(8,128)(2,1)S(1)} %get-tuple-element.56), channel_id=1, source_target_pairs={{0,4},{1,5},{2,6},{3,7},{4,0},{5,1},{6,2},{7,3},{8,12},{9,13},{10,... | collective-permute-start | bytes 393224 | tf_op jit(solution)/shard_map/ppermute | solution.py:527
  54.3 11.4 %copy-start.4 = (f32[4096]{0:T(1024)S(1)}, f32[4096]{0:T(1024)}, u32[]{:S(2)}) copy-start(f32[4096]{0:T(1024)} %param.14) | copy-start | bytes 49156
  54.4 7.7 %collective-permute-start.14 = (bf16[512,128]{1,0:T(8,128)(2,1)S(1)}, bf16[512,128]{1,0:T(8,128)(2,1)S(1)}, u32[]{:S(2)}, u32[]{:S(2)}) collective-permute-start(bf16[512,128]{1,0:T(8,128)(2,1)S(1)} %get-tuple-element.58), channel_id=1, source_target_pairs={{0,6},{1,7},{2,4},{3,5},{4,2},{5,3},{6,0},{7,1},{8,14},{9,15},{10,... | collective-permute-start | bytes 393224 | tf_op jit(solution)/shard_map/ppermute | solution.py:527
  62.1 3.6 %collective-permute-start.15 = (bf16[16,128,128]{2,1,0:T(8,128)(2,1)S(1)}, bf16[16,128,128]{2,1,0:T(8,128)(2,1)S(1)}, u32[]{:S(2)}, u32[]{:S(2)}) collective-permute-start(bf16[16,128,128]{2,1,0:T(8,128)(2,1)S(1)} %gather_entry.1.own_ref), channel_id=1, source_target_pairs={{0,1},{1,0},{2,3},{3,2},{4,5},{5,4},{6,7},{7,6},{8,9},{9,8},{10,11... | collective-permute-start | bytes 1572872 | tf_op jit(solution)/shard_map/ppermute | solution.py:533
  62.1 9.2 %collective-permute-start.16 = (bf16[1024,128]{1,0:T(8,128)(2,1)S(1)}, bf16[1024,128]{1,0:T(8,128)(2,1)S(1)}, u32[]{:S(2)}, u32[]{:S(2)}) collective-permute-start(bf16[1024,128]{1,0:T(8,128)(2,1)S(1)} %get-tuple-element.61), channel_id=1, source_target_pairs={{0,2},{1,3},{2,0},{3,1},{4,6},{5,7},{6,4},{7,5},{8,10},{9,11},{10,... | collective-permute-start | bytes 786440 | tf_op jit(solution)/shard_map/ppermute | solution.py:527
  63.2 13.8 %collective-permute-start.17 = (bf16[1024,128]{1,0:T(8,128)(2,1)S(1)}, bf16[1024,128]{1,0:T(8,128)(2,1)S(1)}, u32[]{:S(2)}, u32[]{:S(2)}) collective-permute-start(bf16[1024,128]{1,0:T(8,128)(2,1)S(1)} %get-tuple-element.62), channel_id=1, source_target_pairs={{0,4},{1,5},{2,6},{3,7},{4,0},{5,1},{6,2},{7,3},{8,12},{9,13},{10,... | collective-permute-start | bytes 786440 | tf_op jit(solution)/shard_map/ppermute | solution.py:527
  64.5 12.5 %collective-permute-start.18 = (bf16[1024,128]{1,0:T(8,128)(2,1)S(1)}, bf16[1024,128]{1,0:T(8,128)(2,1)S(1)}, u32[]{:S(2)}, u32[]{:S(2)}) collective-permute-start(bf16[1024,128]{1,0:T(8,128)(2,1)S(1)} %get-tuple-element.63), channel_id=1, source_target_pairs={{0,6},{1,7},{2,4},{3,5},{4,2},{5,3},{6,0},{7,1},{8,14},{9,15},{10,... | collective-permute-start | bytes 786440 | tf_op jit(solution)/shard_map/ppermute | solution.py:527

commit v5 on v4

--- a/solution.py
+++ b/solution.py
@@ -64,55 +64,63 @@
     cut = rows // pieces
 
     def kernel(place_ref, decay_ref, q_ref, k_ref, v_ref, *rest):
-        outs, (landed, turned, padded, in_sems, out_sems) = rest[:-5], rest[-5:]
+        outs, (landed, turned, in_sems, out_sems, decay_sem) = rest[:-5], rest[-5:]
         chip = place_ref[0] // PAIR
-        arriving = [
-            pltpu.make_async_copy(
-                ref.at[pl.ds(piece * cut, cut)],
-                landed.at[which, pl.ds(piece * cut, cut)],
-                in_sems.at[which, piece],
-            )
-            for which, ref in enumerate((q_ref, k_ref, v_ref))
-            for piece in range(pieces)
-        ]
-        for copy in arriving:
-            copy.start()
-        padded[...] = jnp.zeros_like(padded)
-        padded[0, 0:lin_heads, :] = decay_ref[...]
+        order = [(1, k_ref), (0, q_ref), (2, v_ref)]
+        arriving = {}
+        for which, ref in order:
+            for piece in range(pieces):
+                span = pl.ds(piece * cut, cut)
+                arriving[which, piece] = pltpu.make_async_copy(
+                    ref.at[span], landed.at[which, span], in_sems.at[which, piece]
+                )
+                arriving[which, piece].start()
         leaving = [
-            pltpu.make_async_copy(padded, outs[0].at[pl.ds(3 * hosted, 1)], out_sems.at[3 * chips])
+            pltpu.make_async_copy(decay_ref, outs[0].at[3 * hosted, pl.ds(0, lin_heads)], decay_sem)
         ]
         leaving[-1].start()
-        for which in range(3):
-            for piece in range(pieces):
-                arriving[which * pieces + piece].wait()
-            for at, step in turns(heads):
-                block = jnp.swapaxes(landed[which, :, at : at + step, :], 0, 1)
-                for h in range(step):
-                    turned[which, at + h] = block[h].T if which == 1 else block[h]
+
+        def send(which, piece, span):
             for m in range(chips):
                 leaving.append(
                     pltpu.make_async_copy(
-                        turned.at[which, pl.ds((chip ^ m) * hosted, hosted)],
-                        outs[m].at[pl.ds(which * hosted, hosted)],
-                        out_sems.at[which * chips + m],
+                        turned.at[which, pl.ds((chip ^ m) * hosted, hosted), span],
+                        outs[m].at[pl.ds(which * hosted, hosted), span],
+                        out_sems.at[which, piece, m],
                     )
                 )
                 leaving[-1].start()
+
+        for which, _ in order:
+            for piece in range(pieces):
+                arriving[which, piece].wait()
+                if which == 1:
+                    continue
+                at_rows = slice(piece * cut, (piece + 1) * cut)
+                for at, step in turns(heads):
+                    block = jnp.swapaxes(landed[which, at_rows, at : at + step, :], 0, 1)
+                    turned[which, at : at + step, at_rows, :] = block
+                send(which, piece, pl.ds(piece * cut, cut))
+            if which == 1:
+                for at, step in turns(heads):
+                    block = jnp.swapaxes(landed[which, :, at : at + step, :], 0, 1)
+                    for h in range(step):
+                        turned[which, at + h] = block[h].T
+                send(which, 0, pl.ds(0, rows))
         for copy in leaving:
             copy.wait()
 
     return pl.pallas_call(
         kernel,
         out_shape=[shape((3 * hosted + (m == 0), rows, width), jnp.bfloat16) for m in range(chips)],
-        in_specs=[SMEM, VMEM, ANY, ANY, ANY],
+        in_specs=[SMEM, ANY, ANY, ANY, ANY],
         out_specs=[ANY] * chips,
         scratch_shapes=[
             pltpu.VMEM((3, rows, heads, width), jnp.bfloat16),
             pltpu.VMEM((3, heads, rows, width), jnp.bfloat16),
-            pltpu.VMEM((1, rows, width), jnp.bfloat16),
             pltpu.SemaphoreType.DMA((3, pieces)),
-            pltpu.SemaphoreType.DMA((3 * chips + 1,)),
+            pltpu.SemaphoreType.DMA((3, pieces, chips)),
+            pltpu.SemaphoreType.DMA,
         ],
         compiler_params=params(56),
         cost_estimate=cost(4),
@@ -541,9 +549,10 @@
     lin_decay = lin_decay.T
     near_k, near_v = swap_cores(lin_k), swap_cores(lin_v)
     packed = pack(place, (soft_q, soft_k, soft_v), lin_decay, chips)
-    own = exchange_all(packed)
-    across = swap_cores(own[0])
-    totals = exchange_all(totals_of(place, lin_k, lin_v, lin_decay, near_k, near_v, across, chips))
+    across = swap_cores(packed[0])
+    totals = totals_of(place, lin_k, lin_v, lin_decay, near_k, near_v, across, chips)
+    own = exchange_all([*packed[:-1], after(packed[-1], totals[0])])
+    totals = exchange_all(totals)
     inner = within(place, lin_q, lin_k, lin_v, lin_decay, near_k, near_v, after(across, totals[0]))
     arrived = together([*own, *totals, inner])
     own, totals, inner = arrived[:chips], arrived[chips:-1], arrived[-1]

time: 78.5 us -> 77.9 us (level)
  no operation moved by 1% of the time
where the time goes in v5:
time: 77.9 us; the launch traced here: 77.7 us
  waiting for transfers between devices  35.4 us (45%)
  Pallas kernels  22.1 us (28%)
  starting transfers between devices  19.4 us (25%)
  between operations  0.8 us (1%)
    ppermute x12, waiting for transfers between devices, exchange(): return lax.ppermute(value, 'seq', [(i, i ^ PAIR * m) for i in range(count)])  35.4 us
    ppermute x12, starting transfers between devices, exchange(): return lax.ppermute(value, 'seq', [(i, i ^ PAIR * m) for i in range(count)])  17.6 us
    pallas_call x1, Pallas kernels, attend(): pl.pallas_call(kernel, out_shape=[shape((each * rows, width), jnp.bfloat1...  5.04 us
    pallas_call x1, Pallas kernels, within(): pl.pallas_call(kernel, out_shape=shape((heads, rows, width), jnp.float32)...  5.03 us
    pallas_call x1, Pallas kernels, pack(): pl.pallas_call(kernel, out_shape=[shape((3 * hosted + (m == 0), rows, wid...  3.73 us
    pallas_call x1, Pallas kernels, totals_of(): pl.pallas_call(kernel, out_shape=[shape((few * width + LOG_ROWS, width),...  3.39 us
    pallas_call x1, Pallas kernels, finish(): pl.pallas_call(kernel, out_shape=shape((rows, heads, width), jnp.bfloat16...  2.88 us
    ppermute x7, starting transfers between devices, swap_cores(): return lax.ppermute(value, 'seq', [(i, i ^ 1) for i in range(count)])  1.74 us
  transfers between devices with their start and end apart: 19, of which 7 were waited for; matrix products, arithmetic and copies ran while one was open for 0% of the time, Pallas kernels for 27%

profile of v5, /device:TPU:0, one launch (start us, length us, event | category | flops | bytes accessed | tf_op | source)
XLA Modules:
  0.0 77.7 jit_solution(9464792861424506333)
XLA Ops:
  0.6 0.5 collective-permute-start.2
  1.1 0.1 collective-permute-start.3
  1.2 3.7 %pack.1 = (bf16[25,128,128]{2,1,0:T(8,128)(2,1)}, bf16[24,128,128]{2,1,0:T(8,128)(2,1)}, bf16[24,128,128]{2,1,0:T(8,128)(2,1)}, bf16[24,128,128]{2,1,0:T(8,128)(2,1)}) custom-call(s32[1]{0:T(128)} %bitcast.place_ref, bf16[32,128]{1,0:T(8,128)(2,1)} %bitcast.4, bf16[128,32,128]{2,1,0:T(8,128)(2,1)} %q_ref.3, bf16[128,32,128]{2,1,0:T(8,128)(2,1)} %k_ref.3, ...), custom_call_target="tpu_custom_call" | custom-call | flops 2147483648 | bytes 1 | tf_op jit(solution)/shard_map/pack/pallas_call | solution.py:113
  5.0 0.5 collective-permute-start.4
  5.5 2.6 %collective-permute-start = (bf16[24,128,128]{2,1,0:T(8,128)(2,1)}, bf16[24,128,128]{2,1,0:T(8,128)(2,1)S(1)}, u32[]{:S(2)}, u32[]{:S(2)}) collective-permute-start(bf16[24,128,128]{2,1,0:T(8,128)(2,1)} %get-tuple-element.35), channel_id=1, source_target_pairs={{0,2},{1,3},{2,0},{3,1},{4,6},{5,7},{6,4},{7,5},{8,10},{9,11},{10,... | collective-permute-start | bytes 2359304 | tf_op jit(solution)/shard_map/ppermute | solution.py:535
  8.0 1.5 %collective-permute-start.1 = (bf16[24,128,128]{2,1,0:T(8,128)(2,1)}, bf16[24,128,128]{2,1,0:T(8,128)(2,1)S(1)}, u32[]{:S(2)}, u32[]{:S(2)}) collective-permute-start(bf16[24,128,128]{2,1,0:T(8,128)(2,1)} %get-tuple-element.36), channel_id=1, source_target_pairs={{0,4},{1,5},{2,6},{3,7},{4,0},{5,1},{6,2},{7,3},{8,12},{9,13},{10,... | collective-permute-start | bytes 2359304 | tf_op jit(solution)/shard_map/ppermute | solution.py:535
  9.6 3.4 %totals_of.1 = (bf16[528,128]{1,0:T(8,128)(2,1)S(1)}, bf16[528,128]{1,0:T(8,128)(2,1)S(1)}, bf16[528,128]{1,0:T(8,128)(2,1)S(1)}, bf16[528,128]{1,0:T(8,128)(2,1)S(1)}) custom-call(s32[1]{0:T(128)} %bitcast.place_ref, bf16[128,32,128]{2,1,0:T(8,128)(2,1)S(1)} %copy-done, bf16[128,32,128]{2,1,0:T(8,128)(2,1)S(1)} %copy-done.1, bf16[32,128]{1,0:T(8,128)(2,1)S(1)} %bitcast.5, ...), custom_call_target="tpu_custom_call" | custom-call | flops 3221225472 | bytes 1 | tf_op jit(solution)/shard_map/totals_of/pallas_call | solution.py:333
  13.0 1.9 %collective-permute-start.5 = (bf16[24,128,128]{2,1,0:T(8,128)(2,1)S(1)}, bf16[24,128,128]{2,1,0:T(8,128)(2,1)S(1)}, u32[]{:S(2)}, u32[]{:S(2)}) collective-permute-start(bf16[24,128,128]{2,1,0:T(8,128)(2,1)S(1)} %copy-done.8), channel_id=1, source_target_pairs={{0,6},{1,7},{2,4},{3,5},{4,2},{5,3},{6,0},{7,1},{8,14},{9,15},{10,... | collective-permute-start | bytes 2359304 | tf_op jit(solution)/shard_map/ppermute | solution.py:535
  15.0 0.5 collective-permute-start.6
  15.5 1.1 %collective-permute-start.7 = (bf16[528,128]{1,0:T(8,128)(2,1)S(1)}, bf16[528,128]{1,0:T(8,128)(2,1)S(1)}, u32[]{:S(2)}, u32[]{:S(2)}) collective-permute-start(bf16[528,128]{1,0:T(8,128)(2,1)S(1)} %get-tuple-element.41), channel_id=1, source_target_pairs={{0,4},{1,5},{2,6},{3,7},{4,0},{5,1},{6,2},{7,3},{8,12},{9,13},{10,... | collective-permute-start | bytes 405512 | tf_op jit(solution)/shard_map/ppermute | solution.py:535
  16.6 10.1 %collective-permute-done.rest_1_ = bf16[24,128,128]{2,1,0:T(8,128)(2,1)S(1)} collective-permute-done((bf16[24,128,128]{2,1,0:T(8,128)(2,1)}, bf16[24,128,128]{2,1,0:T(8,128)(2,1)S(1)}, u32[]{:S(2)}, u32[]{:S(2)}) %collective-permute-start) | collective-permute-done | bytes 786464 | tf_op jit(solution)/shard_map/ppermute | solution.py:535
  26.6 2.9 %collective-permute-start.8 = (bf16[528,128]{1,0:T(8,128)(2,1)S(1)}, bf16[528,128]{1,0:T(8,128)(2,1)S(1)}, u32[]{:S(2)}, u32[]{:S(2)}) collective-permute-start(bf16[528,128]{1,0:T(8,128)(2,1)S(1)} %get-tuple-element.42), channel_id=1, source_target_pairs={{0,6},{1,7},{2,4},{3,5},{4,2},{5,3},{6,0},{7,1},{8,14},{9,15},{10,... | collective-permute-start | bytes 405512 | tf_op jit(solution)/shard_map/ppermute | solution.py:535
  29.5 5.0 %within.1.inner_ref = f32[32,128,128]{2,1,0:T(8,128)S(1)} custom-call(s32[1]{0:T(128)} %bitcast.place_ref, bf16[128,32,128]{2,1,0:T(8,128)(2,1)S(1)} %copy-done.2, bf16[128,32,128]{2,1,0:T(8,128)(2,1)S(1)} %copy-done, bf16[128,32,128]{2,1,0:T(8,128)(2,1)S(1)} %copy-done.1, bf16[32,128]{1,0:T(8,128)(2,1)S(1)} %bitcast.6, ...), custom_call_target="tpu_custom_call" | custom-call | flops 7516192768 | bytes 1 | tf_op jit(solution)/shard_map/within/pallas_call | solution.py:386
  34.6 10.9 %collective-permute-done.1.rest_2_ = bf16[24,128,128]{2,1,0:T(8,128)(2,1)S(1)} collective-permute-done((bf16[24,128,128]{2,1,0:T(8,128)(2,1)}, bf16[24,128,128]{2,1,0:T(8,128)(2,1)S(1)}, u32[]{:S(2)}, u32[]{:S(2)}) %collective-permute-start.1) | collective-permute-done | bytes 786464 | tf_op jit(solution)/shard_map/ppermute | solution.py:535
  45.5 0.9 %collective-permute-done.6.rest_1_ = bf16[528,128]{1,0:T(8,128)(2,1)S(1)} collective-permute-done((bf16[528,128]{1,0:T(8,128)(2,1)S(1)}, bf16[528,128]{1,0:T(8,128)(2,1)S(1)}, u32[]{:S(2)}, u32[]{:S(2)}) %collective-permute-start.6) | collective-permute-done | bytes 135200 | tf_op jit(solution)/shard_map/ppermute | solution.py:535
  46.4 4.1 %collective-permute-done.7.rest_2_ = bf16[528,128]{1,0:T(8,128)(2,1)S(1)} collective-permute-done((bf16[528,128]{1,0:T(8,128)(2,1)S(1)}, bf16[528,128]{1,0:T(8,128)(2,1)S(1)}, u32[]{:S(2)}, u32[]{:S(2)}) %collective-permute-start.7) | collective-permute-done | bytes 135200 | tf_op jit(solution)/shard_map/ppermute | solution.py:535
  50.5 0.5 collective-permute-start.10
  51.0 0.1 collective-permute-start.11
  51.1 0.6 scan_chips.1
  51.7 1.3 %collective-permute-start.12 = (bf16[512,128]{1,0:T(8,128)(2,1)S(1)}, bf16[512,128]{1,0:T(8,128)(2,1)S(1)}, u32[]{:S(2)}, u32[]{:S(2)}) collective-permute-start(bf16[512,128]{1,0:T(8,128)(2,1)S(1)} %get-tuple-element.56), channel_id=1, source_target_pairs={{0,2},{1,3},{2,0},{3,1},{4,6},{5,7},{6,4},{7,5},{8,10},{9,11},{10,... | collective-permute-start | bytes 393224 | tf_op jit(solution)/shard_map/ppermute | solution.py:535
  52.9 0.9 %collective-permute-start.13 = (bf16[512,128]{1,0:T(8,128)(2,1)S(1)}, bf16[512,128]{1,0:T(8,128)(2,1)S(1)}, u32[]{:S(2)}, u32[]{:S(2)}) collective-permute-start(bf16[512,128]{1,0:T(8,128)(2,1)S(1)} %get-tuple-element.58), channel_id=1, source_target_pairs={{0,4},{1,5},{2,6},{3,7},{4,0},{5,1},{6,2},{7,3},{8,12},{9,13},{10,... | collective-permute-start | bytes 393224 | tf_op jit(solution)/shard_map/ppermute | solution.py:535
  53.8 1.4 %collective-permute-start.14 = (bf16[512,128]{1,0:T(8,128)(2,1)S(1)}, bf16[512,128]{1,0:T(8,128)(2,1)S(1)}, u32[]{:S(2)}, u32[]{:S(2)}) collective-permute-start(bf16[512,128]{1,0:T(8,128)(2,1)S(1)} %get-tuple-element.60), channel_id=1, source_target_pairs={{0,6},{1,7},{2,4},{3,5},{4,2},{5,3},{6,0},{7,1},{8,14},{9,15},{10,... | collective-permute-start | bytes 393224 | tf_op jit(solution)/shard_map/ppermute | solution.py:535
  55.3 5.0 %attend.1 = (bf16[1024,128]{1,0:T(8,128)(2,1)S(1)}, bf16[1024,128]{1,0:T(8,128)(2,1)S(1)}, bf16[1024,128]{1,0:T(8,128)(2,1)S(1)}, bf16[1024,128]{1,0:T(8,128)(2,1)S(1)}) custom-call(s32[1]{0:T(128)} %bitcast.place_ref, s32[8,8]{1,0:T(8,128)S(1)} %copy-done.6, s32[8]{0:T(128)S(1)} %copy-done.7, bf16[25,128,128]{2,1,0:T(8,128)(2,1)S(1)} %copy-done.3, ...), custom_call_target="tpu_custom_call" | custom-call | flops 7516192768 | bytes 1 | tf_op jit(solution)/shard_map/attend/pallas_call | solution.py:233
  60.3 1.1 %collective-permute-done.14.rest_3_ = bf16[512,128]{1,0:T(8,128)(2,1)S(1)} collective-permute-done((bf16[512,128]{1,0:T(8,128)(2,1)S(1)}, bf16[512,128]{1,0:T(8,128)(2,1)S(1)}, u32[]{:S(2)}, u32[]{:S(2)}) %collective-permute-start.14) | collective-permute-done | bytes 131104 | tf_op jit(solution)/shard_map/ppermute | solution.py:535
  61.4 0.1 collective-permute-start.15
  61.5 1.0 %collective-permute-start.16 = (bf16[1024,128]{1,0:T(8,128)(2,1)S(1)}, bf16[1024,128]{1,0:T(8,128)(2,1)S(1)}, u32[]{:S(2)}, u32[]{:S(2)}) collective-permute-start(bf16[1024,128]{1,0:T(8,128)(2,1)S(1)} %get-tuple-element.63), channel_id=1, source_target_pairs={{0,2},{1,3},{2,0},{3,1},{4,6},{5,7},{6,4},{7,5},{8,10},{9,11},{10,... | collective-permute-start | bytes 786440 | tf_op jit(solution)/shard_map/ppermute | solution.py:535
  62.5 1.3 %collective-permute-start.17 = (bf16[1024,128]{1,0:T(8,128)(2,1)S(1)}, bf16[1024,128]{1,0:T(8,128)(2,1)S(1)}, u32[]{:S(2)}, u32[]{:S(2)}) collective-permute-start(bf16[1024,128]{1,0:T(8,128)(2,1)S(1)} %get-tuple-element.64), channel_id=1, source_target_pairs={{0,4},{1,5},{2,6},{3,7},{4,0},{5,1},{6,2},{7,3},{8,12},{9,13},{10,... | collective-permute-start | bytes 786440 | tf_op jit(solution)/shard_map/ppermute | solution.py:535
  63.8 1.2 %collective-permute-start.18 = (bf16[1024,128]{1,0:T(8,128)(2,1)S(1)}, bf16[1024,128]{1,0:T(8,128)(2,1)S(1)}, u32[]{:S(2)}, u32[]{:S(2)}) collective-permute-start(bf16[1024,128]{1,0:T(8,128)(2,1)S(1)} %get-tuple-element.65), channel_id=1, source_target_pairs={{0,6},{1,7},{2,4},{3,5},{4,2},{5,3},{6,0},{7,1},{8,14},{9,15},{10,... | collective-permute-start | bytes 786440 | tf_op jit(solution)/shard_map/ppermute | solution.py:535
  65.1 2.9 %finish.1 = bf16[128,32,128]{2,1,0:T(8,128)(2,1)} custom-call(s32[1]{0:T(128)} %bitcast.place_ref, bf16[128,32,128]{2,1,0:T(8,128)(2,1)S(1)} %copy-done.2, bf16[32,128]{1,0:T(8,128)(2,1)S(1)} %bitcast.7, f32[32,128]{1,0:T(8,128)S(1)} %bitcast.3, f32[32,128,128]{2,1,0:T(8,128)S(1)} %within.1.inner_ref, bf16[16,128,128]{2,1,0:T(8,128)(2,1)S(1)} %gather_entry.1.own_ref, ...), custom_call_target="tpu_custom_call" | custom-call | flops 4294967296 | bytes 1 | tf_op jit(solution)/shard_map/finish/pallas_call | solution.py:507
  68.0 2.7 %collective-permute-done.16.rest_1_ = bf16[1024,128]{1,0:T(8,128)(2,1)S(1)} collective-permute-done((bf16[1024,128]{1,0:T(8,128)(2,1)S(1)}, bf16[1024,128]{1,0:T(8,128)(2,1)S(1)}, u32[]{:S(2)}, u32[]{:S(2)}) %collective-permute-start.16) | collective-permute-done | bytes 262176 | tf_op jit(solution)/shard_map/ppermute | solution.py:535
  70.7 5.6 %collective-permute-done.17.rest_2_ = bf16[1024,128]{1,0:T(8,128)(2,1)S(1)} collective-permute-done((bf16[1024,128]{1,0:T(8,128)(2,1)S(1)}, bf16[1024,128]{1,0:T(8,128)(2,1)S(1)}, u32[]{:S(2)}, u32[]{:S(2)}) %collective-permute-start.17) | collective-permute-done | bytes 262176 | tf_op jit(solution)/shard_map/ppermute | solution.py:535
  76.3 1.4 %unpack.1 = bf16[128,32,128]{2,1,0:T(8,128)(2,1)} custom-call(s32[1]{0:T(128)} %bitcast.place_ref, bf16[1024,128]{1,0:T(8,128)(2,1)S(1)} %get-tuple-element.62.rest_0_, bf16[1024,128]{1,0:T(8,128)(2,1)S(1)} %collective-permute-done.16.rest_1_, bf16[1024,128]{1,0:T(8,128)(2,1)S(1)} %collective-permute-done.17.rest_2_, ...), custom_call_target="tpu_custom_call" | custom-call | flops 2147483648 | bytes 1 | tf_op jit(solution)/shard_map/unpack/pallas_call | solution.py:268
  (32 shorter events, 0.1 us)
Async XLA Ops:
  0.6 8.9 %collective-permute-start.2 = (bf16[128,32,128]{2,1,0:T(8,128)(2,1)}, bf16[128,32,128]{2,1,0:T(8,128)(2,1)S(1)}, u32[]{:S(2)}, u32[]{:S(2)}) collective-permute-start(bf16[128,32,128]{2,1,0:T(8,128)(2,1)} %k_ref.5), channel_id=1, source_target_pairs={{0,1},{1,0},{2,3},{3,2},{4,5},{5,4},{6,7},{7,6},{8,9},{9,8},{10,11... | collective-permute-start | bytes 3145736 | tf_op jit(solution)/shard_map/ppermute | solution.py:541
  1.1 8.4 %collective-permute-start.3 = (bf16[128,32,128]{2,1,0:T(8,128)(2,1)}, bf16[128,32,128]{2,1,0:T(8,128)(2,1)S(1)}, u32[]{:S(2)}, u32[]{:S(2)}) collective-permute-start(bf16[128,32,128]{2,1,0:T(8,128)(2,1)} %v_ref.5), channel_id=1, source_target_pairs={{0,1},{1,0},{2,3},{3,2},{4,5},{5,4},{6,7},{7,6},{8,9},{9,8},{10,11... | collective-permute-start | bytes 3145736 | tf_op jit(solution)/shard_map/ppermute | solution.py:541
  1.2 8.3 %copy-start = (bf16[128,32,128]{2,1,0:T(8,128)(2,1)S(1)}, bf16[128,32,128]{2,1,0:T(8,128)(2,1)}, u32[]{:S(2)}) copy-start(bf16[128,32,128]{2,1,0:T(8,128)(2,1)} %k_ref.5) | copy-start | bytes 3145732
  1.2 8.4 %copy-start.1 = (bf16[128,32,128]{2,1,0:T(8,128)(2,1)S(1)}, bf16[128,32,128]{2,1,0:T(8,128)(2,1)}, u32[]{:S(2)}) copy-start(bf16[128,32,128]{2,1,0:T(8,128)(2,1)} %v_ref.5) | copy-start | bytes 3145732
  1.2 8.4 %copy-start.5 = (bf16[128,32]{0,1:T(8,128)(2,1)S(1)}, bf16[128,32]{0,1:T(8,128)(2,1)}, u32[]{:S(2)}) copy-start(bf16[128,32]{0,1:T(8,128)(2,1)} %param.13) | copy-start | bytes 24580
  5.0 4.6 %collective-permute-start.4 = (bf16[25,128,128]{2,1,0:T(8,128)(2,1)}, bf16[25,128,128]{2,1,0:T(8,128)(2,1)S(1)}, u32[]{:S(2)}, u32[]{:S(2)}) collective-permute-start(bf16[25,128,128]{2,1,0:T(8,128)(2,1)} %get-tuple-element.50.rest_0_), channel_id=1, source_target_pairs={{0,1},{1,0},{2,3},{3,2},{4,5},{5,4},{6,7},{7,6},{8,9},{9,8},{10,11... | collective-permute-start | bytes 2457608 | tf_op jit(solution)/shard_map/ppermute | solution.py:541
  5.5 21.2 %collective-permute-start = (bf16[24,128,128]{2,1,0:T(8,128)(2,1)}, bf16[24,128,128]{2,1,0:T(8,128)(2,1)S(1)}, u32[]{:S(2)}, u32[]{:S(2)}) collective-permute-start(bf16[24,128,128]{2,1,0:T(8,128)(2,1)} %get-tuple-element.35), channel_id=1, source_target_pairs={{0,2},{1,3},{2,0},{3,1},{4,6},{5,7},{6,4},{7,5},{8,10},{9,11},{10,... | collective-permute-start | bytes 2359304 | tf_op jit(solution)/shard_map/ppermute | solution.py:535
  8.0 5.0 %copy-start.8 = (bf16[24,128,128]{2,1,0:T(8,128)(2,1)S(1)}, bf16[24,128,128]{2,1,0:T(8,128)(2,1)}, u32[]{:S(2)}) copy-start(bf16[24,128,128]{2,1,0:T(8,128)(2,1)} %get-tuple-element.39) | copy-start | bytes 2359300
  8.0 21.5 %copy-start.2 = (bf16[128,32,128]{2,1,0:T(8,128)(2,1)S(1)}, bf16[128,32,128]{2,1,0:T(8,128)(2,1)}, u32[]{:S(2)}) copy-start(bf16[128,32,128]{2,1,0:T(8,128)(2,1)} %q_ref.5) | copy-start | bytes 3145732
  8.0 37.5 %collective-permute-start.1 = (bf16[24,128,128]{2,1,0:T(8,128)(2,1)}, bf16[24,128,128]{2,1,0:T(8,128)(2,1)S(1)}, u32[]{:S(2)}, u32[]{:S(2)}) collective-permute-start(bf16[24,128,128]{2,1,0:T(8,128)(2,1)} %get-tuple-element.36), channel_id=1, source_target_pairs={{0,4},{1,5},{2,6},{3,7},{4,0},{5,1},{6,2},{7,3},{8,12},{9,13},{10,... | collective-permute-start | bytes 2359304 | tf_op jit(solution)/shard_map/ppermute | solution.py:535
  13.0 37.5 %collective-permute-start.5 = (bf16[24,128,128]{2,1,0:T(8,128)(2,1)S(1)}, bf16[24,128,128]{2,1,0:T(8,128)(2,1)S(1)}, u32[]{:S(2)}, u32[]{:S(2)}) collective-permute-start(bf16[24,128,128]{2,1,0:T(8,128)(2,1)S(1)} %copy-done.8), channel_id=1, source_target_pairs={{0,6},{1,7},{2,4},{3,5},{4,2},{5,3},{6,0},{7,1},{8,14},{9,15},{10,... | collective-permute-start | bytes 2359304 | tf_op jit(solution)/shard_map/ppermute | solution.py:535
  15.0 31.5 %collective-permute-start.6 = (bf16[528,128]{1,0:T(8,128)(2,1)S(1)}, bf16[528,128]{1,0:T(8,128)(2,1)S(1)}, u32[]{:S(2)}, u32[]{:S(2)}) collective-permute-start(bf16[528,128]{1,0:T(8,128)(2,1)S(1)} %get-tuple-element.40), channel_id=1, source_target_pairs={{0,2},{1,3},{2,0},{3,1},{4,6},{5,7},{6,4},{7,5},{8,10},{9,11},{10,... | collective-permute-start | bytes 405512 | tf_op jit(solution)/shard_map/ppermute | solution.py:535
  15.5 35.0 %collective-permute-start.7 = (bf16[528,128]{1,0:T(8,128)(2,1)S(1)}, bf16[528,128]{1,0:T(8,128)(2,1)S(1)}, u32[]{:S(2)}, u32[]{:S(2)}) collective-permute-start(bf16[528,128]{1,0:T(8,128)(2,1)S(1)} %get-tuple-element.41), channel_id=1, source_target_pairs={{0,4},{1,5},{2,6},{3,7},{4,0},{5,1},{6,2},{7,3},{8,12},{9,13},{10,... | collective-permute-start | bytes 405512 | tf_op jit(solution)/shard_map/ppermute | solution.py:535
  26.6 23.9 %collective-permute-start.8 = (bf16[528,128]{1,0:T(8,128)(2,1)S(1)}, bf16[528,128]{1,0:T(8,128)(2,1)S(1)}, u32[]{:S(2)}, u32[]{:S(2)}) collective-permute-start(bf16[528,128]{1,0:T(8,128)(2,1)S(1)} %get-tuple-element.42), channel_id=1, source_target_pairs={{0,6},{1,7},{2,4},{3,5},{4,2},{5,3},{6,0},{7,1},{8,14},{9,15},{10,... | collective-permute-start | bytes 405512 | tf_op jit(solution)/shard_map/ppermute | solution.py:535
  34.6 20.6 %copy-start.3 = (bf16[25,128,128]{2,1,0:T(8,128)(2,1)S(1)}, bf16[25,128,128]{2,1,0:T(8,128)(2,1)}, u32[]{:S(2)}) copy-start(bf16[25,128,128]{2,1,0:T(8,128)(2,1)} %get-tuple-element.50.rest_0_) | copy-start | bytes 2457604
  34.6 20.6 %copy-start.6 = (s32[8,8]{1,0:T(8,128)S(1)}, s32[8,8]{1,0:T(8,128)}, u32[]{:S(2)}) copy-start(s32[8,8]{1,0:T(8,128)} %bits_ref.1) | copy-start | bytes 772
  34.6 20.6 %copy-start.7 = (s32[8]{0:T(128)S(1)}, s32[8]{0:T(128)}, u32[]{:S(2)}) copy-start(s32[8]{0:T(128)} %agents_ref.1) | copy-start | bytes 100
  50.5 3.3 %collective-permute-start.9 = (bf16[24,128,128]{2,1,0:T(8,128)(2,1)S(1)}, bf16[24,128,128]{2,1,0:T(8,128)(2,1)S(1)}, u32[]{:S(2)}, u32[]{:S(2)}) collective-permute-start(bf16[24,128,128]{2,1,0:T(8,128)(2,1)S(1)} %collective-permute-done.rest_1_), channel_id=1, source_target_pairs={{0,1},{1,0},{2,3},{3,2},{4,5},{5,4},{6,7},{7,6},{8,9},{9,8},{10,11... | collective-permute-start | bytes 2359304 | tf_op jit(solution)/shard_map/ppermute | solution.py:541
  50.5 4.7 %collective-permute-start.10 = (bf16[24,128,128]{2,1,0:T(8,128)(2,1)S(1)}, bf16[24,128,128]{2,1,0:T(8,128)(2,1)S(1)}, u32[]{:S(2)}, u32[]{:S(2)}) collective-permute-start(bf16[24,128,128]{2,1,0:T(8,128)(2,1)S(1)} %collective-permute-done.1.rest_2_), channel_id=1, source_target_pairs={{0,1},{1,0},{2,3},{3,2},{4,5},{5,4},{6,7},{7,6},{8,9},{9,8},{10,11... | collective-permute-start | bytes 2359304 | tf_op jit(solution)/shard_map/ppermute | solution.py:541
  51.0 4.2 %collective-permute-start.11 = (bf16[24,128,128]{2,1,0:T(8,128)(2,1)S(1)}, bf16[24,128,128]{2,1,0:T(8,128)(2,1)S(1)}, u32[]{:S(2)}, u32[]{:S(2)}) collective-permute-start(bf16[24,128,128]{2,1,0:T(8,128)(2,1)S(1)} %collective-permute-done.5.rest_3_), channel_id=1, source_target_pairs={{0,1},{1,0},{2,3},{3,2},{4,5},{5,4},{6,7},{7,6},{8,9},{9,8},{10,11... | collective-permute-start | bytes 2359304 | tf_op jit(solution)/shard_map/ppermute | solution.py:541
  51.7 9.7 %collective-permute-start.12 = (bf16[512,128]{1,0:T(8,128)(2,1)S(1)}, bf16[512,128]{1,0:T(8,128)(2,1)S(1)}, u32[]{:S(2)}, u32[]{:S(2)}) collective-permute-start(bf16[512,128]{1,0:T(8,128)(2,1)S(1)} %get-tuple-element.56), channel_id=1, source_target_pairs={{0,2},{1,3},{2,0},{3,1},{4,6},{5,7},{6,4},{7,5},{8,10},{9,11},{10,... | collective-permute-start | bytes 393224 | tf_op jit(solution)/shard_map/ppermute | solution.py:535
  52.9 8.4 %collective-permute-start.13 = (bf16[512,128]{1,0:T(8,128)(2,1)S(1)}, bf16[512,128]{1,0:T(8,128)(2,1)S(1)}, u32[]{:S(2)}, u32[]{:S(2)}) collective-permute-start(bf16[512,128]{1,0:T(8,128)(2,1)S(1)} %get-tuple-element.58), channel_id=1, source_target_pairs={{0,4},{1,5},{2,6},{3,7},{4,0},{5,1},{6,2},{7,3},{8,12},{9,13},{10,... | collective-permute-start | bytes 393224 | tf_op jit(solution)/shard_map/ppermute | solution.py:535
  53.8 11.3 %copy-start.4 = (f32[4096]{0:T(1024)S(1)}, f32[4096]{0:T(1024)}, u32[]{:S(2)}) copy-start(f32[4096]{0:T(1024)} %param.14) | copy-start | bytes 49156
  53.8 7.6 %collective-permute-start.14 = (bf16[512,128]{1,0:T(8,128)(2,1)S(1)}, bf16[512,128]{1,0:T(8,128)(2,1)S(1)}, u32[]{:S(2)}, u32[]{:S(2)}) collective-permute-start(bf16[512,128]{1,0:T(8,128)(2,1)S(1)} %get-tuple-element.60), channel_id=1, source_target_pairs={{0,6},{1,7},{2,4},{3,5},{4,2},{5,3},{6,0},{7,1},{8,14},{9,15},{10,... | collective-permute-start | bytes 393224 | tf_op jit(solution)/shard_map/ppermute | solution.py:535
  61.4 3.6 %collective-permute-start.15 = (bf16[16,128,128]{2,1,0:T(8,128)(2,1)S(1)}, bf16[16,128,128]{2,1,0:T(8,128)(2,1)S(1)}, u32[]{:S(2)}, u32[]{:S(2)}) collective-permute-start(bf16[16,128,128]{2,1,0:T(8,128)(2,1)S(1)} %gather_entry.1.own_ref), channel_id=1, source_target_pairs={{0,1},{1,0},{2,3},{3,2},{4,5},{5,4},{6,7},{7,6},{8,9},{9,8},{10,11... | collective-permute-start | bytes 1572872 | tf_op jit(solution)/shard_map/ppermute | solution.py:541
  61.5 9.2 %collective-permute-start.16 = (bf16[1024,128]{1,0:T(8,128)(2,1)S(1)}, bf16[1024,128]{1,0:T(8,128)(2,1)S(1)}, u32[]{:S(2)}, u32[]{:S(2)}) collective-permute-start(bf16[1024,128]{1,0:T(8,128)(2,1)S(1)} %get-tuple-element.63), channel_id=1, source_target_pairs={{0,2},{1,3},{2,0},{3,1},{4,6},{5,7},{6,4},{7,5},{8,10},{9,11},{10,... | collective-permute-start | bytes 786440 | tf_op jit(solution)/shard_map/ppermute | solution.py:535
  62.5 13.8 %collective-permute-start.17 = (bf16[1024,128]{1,0:T(8,128)(2,1)S(1)}, bf16[1024,128]{1,0:T(8,128)(2,1)S(1)}, u32[]{:S(2)}, u32[]{:S(2)}) collective-permute-start(bf16[1024,128]{1,0:T(8,128)(2,1)S(1)} %get-tuple-element.64), channel_id=1, source_target_pairs={{0,4},{1,5},{2,6},{3,7},{4,0},{5,1},{6,2},{7,3},{8,12},{9,13},{10,... | collective-permute-start | bytes 786440 | tf_op jit(solution)/shard_map/ppermute | solution.py:535
  63.8 12.5 %collective-permute-start.18 = (bf16[1024,128]{1,0:T(8,128)(2,1)S(1)}, bf16[1024,128]{1,0:T(8,128)(2,1)S(1)}, u32[]{:S(2)}, u32[]{:S(2)}) collective-permute-start(bf16[1024,128]{1,0:T(8,128)(2,1)S(1)} %get-tuple-element.65), channel_id=1, source_target_pairs={{0,6},{1,7},{2,4},{3,5},{4,2},{5,3},{6,0},{7,1},{8,14},{9,15},{10,... | collective-permute-start | bytes 786440 | tf_op jit(solution)/shard_map/ppermute | solution.py:535

commit v6 on v5

--- a/solution.py
+++ b/solution.py
@@ -7,8 +7,7 @@
 
 EPSILON = 1e-06
 PAIR = 2
-ABREAST = 2
-WEIGHT = 1 << 29
+WEIGHT = 1 << 31
 TURN = 8
 LOG_ROWS = 16
 LOG2E = 1.4426950408889634
@@ -133,67 +132,48 @@
     _, rows, width = own[0].shape
     slots = PAIR * chips
     scale = width**-0.5 * LOG2E
-    most = sum(PAIR * chip + PAIR - 1 for chip in range(chips)) + ABREAST - 1
+    most = sum(PAIR * chip + PAIR - 1 for chip in range(chips))
 
     def kernel(place_ref, bits_ref, agents_ref, *rest):
         ins, outs = rest[:slots], rest[slots : slots + chips]
-        held, scores, top, total, mixed, probs, query_of, key_of, sems = rest[slots + chips :]
+        queries, scores, top, total, mixed, probs, query_of = rest[slots + chips :]
         me = place_ref[0]
         chip, core = me // PAIR, me % PAIR
-        spans = [(0, 3 * each)] * chips + [(each, 2 * each)] * chips
-        copies = [
-            pltpu.make_async_copy(ins[j].at[pl.ds(at, size)], held.at[j, pl.ds(at, size)], sems.at[j])
-            for j, (at, size) in enumerate(spans)
-        ]
-        for copy in copies[:chips]:
-            copy.start()
-
-        found = jnp.int32(0)
-        for i in range(chips):
-            query_block = PAIR * (chip ^ i) + core
-
-            def list_pair(key_block, found, i=i, query_block=query_block):
-                seen = (bits_ref[query_block, key_block] == 1) | (
-                    agents_ref[query_block] == agents_ref[key_block]
+
+        found, ends = jnp.int32(0), []
+        for j in range(slots):
+            key_block = PAIR * (chip ^ (j % chips)) + (core if j < chips else PAIR - 1 - core)
+
+            for i in range(chips):
+                query_block = PAIR * (chip ^ i) + core
+                seen = (key_block < query_block) & (
+                    (bits_ref[query_block, key_block] == 1) | (agents_ref[query_block] == agents_ref[key_block])
                 )
                 query_of[found] = i
-                key_of[found] = (chip ^ (key_block // PAIR)) + chips * ((core + key_block) & (PAIR - 1))
-                return found + seen.astype(jnp.int32)
-
-            found = lax.fori_loop(0, query_block, list_pair, found)
-        for spare in range(ABREAST - 1):
-            query_of[found + spare] = 0
-            key_of[found + spare] = 0
-        rounds = (found + ABREAST - 1) // ABREAST
-
-        def head(j, which, h):
-            return held[j, which * each + h]
+                found = found + seen.astype(jnp.int32)
+            ends.append(found)
 
         lower = triangle(rows)
-        for copy in copies[:chips]:
-            copy.wait()
-        for copy in copies[chips:]:
-            copy.start()
         for i in range(chips):
             for h in range(each):
-                top[i, h] = jnp.where(lower, nn(head(i, 0, h), head(i, 1, h)), -1e30)
+                queries[i, h] = ins[i][h]
+                top[i, h] = jnp.where(lower, nn(ins[i][h], ins[i][each + h]), -1e30)
         for i in range(chips):
             for h in range(each):
                 total[i, h] = top[i, h]
-        for copy in copies[chips:]:
-            copy.wait()
-
-        def score(turn, carry):
-            for lane in range(ABREAST):
-                at = ABREAST * turn + lane
-                i, j = query_of[at], key_of[at]
+
+        for j in range(slots):
+
+            def score(at, carry, j=j):
+                i = query_of[at]
                 for h in range(each):
-                    s = jnp.where(at < found, nn(head(i, 0, h), head(j, 1, h)), -1e30)
+                    s = nn(queries[i, h], ins[j][each + h])
                     scores[at, h] = s
                     top[i, h] = jnp.maximum(top[i, h], s)
-            return carry
-
-        lax.fori_loop(0, rounds, score, 0)
+                return carry
+
+            lax.fori_loop(ends[j - 1] if j else 0, ends[j], score, 0)
+
         for i in range(chips):
             for h in range(each):
                 top[i, h] = jnp.broadcast_to(jnp.max(top[i, h], axis=1, keepdims=True), (rows, rows))
@@ -204,49 +184,45 @@
                 probs[i, h] = p.astype(jnp.bfloat16)
         for i in range(chips):
             for h in range(each):
-                mixed[i, h] = nn(probs[i, h], head(i, 2, h))
-
-        def weigh(turn, carry):
-            for lane in range(ABREAST):
-                at = ABREAST * turn + lane
+                mixed[i, h] = nn(probs[i, h], ins[i][2 * each + h])
+
+        for j in range(slots):
+
+            def weigh(at, carry, j=j):
                 i = query_of[at]
                 for h in range(each):
                     p = jnp.exp2((scores[at, h] - top[i, h]) * scale)
                     total[i, h] += p
-                    probs[lane, h] = p.astype(jnp.bfloat16)
-            for lane in range(ABREAST):
-                at = ABREAST * turn + lane
-                i, j = query_of[at], key_of[at]
+                    probs[0, h] = p.astype(jnp.bfloat16)
                 for h in range(each):
-                    mixed[i, h] += nn(probs[lane, h], head(j, 2, h))
-            return carry
-
-        lax.fori_loop(0, rounds, weigh, 0)
+                    mixed[i, h] += nn(probs[0, h], ins[j][2 * each + h])
+                return carry
+
+            lax.fori_loop(ends[j - 1] if j else 0, ends[j], weigh, 0)
+
         for i in range(chips):
             for h in range(each):
                 sums = jnp.sum(total[i, h], axis=1, keepdims=True)
                 outs[i][span_of(h, rows)] = (mixed[i, h] / sums).astype(jnp.bfloat16)
 
     block = (chips, each, rows, rows)
-    held_bytes = 2 * each * rows * (3 * slots * width + (chips + max(chips, ABREAST)) * rows)
+    in_bytes = 2 * each * rows * (3 * slots * width + 3 * chips * rows)
     score_bytes = 4 * each * rows * ((most + 2 * chips) * rows + chips * width)
     return pl.pallas_call(
         kernel,
         out_shape=[shape((each * rows, width), jnp.bfloat16)] * chips,
-        in_specs=[SMEM, SMEM, SMEM] + [ANY] * slots,
+        in_specs=[SMEM, SMEM, SMEM] + [VMEM] * slots,
         out_specs=[VMEM] * chips,
         scratch_shapes=[
-            pltpu.VMEM((slots, 3 * each, rows, width), jnp.bfloat16),
+            pltpu.VMEM((chips, each, rows, width), jnp.bfloat16),
             pltpu.VMEM((most, each, rows, rows), jnp.float32),
             pltpu.VMEM(block, jnp.float32),
             pltpu.VMEM(block, jnp.float32),
             pltpu.VMEM((chips, each, rows, width), jnp.float32),
-            pltpu.VMEM((max(chips, ABREAST), each, rows, rows), jnp.bfloat16),
-            pltpu.SMEM((most,), jnp.int32),
-            pltpu.SMEM((most,), jnp.int32),
-            pltpu.SemaphoreType.DMA((slots,)),
+            pltpu.VMEM(block, jnp.bfloat16),
+            pltpu.SMEM((most + 1,), jnp.int32),
         ],
-        compiler_params=params(8 + (held_bytes + score_bytes >> 20)),
+        compiler_params=params(6 + (in_bytes + score_bytes >> 20)),
         cost_estimate=cost(14),
         name="attend",
     )(place, bits, agents, *own, *other)

time: 77.9 us -> 78 us (level)
  Pallas kernels: 22.1 us -> 23.1 us
    pallas_call x1, Pallas kernels: 5.04 us -> 5.84 us  [attend(): pl.pallas_call(kernel, out_shape=[shape((each * rows, width), jnp.bfloat1...]
  transfers between devices with their start and end apart: 19 -> 19, of which waited for: 7 -> 6; matrix products, arithmetic and copies ran while one was open for 0% -> 0% of each run, Pallas kernels for 27% -> 28%
where the time goes in v6:
time: 78 us
  waiting for transfers between devices  34.7 us (44%)
  Pallas kernels  23.1 us (30%)
  starting transfers between devices  19.4 us (25%)
  between operations  0.81 us (1%)
    ppermute x12, waiting for transfers between devices, exchange(): return lax.ppermute(value, 'seq', [(i, i ^ PAIR * m) for i in range(count)])  34.7 us
    ppermute x12, starting transfers between devices, exchange(): return lax.ppermute(value, 'seq', [(i, i ^ PAIR * m) for i in range(count)])  17.6 us
    pallas_call x1, Pallas kernels, attend(): pl.pallas_call(kernel, out_shape=[shape((each * rows, width), jnp.bfloat1...  5.84 us
    pallas_call x1, Pallas kernels, within(): pl.pallas_call(kernel, out_shape=shape((heads, rows, width), jnp.float32)...  5.21 us
    pallas_call x1, Pallas kernels, pack(): pl.pallas_call(kernel, out_shape=[shape((3 * hosted + (m == 0), rows, wid...  3.73 us
    pallas_call x1, Pallas kernels, totals_of(): pl.pallas_call(kernel, out_shape=[shape((few * width + LOG_ROWS, width),...  3.39 us
    pallas_call x1, Pallas kernels, finish(): pl.pallas_call(kernel, out_shape=shape((rows, heads, width), jnp.bfloat16...  2.88 us
    ppermute x7, starting transfers between devices, swap_cores(): return lax.ppermute(value, 'seq', [(i, i ^ 1) for i in range(count)])  1.74 us
  transfers between devices with their start and end apart: 19, of which 6 were waited for; matrix products, arithmetic and copies ran while one was open for 0% of the time, Pallas kernels for 28%

profile of v6, /device:TPU:0, one launch (start us, length us, event | category | flops | bytes accessed | tf_op | source)
XLA Modules:
  0.0 78.0 jit_solution(11986024501224372043)
XLA Ops:
  0.6 0.5 collective-permute-start.2
  1.1 0.1 collective-permute-start.3
  1.2 3.7 %pack.1 = (bf16[25,128,128]{2,1,0:T(8,128)(2,1)}, bf16[24,128,128]{2,1,0:T(8,128)(2,1)}, bf16[24,128,128]{2,1,0:T(8,128)(2,1)}, bf16[24,128,128]{2,1,0:T(8,128)(2,1)}) custom-call(s32[1]{0:T(128)} %bitcast.place_ref, bf16[32,128]{1,0:T(8,128)(2,1)} %bitcast.4, bf16[128,32,128]{2,1,0:T(8,128)(2,1)} %q_ref.3, bf16[128,32,128]{2,1,0:T(8,128)(2,1)} %k_ref.3, ...), custom_call_target="tpu_custom_call" | custom-call | flops 8589934592 | bytes 1 | tf_op jit(solution)/shard_map/pack/pallas_call | solution.py:112
  5.0 0.5 collective-permute-start.4
  5.5 2.6 %collective-permute-start = (bf16[24,128,128]{2,1,0:T(8,128)(2,1)}, bf16[24,128,128]{2,1,0:T(8,128)(2,1)S(1)}, u32[]{:S(2)}, u32[]{:S(2)}) collective-permute-start(bf16[24,128,128]{2,1,0:T(8,128)(2,1)} %get-tuple-element.35), channel_id=1, source_target_pairs={{0,2},{1,3},{2,0},{3,1},{4,6},{5,7},{6,4},{7,5},{8,10},{9,11},{10,... | collective-permute-start | bytes 2359304 | tf_op jit(solution)/shard_map/ppermute | solution.py:511
  8.0 1.5 %collective-permute-start.1 = (bf16[24,128,128]{2,1,0:T(8,128)(2,1)}, bf16[24,128,128]{2,1,0:T(8,128)(2,1)S(1)}, u32[]{:S(2)}, u32[]{:S(2)}) collective-permute-start(bf16[24,128,128]{2,1,0:T(8,128)(2,1)} %get-tuple-element.36), channel_id=1, source_target_pairs={{0,4},{1,5},{2,6},{3,7},{4,0},{5,1},{6,2},{7,3},{8,12},{9,13},{10,... | collective-permute-start | bytes 2359304 | tf_op jit(solution)/shard_map/ppermute | solution.py:511
  9.6 3.4 %totals_of.1 = (bf16[528,128]{1,0:T(8,128)(2,1)S(1)}, bf16[528,128]{1,0:T(8,128)(2,1)S(1)}, bf16[528,128]{1,0:T(8,128)(2,1)S(1)}, bf16[528,128]{1,0:T(8,128)(2,1)S(1)}) custom-call(s32[1]{0:T(128)} %bitcast.place_ref, bf16[128,32,128]{2,1,0:T(8,128)(2,1)S(1)} %copy-done, bf16[128,32,128]{2,1,0:T(8,128)(2,1)S(1)} %copy-done.1, bf16[32,128]{1,0:T(8,128)(2,1)S(1)} %bitcast.5, ...), custom_call_target="tpu_custom_call" | custom-call | flops 12884901888 | bytes 1 | tf_op jit(solution)/shard_map/totals_of/pallas_call | solution.py:309
  13.0 1.0 %collective-permute-start.6 = (bf16[528,128]{1,0:T(8,128)(2,1)S(1)}, bf16[528,128]{1,0:T(8,128)(2,1)S(1)}, u32[]{:S(2)}, u32[]{:S(2)}) collective-permute-start(bf16[528,128]{1,0:T(8,128)(2,1)S(1)} %get-tuple-element.40), channel_id=1, source_target_pairs={{0,2},{1,3},{2,0},{3,1},{4,6},{5,7},{6,4},{7,5},{8,10},{9,11},{10,... | collective-permute-start | bytes 405512 | tf_op jit(solution)/shard_map/ppermute | solution.py:511
  14.0 1.5 %collective-permute-start.7 = (bf16[528,128]{1,0:T(8,128)(2,1)S(1)}, bf16[528,128]{1,0:T(8,128)(2,1)S(1)}, u32[]{:S(2)}, u32[]{:S(2)}) collective-permute-start(bf16[528,128]{1,0:T(8,128)(2,1)S(1)} %get-tuple-element.41), channel_id=1, source_target_pairs={{0,4},{1,5},{2,6},{3,7},{4,0},{5,1},{6,2},{7,3},{8,12},{9,13},{10,... | collective-permute-start | bytes 405512 | tf_op jit(solution)/shard_map/ppermute | solution.py:511
  15.5 1.0 %collective-permute-start.8 = (bf16[528,128]{1,0:T(8,128)(2,1)S(1)}, bf16[528,128]{1,0:T(8,128)(2,1)S(1)}, u32[]{:S(2)}, u32[]{:S(2)}) collective-permute-start(bf16[528,128]{1,0:T(8,128)(2,1)S(1)} %get-tuple-element.42), channel_id=1, source_target_pairs={{0,6},{1,7},{2,4},{3,5},{4,2},{5,3},{6,0},{7,1},{8,14},{9,15},{10,... | collective-permute-start | bytes 405512 | tf_op jit(solution)/shard_map/ppermute | solution.py:511
  16.6 10.1 %collective-permute-done.rest_1_ = bf16[24,128,128]{2,1,0:T(8,128)(2,1)S(1)} collective-permute-done((bf16[24,128,128]{2,1,0:T(8,128)(2,1)}, bf16[24,128,128]{2,1,0:T(8,128)(2,1)S(1)}, u32[]{:S(2)}, u32[]{:S(2)}) %collective-permute-start) | collective-permute-done | bytes 786464 | tf_op jit(solution)/shard_map/ppermute | solution.py:511
  26.6 2.9 %collective-permute-start.5 = (bf16[24,128,128]{2,1,0:T(8,128)(2,1)S(1)}, bf16[24,128,128]{2,1,0:T(8,128)(2,1)S(1)}, u32[]{:S(2)}, u32[]{:S(2)}) collective-permute-start(bf16[24,128,128]{2,1,0:T(8,128)(2,1)S(1)} %copy-done.8), channel_id=1, source_target_pairs={{0,6},{1,7},{2,4},{3,5},{4,2},{5,3},{6,0},{7,1},{8,14},{9,15},{10,... | collective-permute-start | bytes 2359304 | tf_op jit(solution)/shard_map/ppermute | solution.py:511
  29.6 5.2 %within.1.inner_ref = f32[32,128,128]{2,1,0:T(8,128)S(1)} custom-call(s32[1]{0:T(128)} %bitcast.place_ref, bf16[128,32,128]{2,1,0:T(8,128)(2,1)S(1)} %copy-done.2, bf16[128,32,128]{2,1,0:T(8,128)(2,1)S(1)} %copy-done, bf16[128,32,128]{2,1,0:T(8,128)(2,1)S(1)} %copy-done.1, bf16[32,128]{1,0:T(8,128)(2,1)S(1)} %bitcast.6, ...), custom_call_target="tpu_custom_call" | custom-call | flops 30064771072 | bytes 1 | tf_op jit(solution)/shard_map/within/pallas_call | solution.py:362
  34.8 0.0 copy-start.3
  34.8 15.7 %collective-permute-done.7.rest_2_ = bf16[528,128]{1,0:T(8,128)(2,1)S(1)} collective-permute-done((bf16[528,128]{1,0:T(8,128)(2,1)S(1)}, bf16[528,128]{1,0:T(8,128)(2,1)S(1)}, u32[]{:S(2)}, u32[]{:S(2)}) %collective-permute-start.7) | collective-permute-done | bytes 135200 | tf_op jit(solution)/shard_map/ppermute | solution.py:511
  50.5 0.5 collective-permute-start.10
  51.0 0.1 collective-permute-start.11
  51.1 0.6 scan_chips.1
  51.7 1.2 %collective-permute-start.12 = (bf16[512,128]{1,0:T(8,128)(2,1)S(1)}, bf16[512,128]{1,0:T(8,128)(2,1)S(1)}, u32[]{:S(2)}, u32[]{:S(2)}) collective-permute-start(bf16[512,128]{1,0:T(8,128)(2,1)S(1)} %get-tuple-element.56), channel_id=1, source_target_pairs={{0,2},{1,3},{2,0},{3,1},{4,6},{5,7},{6,4},{7,5},{8,10},{9,11},{10,... | collective-permute-start | bytes 393224 | tf_op jit(solution)/shard_map/ppermute | solution.py:511
  52.9 0.9 %collective-permute-start.13 = (bf16[512,128]{1,0:T(8,128)(2,1)S(1)}, bf16[512,128]{1,0:T(8,128)(2,1)S(1)}, u32[]{:S(2)}, u32[]{:S(2)}) collective-permute-start(bf16[512,128]{1,0:T(8,128)(2,1)S(1)} %get-tuple-element.58), channel_id=1, source_target_pairs={{0,4},{1,5},{2,6},{3,7},{4,0},{5,1},{6,2},{7,3},{8,12},{9,13},{10,... | collective-permute-start | bytes 393224 | tf_op jit(solution)/shard_map/ppermute | solution.py:511
  53.8 1.4 %collective-permute-start.14 = (bf16[512,128]{1,0:T(8,128)(2,1)S(1)}, bf16[512,128]{1,0:T(8,128)(2,1)S(1)}, u32[]{:S(2)}, u32[]{:S(2)}) collective-permute-start(bf16[512,128]{1,0:T(8,128)(2,1)S(1)} %get-tuple-element.60), channel_id=1, source_target_pairs={{0,6},{1,7},{2,4},{3,5},{4,2},{5,3},{6,0},{7,1},{8,14},{9,15},{10,... | collective-permute-start | bytes 393224 | tf_op jit(solution)/shard_map/ppermute | solution.py:511
  55.3 5.8 %attend.1 = (bf16[1024,128]{1,0:T(8,128)(2,1)S(1)}, bf16[1024,128]{1,0:T(8,128)(2,1)S(1)}, bf16[1024,128]{1,0:T(8,128)(2,1)S(1)}, bf16[1024,128]{1,0:T(8,128)(2,1)S(1)}) custom-call(s32[1]{0:T(128)} %bitcast.place_ref, s32[8,8]{1,0:T(8,128)S(1)} %copy-done.6, s32[8]{0:T(128)S(1)} %copy-done.7, bf16[25,128,128]{2,1,0:T(8,128)(2,1)S(1)} %copy-done.3, ...), custom_call_target="tpu_custom_call" | custom-call | flops 30064771072 | bytes 1 | tf_op jit(solution)/shard_map/attend/pallas_call | solution.py:211
  61.1 0.2 collective-permute-done.14.rest_3_
  61.4 0.1 collective-permute-start.15
  61.5 1.0 %collective-permute-start.16 = (bf16[1024,128]{1,0:T(8,128)(2,1)S(1)}, bf16[1024,128]{1,0:T(8,128)(2,1)S(1)}, u32[]{:S(2)}, u32[]{:S(2)}) collective-permute-start(bf16[1024,128]{1,0:T(8,128)(2,1)S(1)} %get-tuple-element.63), channel_id=1, source_target_pairs={{0,2},{1,3},{2,0},{3,1},{4,6},{5,7},{6,4},{7,5},{8,10},{9,11},{10,... | collective-permute-start | bytes 786440 | tf_op jit(solution)/shard_map/ppermute | solution.py:511
  62.5 1.3 %collective-permute-start.17 = (bf16[1024,128]{1,0:T(8,128)(2,1)S(1)}, bf16[1024,128]{1,0:T(8,128)(2,1)S(1)}, u32[]{:S(2)}, u32[]{:S(2)}) collective-permute-start(bf16[1024,128]{1,0:T(8,128)(2,1)S(1)} %get-tuple-element.64), channel_id=1, source_target_pairs={{0,4},{1,5},{2,6},{3,7},{4,0},{5,1},{6,2},{7,3},{8,12},{9,13},{10,... | collective-permute-start | bytes 786440 | tf_op jit(solution)/shard_map/ppermute | solution.py:511
  63.8 1.2 %collective-permute-start.18 = (bf16[1024,128]{1,0:T(8,128)(2,1)S(1)}, bf16[1024,128]{1,0:T(8,128)(2,1)S(1)}, u32[]{:S(2)}, u32[]{:S(2)}) collective-permute-start(bf16[1024,128]{1,0:T(8,128)(2,1)S(1)} %get-tuple-element.65), channel_id=1, source_target_pairs={{0,6},{1,7},{2,4},{3,5},{4,2},{5,3},{6,0},{7,1},{8,14},{9,15},{10,... | collective-permute-start | bytes 786440 | tf_op jit(solution)/shard_map/ppermute | solution.py:511
  65.0 2.9 %finish.1 = bf16[128,32,128]{2,1,0:T(8,128)(2,1)} custom-call(s32[1]{0:T(128)} %bitcast.place_ref, bf16[128,32,128]{2,1,0:T(8,128)(2,1)S(1)} %copy-done.2, bf16[32,128]{1,0:T(8,128)(2,1)S(1)} %bitcast.7, f32[32,128]{1,0:T(8,128)S(1)} %bitcast.3, f32[32,128,128]{2,1,0:T(8,128)S(1)} %within.1.inner_ref, bf16[16,128,128]{2,1,0:T(8,128)(2,1)S(1)} %gather_entry.1.own_ref, ...), custom_call_target="tpu_custom_call" | custom-call | flops 17179869184 | bytes 1 | tf_op jit(solution)/shard_map/finish/pallas_call | solution.py:483
  67.9 2.7 %collective-permute-done.16.rest_1_ = bf16[1024,128]{1,0:T(8,128)(2,1)S(1)} collective-permute-done((bf16[1024,128]{1,0:T(8,128)(2,1)S(1)}, bf16[1024,128]{1,0:T(8,128)(2,1)S(1)}, u32[]{:S(2)}, u32[]{:S(2)}) %collective-permute-start.16) | collective-permute-done | bytes 262176 | tf_op jit(solution)/shard_map/ppermute | solution.py:511
  70.7 4.7 %collective-permute-done.17.rest_2_ = bf16[1024,128]{1,0:T(8,128)(2,1)S(1)} collective-permute-done((bf16[1024,128]{1,0:T(8,128)(2,1)S(1)}, bf16[1024,128]{1,0:T(8,128)(2,1)S(1)}, u32[]{:S(2)}, u32[]{:S(2)}) %collective-permute-start.17) | collective-permute-done | bytes 262176 | tf_op jit(solution)/shard_map/ppermute | solution.py:511
  75.4 1.2 %collective-permute-done.18.rest_3_ = bf16[1024,128]{1,0:T(8,128)(2,1)S(1)} collective-permute-done((bf16[1024,128]{1,0:T(8,128)(2,1)S(1)}, bf16[1024,128]{1,0:T(8,128)(2,1)S(1)}, u32[]{:S(2)}, u32[]{:S(2)}) %collective-permute-start.18) | collective-permute-done | bytes 262176 | tf_op jit(solution)/shard_map/ppermute | solution.py:511
  76.6 1.4 %unpack.1 = bf16[128,32,128]{2,1,0:T(8,128)(2,1)} custom-call(s32[1]{0:T(128)} %bitcast.place_ref, bf16[1024,128]{1,0:T(8,128)(2,1)S(1)} %get-tuple-element.62.rest_0_, bf16[1024,128]{1,0:T(8,128)(2,1)S(1)} %collective-permute-done.16.rest_1_, bf16[1024,128]{1,0:T(8,128)(2,1)S(1)} %collective-permute-done.17.rest_2_, ...), custom_call_target="tpu_custom_call" | custom-call | flops 8589934592 | bytes 1 | tf_op jit(solution)/shard_map/unpack/pallas_call | solution.py:244
  (32 shorter events, 0.1 us)
Async XLA Ops:
  0.6 8.9 %collective-permute-start.2 = (bf16[128,32,128]{2,1,0:T(8,128)(2,1)}, bf16[128,32,128]{2,1,0:T(8,128)(2,1)S(1)}, u32[]{:S(2)}, u32[]{:S(2)}) collective-permute-start(bf16[128,32,128]{2,1,0:T(8,128)(2,1)} %k_ref.5), channel_id=1, source_target_pairs={{0,1},{1,0},{2,3},{3,2},{4,5},{5,4},{6,7},{7,6},{8,9},{9,8},{10,11... | collective-permute-start | bytes 3145736 | tf_op jit(solution)/shard_map/ppermute | solution.py:517
  1.1 8.4 %collective-permute-start.3 = (bf16[128,32,128]{2,1,0:T(8,128)(2,1)}, bf16[128,32,128]{2,1,0:T(8,128)(2,1)S(1)}, u32[]{:S(2)}, u32[]{:S(2)}) collective-permute-start(bf16[128,32,128]{2,1,0:T(8,128)(2,1)} %v_ref.5), channel_id=1, source_target_pairs={{0,1},{1,0},{2,3},{3,2},{4,5},{5,4},{6,7},{7,6},{8,9},{9,8},{10,11... | collective-permute-start | bytes 3145736 | tf_op jit(solution)/shard_map/ppermute | solution.py:517
  1.2 8.3 %copy-start = (bf16[128,32,128]{2,1,0:T(8,128)(2,1)S(1)}, bf16[128,32,128]{2,1,0:T(8,128)(2,1)}, u32[]{:S(2)}) copy-start(bf16[128,32,128]{2,1,0:T(8,128)(2,1)} %k_ref.5) | copy-start | bytes 3145732
  1.2 8.4 %copy-start.1 = (bf16[128,32,128]{2,1,0:T(8,128)(2,1)S(1)}, bf16[128,32,128]{2,1,0:T(8,128)(2,1)}, u32[]{:S(2)}) copy-start(bf16[128,32,128]{2,1,0:T(8,128)(2,1)} %v_ref.5) | copy-start | bytes 3145732
  1.2 8.4 %copy-start.5 = (bf16[128,32]{0,1:T(8,128)(2,1)S(1)}, bf16[128,32]{0,1:T(8,128)(2,1)}, u32[]{:S(2)}) copy-start(bf16[128,32]{0,1:T(8,128)(2,1)} %param.13) | copy-start | bytes 24580
  5.0 4.6 %collective-permute-start.4 = (bf16[25,128,128]{2,1,0:T(8,128)(2,1)}, bf16[25,128,128]{2,1,0:T(8,128)(2,1)S(1)}, u32[]{:S(2)}, u32[]{:S(2)}) collective-permute-start(bf16[25,128,128]{2,1,0:T(8,128)(2,1)} %get-tuple-element.50.rest_0_), channel_id=1, source_target_pairs={{0,1},{1,0},{2,3},{3,2},{4,5},{5,4},{6,7},{7,6},{8,9},{9,8},{10,11... | collective-permute-start | bytes 2457608 | tf_op jit(solution)/shard_map/ppermute | solution.py:517
  5.5 21.2 %collective-permute-start = (bf16[24,128,128]{2,1,0:T(8,128)(2,1)}, bf16[24,128,128]{2,1,0:T(8,128)(2,1)S(1)}, u32[]{:S(2)}, u32[]{:S(2)}) collective-permute-start(bf16[24,128,128]{2,1,0:T(8,128)(2,1)} %get-tuple-element.35), channel_id=1, source_target_pairs={{0,2},{1,3},{2,0},{3,1},{4,6},{5,7},{6,4},{7,5},{8,10},{9,11},{10,... | collective-permute-start | bytes 2359304 | tf_op jit(solution)/shard_map/ppermute | solution.py:511
  8.0 18.6 %copy-start.8 = (bf16[24,128,128]{2,1,0:T(8,128)(2,1)S(1)}, bf16[24,128,128]{2,1,0:T(8,128)(2,1)}, u32[]{:S(2)}) copy-start(bf16[24,128,128]{2,1,0:T(8,128)(2,1)} %get-tuple-element.39) | copy-start | bytes 2359300
  8.0 21.5 %copy-start.2 = (bf16[128,32,128]{2,1,0:T(8,128)(2,1)S(1)}, bf16[128,32,128]{2,1,0:T(8,128)(2,1)}, u32[]{:S(2)}) copy-start(bf16[128,32,128]{2,1,0:T(8,128)(2,1)} %q_ref.5) | copy-start | bytes 3145732
  8.0 26.8 %collective-permute-start.1 = (bf16[24,128,128]{2,1,0:T(8,128)(2,1)}, bf16[24,128,128]{2,1,0:T(8,128)(2,1)S(1)}, u32[]{:S(2)}, u32[]{:S(2)}) collective-permute-start(bf16[24,128,128]{2,1,0:T(8,128)(2,1)} %get-tuple-element.36), channel_id=1, source_target_pairs={{0,4},{1,5},{2,6},{3,7},{4,0},{5,1},{6,2},{7,3},{8,12},{9,13},{10,... | collective-permute-start | bytes 2359304 | tf_op jit(solution)/shard_map/ppermute | solution.py:511
  13.0 21.8 %collective-permute-start.6 = (bf16[528,128]{1,0:T(8,128)(2,1)S(1)}, bf16[528,128]{1,0:T(8,128)(2,1)S(1)}, u32[]{:S(2)}, u32[]{:S(2)}) collective-permute-start(bf16[528,128]{1,0:T(8,128)(2,1)S(1)} %get-tuple-element.40), channel_id=1, source_target_pairs={{0,2},{1,3},{2,0},{3,1},{4,6},{5,7},{6,4},{7,5},{8,10},{9,11},{10,... | collective-permute-start | bytes 405512 | tf_op jit(solution)/shard_map/ppermute | solution.py:511
  14.0 36.5 %collective-permute-start.7 = (bf16[528,128]{1,0:T(8,128)(2,1)S(1)}, bf16[528,128]{1,0:T(8,128)(2,1)S(1)}, u32[]{:S(2)}, u32[]{:S(2)}) collective-permute-start(bf16[528,128]{1,0:T(8,128)(2,1)S(1)} %get-tuple-element.41), channel_id=1, source_target_pairs={{0,4},{1,5},{2,6},{3,7},{4,0},{5,1},{6,2},{7,3},{8,12},{9,13},{10,... | collective-permute-start | bytes 405512 | tf_op jit(solution)/shard_map/ppermute | solution.py:511
  15.5 35.0 %collective-permute-start.8 = (bf16[528,128]{1,0:T(8,128)(2,1)S(1)}, bf16[528,128]{1,0:T(8,128)(2,1)S(1)}, u32[]{:S(2)}, u32[]{:S(2)}) collective-permute-start(bf16[528,128]{1,0:T(8,128)(2,1)S(1)} %get-tuple-element.42), channel_id=1, source_target_pairs={{0,6},{1,7},{2,4},{3,5},{4,2},{5,3},{6,0},{7,1},{8,14},{9,15},{10,... | collective-permute-start | bytes 405512 | tf_op jit(solution)/shard_map/ppermute | solution.py:511
  26.6 23.9 %collective-permute-start.5 = (bf16[24,128,128]{2,1,0:T(8,128)(2,1)S(1)}, bf16[24,128,128]{2,1,0:T(8,128)(2,1)S(1)}, u32[]{:S(2)}, u32[]{:S(2)}) collective-permute-start(bf16[24,128,128]{2,1,0:T(8,128)(2,1)S(1)} %copy-done.8), channel_id=1, source_target_pairs={{0,6},{1,7},{2,4},{3,5},{4,2},{5,3},{6,0},{7,1},{8,14},{9,15},{10,... | collective-permute-start | bytes 2359304 | tf_op jit(solution)/shard_map/ppermute | solution.py:511
  34.8 20.5 %copy-start.3 = (bf16[25,128,128]{2,1,0:T(8,128)(2,1)S(1)}, bf16[25,128,128]{2,1,0:T(8,128)(2,1)}, u32[]{:S(2)}) copy-start(bf16[25,128,128]{2,1,0:T(8,128)(2,1)} %get-tuple-element.50.rest_0_) | copy-start | bytes 2457604
  34.8 20.5 %copy-start.6 = (s32[8,8]{1,0:T(8,128)S(1)}, s32[8,8]{1,0:T(8,128)}, u32[]{:S(2)}) copy-start(s32[8,8]{1,0:T(8,128)} %bits_ref.1) | copy-start | bytes 772
  34.8 20.5 %copy-start.7 = (s32[8]{0:T(128)S(1)}, s32[8]{0:T(128)}, u32[]{:S(2)}) copy-start(s32[8]{0:T(128)} %agents_ref.1) | copy-start | bytes 100
  50.5 3.3 %collective-permute-start.9 = (bf16[24,128,128]{2,1,0:T(8,128)(2,1)S(1)}, bf16[24,128,128]{2,1,0:T(8,128)(2,1)S(1)}, u32[]{:S(2)}, u32[]{:S(2)}) collective-permute-start(bf16[24,128,128]{2,1,0:T(8,128)(2,1)S(1)} %collective-permute-done.rest_1_), channel_id=1, source_target_pairs={{0,1},{1,0},{2,3},{3,2},{4,5},{5,4},{6,7},{7,6},{8,9},{9,8},{10,11... | collective-permute-start | bytes 2359304 | tf_op jit(solution)/shard_map/ppermute | solution.py:517
  50.5 4.7 %collective-permute-start.10 = (bf16[24,128,128]{2,1,0:T(8,128)(2,1)S(1)}, bf16[24,128,128]{2,1,0:T(8,128)(2,1)S(1)}, u32[]{:S(2)}, u32[]{:S(2)}) collective-permute-start(bf16[24,128,128]{2,1,0:T(8,128)(2,1)S(1)} %collective-permute-done.1.rest_2_), channel_id=1, source_target_pairs={{0,1},{1,0},{2,3},{3,2},{4,5},{5,4},{6,7},{7,6},{8,9},{9,8},{10,11... | collective-permute-start | bytes 2359304 | tf_op jit(solution)/shard_map/ppermute | solution.py:517
  51.0 4.2 %collective-permute-start.11 = (bf16[24,128,128]{2,1,0:T(8,128)(2,1)S(1)}, bf16[24,128,128]{2,1,0:T(8,128)(2,1)S(1)}, u32[]{:S(2)}, u32[]{:S(2)}) collective-permute-start(bf16[24,128,128]{2,1,0:T(8,128)(2,1)S(1)} %collective-permute-done.5.rest_3_), channel_id=1, source_target_pairs={{0,1},{1,0},{2,3},{3,2},{4,5},{5,4},{6,7},{7,6},{8,9},{9,8},{10,11... | collective-permute-start | bytes 2359304 | tf_op jit(solution)/shard_map/ppermute | solution.py:517
  51.7 9.7 %collective-permute-start.12 = (bf16[512,128]{1,0:T(8,128)(2,1)S(1)}, bf16[512,128]{1,0:T(8,128)(2,1)S(1)}, u32[]{:S(2)}, u32[]{:S(2)}) collective-permute-start(bf16[512,128]{1,0:T(8,128)(2,1)S(1)} %get-tuple-element.56), channel_id=1, source_target_pairs={{0,2},{1,3},{2,0},{3,1},{4,6},{5,7},{6,4},{7,5},{8,10},{9,11},{10,... | collective-permute-start | bytes 393224 | tf_op jit(solution)/shard_map/ppermute | solution.py:511
  52.9 8.5 %collective-permute-start.13 = (bf16[512,128]{1,0:T(8,128)(2,1)S(1)}, bf16[512,128]{1,0:T(8,128)(2,1)S(1)}, u32[]{:S(2)}, u32[]{:S(2)}) collective-permute-start(bf16[512,128]{1,0:T(8,128)(2,1)S(1)} %get-tuple-element.58), channel_id=1, source_target_pairs={{0,4},{1,5},{2,6},{3,7},{4,0},{5,1},{6,2},{7,3},{8,12},{9,13},{10,... | collective-permute-start | bytes 393224 | tf_op jit(solution)/shard_map/ppermute | solution.py:511
  53.8 7.5 %collective-permute-start.14 = (bf16[512,128]{1,0:T(8,128)(2,1)S(1)}, bf16[512,128]{1,0:T(8,128)(2,1)S(1)}, u32[]{:S(2)}, u32[]{:S(2)}) collective-permute-start(bf16[512,128]{1,0:T(8,128)(2,1)S(1)} %get-tuple-element.60), channel_id=1, source_target_pairs={{0,6},{1,7},{2,4},{3,5},{4,2},{5,3},{6,0},{7,1},{8,14},{9,15},{10,... | collective-permute-start | bytes 393224 | tf_op jit(solution)/shard_map/ppermute | solution.py:511
  61.3 3.7 %copy-start.4 = (f32[4096]{0:T(1024)S(1)}, f32[4096]{0:T(1024)}, u32[]{:S(2)}) copy-start(f32[4096]{0:T(1024)} %param.14) | copy-start | bytes 49156
  61.4 3.6 %collective-permute-start.15 = (bf16[16,128,128]{2,1,0:T(8,128)(2,1)S(1)}, bf16[16,128,128]{2,1,0:T(8,128)(2,1)S(1)}, u32[]{:S(2)}, u32[]{:S(2)}) collective-permute-start(bf16[16,128,128]{2,1,0:T(8,128)(2,1)S(1)} %gather_entry.1.own_ref), channel_id=1, source_target_pairs={{0,1},{1,0},{2,3},{3,2},{4,5},{5,4},{6,7},{7,6},{8,9},{9,8},{10,11... | collective-permute-start | bytes 1572872 | tf_op jit(solution)/shard_map/ppermute | solution.py:517
  61.5 9.2 %collective-permute-start.16 = (bf16[1024,128]{1,0:T(8,128)(2,1)S(1)}, bf16[1024,128]{1,0:T(8,128)(2,1)S(1)}, u32[]{:S(2)}, u32[]{:S(2)}) collective-permute-start(bf16[1024,128]{1,0:T(8,128)(2,1)S(1)} %get-tuple-element.63), channel_id=1, source_target_pairs={{0,2},{1,3},{2,0},{3,1},{4,6},{5,7},{6,4},{7,5},{8,10},{9,11},{10,... | collective-permute-start | bytes 786440 | tf_op jit(solution)/shard_map/ppermute | solution.py:511
  62.5 12.9 %collective-permute-start.17 = (bf16[1024,128]{1,0:T(8,128)(2,1)S(1)}, bf16[1024,128]{1,0:T(8,128)(2,1)S(1)}, u32[]{:S(2)}, u32[]{:S(2)}) collective-permute-start(bf16[1024,128]{1,0:T(8,128)(2,1)S(1)} %get-tuple-element.64), channel_id=1, source_target_pairs={{0,4},{1,5},{2,6},{3,7},{4,0},{5,1},{6,2},{7,3},{8,12},{9,13},{10,... | collective-permute-start | bytes 786440 | tf_op jit(solution)/shard_map/ppermute | solution.py:511
  63.8 12.7 %collective-permute-start.18 = (bf16[1024,128]{1,0:T(8,128)(2,1)S(1)}, bf16[1024,128]{1,0:T(8,128)(2,1)S(1)}, u32[]{:S(2)}, u32[]{:S(2)}) collective-permute-start(bf16[1024,128]{1,0:T(8,128)(2,1)S(1)} %get-tuple-element.65), channel_id=1, source_target_pairs={{0,6},{1,7},{2,4},{3,5},{4,2},{5,3},{6,0},{7,1},{8,14},{9,15},{10,... | collective-permute-start | bytes 786440 | tf_op jit(solution)/shard_map/ppermute | solution.py:511

commit v7 on v6

--- a/solution.py
+++ b/solution.py
@@ -8,7 +8,7 @@
 EPSILON = 1e-06
 PAIR = 2
 WEIGHT = 1 << 31
-TURN = 8
+TURN = 16
 LOG_ROWS = 16
 LOG2E = 1.4426950408889634
 VMEM = pl.BlockSpec(memory_space=pltpu.VMEM)

time: 78 us -> 77.9 us (level)
  Pallas kernels: 23.1 us -> 22.1 us
    pallas_call x1, Pallas kernels: 5.84 us -> 4.81 us  [attend(): pl.pallas_call(kernel, out_shape=[shape((each * rows, width), jnp.bfloat1...]
  transfers between devices with their start and end apart: 19 -> 19, of which waited for: 6 -> 5; matrix products, arithmetic and copies ran while one was open for 0% -> 0% of each run, Pallas kernels for 28% -> 27%
where the time goes in v7:
time: 77.9 us; the launch traced here: 77.8 us
  waiting for transfers between devices  35.4 us (45%)
  Pallas kernels  22.1 us (28%)
  starting transfers between devices  19.4 us (25%)
  between operations  0.81 us (1%)
    ppermute x12, waiting for transfers between devices, exchange(): return lax.ppermute(value, 'seq', [(i, i ^ PAIR * m) for i in range(count)])  35.4 us
    ppermute x12, starting transfers between devices, exchange(): return lax.ppermute(value, 'seq', [(i, i ^ PAIR * m) for i in range(count)])  17.6 us
    pallas_call x1, Pallas kernels, within(): pl.pallas_call(kernel, out_shape=shape((heads, rows, width), jnp.float32)...  5.21 us
    pallas_call x1, Pallas kernels, attend(): pl.pallas_call(kernel, out_shape=[shape((each * rows, width), jnp.bfloat1...  4.81 us
    pallas_call x1, Pallas kernels, pack(): pl.pallas_call(kernel, out_shape=[shape((3 * hosted + (m == 0), rows, wid...  3.73 us
    pallas_call x1, Pallas kernels, totals_of(): pl.pallas_call(kernel, out_shape=[shape((few * width + LOG_ROWS, width),...  3.39 us
    pallas_call x1, Pallas kernels, finish(): pl.pallas_call(kernel, out_shape=shape((rows, heads, width), jnp.bfloat16...  2.94 us
    ppermute x7, starting transfers between devices, swap_cores(): return lax.ppermute(value, 'seq', [(i, i ^ 1) for i in range(count)])  1.74 us
  transfers between devices with their start and end apart: 19, of which 5 were waited for; matrix products, arithmetic and copies ran while one was open for 0% of the time, Pallas kernels for 27%

profile of v7, /device:TPU:0, one launch (start us, length us, event | category | flops | bytes accessed | tf_op | source)
XLA Modules:
  0.0 77.8 jit_solution(6143513998611760489)
XLA Ops:
  0.6 0.5 collective-permute-start.2
  1.1 0.1 collective-permute-start.3
  1.2 3.7 %pack.1 = (bf16[25,128,128]{2,1,0:T(8,128)(2,1)}, bf16[24,128,128]{2,1,0:T(8,128)(2,1)}, bf16[24,128,128]{2,1,0:T(8,128)(2,1)}, bf16[24,128,128]{2,1,0:T(8,128)(2,1)}) custom-call(s32[1]{0:T(128)} %bitcast.place_ref, bf16[32,128]{1,0:T(8,128)(2,1)} %bitcast.4, bf16[128,32,128]{2,1,0:T(8,128)(2,1)} %q_ref.3, bf16[128,32,128]{2,1,0:T(8,128)(2,1)} %k_ref.3, ...), custom_call_target="tpu_custom_call" | custom-call | flops 8589934592 | bytes 1 | tf_op jit(solution)/shard_map/pack/pallas_call | solution.py:112
  5.0 0.5 collective-permute-start.4
  5.5 2.6 %collective-permute-start = (bf16[24,128,128]{2,1,0:T(8,128)(2,1)}, bf16[24,128,128]{2,1,0:T(8,128)(2,1)S(1)}, u32[]{:S(2)}, u32[]{:S(2)}) collective-permute-start(bf16[24,128,128]{2,1,0:T(8,128)(2,1)} %get-tuple-element.35), channel_id=1, source_target_pairs={{0,2},{1,3},{2,0},{3,1},{4,6},{5,7},{6,4},{7,5},{8,10},{9,11},{10,... | collective-permute-start | bytes 2359304 | tf_op jit(solution)/shard_map/ppermute | solution.py:511
  8.0 1.5 %collective-permute-start.1 = (bf16[24,128,128]{2,1,0:T(8,128)(2,1)}, bf16[24,128,128]{2,1,0:T(8,128)(2,1)S(1)}, u32[]{:S(2)}, u32[]{:S(2)}) collective-permute-start(bf16[24,128,128]{2,1,0:T(8,128)(2,1)} %get-tuple-element.36), channel_id=1, source_target_pairs={{0,4},{1,5},{2,6},{3,7},{4,0},{5,1},{6,2},{7,3},{8,12},{9,13},{10,... | collective-permute-start | bytes 2359304 | tf_op jit(solution)/shard_map/ppermute | solution.py:511
  9.6 3.4 %totals_of.1 = (bf16[528,128]{1,0:T(8,128)(2,1)S(1)}, bf16[528,128]{1,0:T(8,128)(2,1)S(1)}, bf16[528,128]{1,0:T(8,128)(2,1)S(1)}, bf16[528,128]{1,0:T(8,128)(2,1)S(1)}) custom-call(s32[1]{0:T(128)} %bitcast.place_ref, bf16[128,32,128]{2,1,0:T(8,128)(2,1)S(1)} %copy-done, bf16[128,32,128]{2,1,0:T(8,128)(2,1)S(1)} %copy-done.1, bf16[32,128]{1,0:T(8,128)(2,1)S(1)} %bitcast.5, ...), custom_call_target="tpu_custom_call" | custom-call | flops 12884901888 | bytes 1 | tf_op jit(solution)/shard_map/totals_of/pallas_call | solution.py:309
  13.0 1.0 %collective-permute-start.6 = (bf16[528,128]{1,0:T(8,128)(2,1)S(1)}, bf16[528,128]{1,0:T(8,128)(2,1)S(1)}, u32[]{:S(2)}, u32[]{:S(2)}) collective-permute-start(bf16[528,128]{1,0:T(8,128)(2,1)S(1)} %get-tuple-element.40), channel_id=1, source_target_pairs={{0,2},{1,3},{2,0},{3,1},{4,6},{5,7},{6,4},{7,5},{8,10},{9,11},{10,... | collective-permute-start | bytes 405512 | tf_op jit(solution)/shard_map/ppermute | solution.py:511
  14.0 1.5 %collective-permute-start.7 = (bf16[528,128]{1,0:T(8,128)(2,1)S(1)}, bf16[528,128]{1,0:T(8,128)(2,1)S(1)}, u32[]{:S(2)}, u32[]{:S(2)}) collective-permute-start(bf16[528,128]{1,0:T(8,128)(2,1)S(1)} %get-tuple-element.41), channel_id=1, source_target_pairs={{0,4},{1,5},{2,6},{3,7},{4,0},{5,1},{6,2},{7,3},{8,12},{9,13},{10,... | collective-permute-start | bytes 405512 | tf_op jit(solution)/shard_map/ppermute | solution.py:511
  15.5 1.0 %collective-permute-start.8 = (bf16[528,128]{1,0:T(8,128)(2,1)S(1)}, bf16[528,128]{1,0:T(8,128)(2,1)S(1)}, u32[]{:S(2)}, u32[]{:S(2)}) collective-permute-start(bf16[528,128]{1,0:T(8,128)(2,1)S(1)} %get-tuple-element.42), channel_id=1, source_target_pairs={{0,6},{1,7},{2,4},{3,5},{4,2},{5,3},{6,0},{7,1},{8,14},{9,15},{10,... | collective-permute-start | bytes 405512 | tf_op jit(solution)/shard_map/ppermute | solution.py:511
  16.6 10.1 %collective-permute-done.rest_1_ = bf16[24,128,128]{2,1,0:T(8,128)(2,1)S(1)} collective-permute-done((bf16[24,128,128]{2,1,0:T(8,128)(2,1)}, bf16[24,128,128]{2,1,0:T(8,128)(2,1)S(1)}, u32[]{:S(2)}, u32[]{:S(2)}) %collective-permute-start) | collective-permute-done | bytes 786464 | tf_op jit(solution)/shard_map/ppermute | solution.py:511
  26.6 2.9 %collective-permute-start.5 = (bf16[24,128,128]{2,1,0:T(8,128)(2,1)S(1)}, bf16[24,128,128]{2,1,0:T(8,128)(2,1)S(1)}, u32[]{:S(2)}, u32[]{:S(2)}) collective-permute-start(bf16[24,128,128]{2,1,0:T(8,128)(2,1)S(1)} %copy-done.8), channel_id=1, source_target_pairs={{0,6},{1,7},{2,4},{3,5},{4,2},{5,3},{6,0},{7,1},{8,14},{9,15},{10,... | collective-permute-start | bytes 2359304 | tf_op jit(solution)/shard_map/ppermute | solution.py:511
  29.6 5.2 %within.1.inner_ref = f32[32,128,128]{2,1,0:T(8,128)S(1)} custom-call(s32[1]{0:T(128)} %bitcast.place_ref, bf16[128,32,128]{2,1,0:T(8,128)(2,1)S(1)} %copy-done.2, bf16[128,32,128]{2,1,0:T(8,128)(2,1)S(1)} %copy-done, bf16[128,32,128]{2,1,0:T(8,128)(2,1)S(1)} %copy-done.1, bf16[32,128]{1,0:T(8,128)(2,1)S(1)} %bitcast.6, ...), custom_call_target="tpu_custom_call" | custom-call | flops 30064771072 | bytes 1 | tf_op jit(solution)/shard_map/within/pallas_call | solution.py:362
  34.8 0.0 copy-start.3
  34.8 0.0 copy-start.6
  34.8 15.7 %collective-permute-done.7.rest_2_ = bf16[528,128]{1,0:T(8,128)(2,1)S(1)} collective-permute-done((bf16[528,128]{1,0:T(8,128)(2,1)S(1)}, bf16[528,128]{1,0:T(8,128)(2,1)S(1)}, u32[]{:S(2)}, u32[]{:S(2)}) %collective-permute-start.7) | collective-permute-done | bytes 135200 | tf_op jit(solution)/shard_map/ppermute | solution.py:511
  50.5 0.5 collective-permute-start.10
  51.0 0.1 collective-permute-start.11
  51.1 0.6 scan_chips.1
  51.7 1.2 %collective-permute-start.12 = (bf16[512,128]{1,0:T(8,128)(2,1)S(1)}, bf16[512,128]{1,0:T(8,128)(2,1)S(1)}, u32[]{:S(2)}, u32[]{:S(2)}) collective-permute-start(bf16[512,128]{1,0:T(8,128)(2,1)S(1)} %get-tuple-element.56), channel_id=1, source_target_pairs={{0,2},{1,3},{2,0},{3,1},{4,6},{5,7},{6,4},{7,5},{8,10},{9,11},{10,... | collective-permute-start | bytes 393224 | tf_op jit(solution)/shard_map/ppermute | solution.py:511
  52.9 0.9 %collective-permute-start.13 = (bf16[512,128]{1,0:T(8,128)(2,1)S(1)}, bf16[512,128]{1,0:T(8,128)(2,1)S(1)}, u32[]{:S(2)}, u32[]{:S(2)}) collective-permute-start(bf16[512,128]{1,0:T(8,128)(2,1)S(1)} %get-tuple-element.58), channel_id=1, source_target_pairs={{0,4},{1,5},{2,6},{3,7},{4,0},{5,1},{6,2},{7,3},{8,12},{9,13},{10,... | collective-permute-start | bytes 393224 | tf_op jit(solution)/shard_map/ppermute | solution.py:511
  53.8 1.4 %collective-permute-start.14 = (bf16[512,128]{1,0:T(8,128)(2,1)S(1)}, bf16[512,128]{1,0:T(8,128)(2,1)S(1)}, u32[]{:S(2)}, u32[]{:S(2)}) collective-permute-start(bf16[512,128]{1,0:T(8,128)(2,1)S(1)} %get-tuple-element.60), channel_id=1, source_target_pairs={{0,6},{1,7},{2,4},{3,5},{4,2},{5,3},{6,0},{7,1},{8,14},{9,15},{10,... | collective-permute-start | bytes 393224 | tf_op jit(solution)/shard_map/ppermute | solution.py:511
  55.3 4.8 %attend.1 = (bf16[1024,128]{1,0:T(8,128)(2,1)S(1)}, bf16[1024,128]{1,0:T(8,128)(2,1)S(1)}, bf16[1024,128]{1,0:T(8,128)(2,1)S(1)}, bf16[1024,128]{1,0:T(8,128)(2,1)S(1)}) custom-call(s32[1]{0:T(128)} %bitcast.place_ref, s32[8,8]{1,0:T(8,128)S(1)} %copy-done.6, s32[8]{0:T(128)S(1)} %copy-done.7, bf16[25,128,128]{2,1,0:T(8,128)(2,1)S(1)} %copy-done.3, ...), custom_call_target="tpu_custom_call" | custom-call | flops 30064771072 | bytes 1 | tf_op jit(solution)/shard_map/attend/pallas_call | solution.py:211
  60.1 1.3 %collective-permute-done.14.rest_3_ = bf16[512,128]{1,0:T(8,128)(2,1)S(1)} collective-permute-done((bf16[512,128]{1,0:T(8,128)(2,1)S(1)}, bf16[512,128]{1,0:T(8,128)(2,1)S(1)}, u32[]{:S(2)}, u32[]{:S(2)}) %collective-permute-start.14) | collective-permute-done | bytes 131104 | tf_op jit(solution)/shard_map/ppermute | solution.py:511
  61.4 0.1 collective-permute-start.15
  61.5 0.8 %collective-permute-start.16 = (bf16[1024,128]{1,0:T(8,128)(2,1)S(1)}, bf16[1024,128]{1,0:T(8,128)(2,1)S(1)}, u32[]{:S(2)}, u32[]{:S(2)}) collective-permute-start(bf16[1024,128]{1,0:T(8,128)(2,1)S(1)} %get-tuple-element.63), channel_id=1, source_target_pairs={{0,2},{1,3},{2,0},{3,1},{4,6},{5,7},{6,4},{7,5},{8,10},{9,11},{10,... | collective-permute-start | bytes 786440 | tf_op jit(solution)/shard_map/ppermute | solution.py:511
  62.3 1.5 %collective-permute-start.17 = (bf16[1024,128]{1,0:T(8,128)(2,1)S(1)}, bf16[1024,128]{1,0:T(8,128)(2,1)S(1)}, u32[]{:S(2)}, u32[]{:S(2)}) collective-permute-start(bf16[1024,128]{1,0:T(8,128)(2,1)S(1)} %get-tuple-element.64), channel_id=1, source_target_pairs={{0,4},{1,5},{2,6},{3,7},{4,0},{5,1},{6,2},{7,3},{8,12},{9,13},{10,... | collective-permute-start | bytes 786440 | tf_op jit(solution)/shard_map/ppermute | solution.py:511
  63.8 1.2 %collective-permute-start.18 = (bf16[1024,128]{1,0:T(8,128)(2,1)S(1)}, bf16[1024,128]{1,0:T(8,128)(2,1)S(1)}, u32[]{:S(2)}, u32[]{:S(2)}) collective-permute-start(bf16[1024,128]{1,0:T(8,128)(2,1)S(1)} %get-tuple-element.65), channel_id=1, source_target_pairs={{0,6},{1,7},{2,4},{3,5},{4,2},{5,3},{6,0},{7,1},{8,14},{9,15},{10,... | collective-permute-start | bytes 786440 | tf_op jit(solution)/shard_map/ppermute | solution.py:511
  65.0 2.9 %finish.1 = bf16[128,32,128]{2,1,0:T(8,128)(2,1)} custom-call(s32[1]{0:T(128)} %bitcast.place_ref, bf16[128,32,128]{2,1,0:T(8,128)(2,1)S(1)} %copy-done.2, bf16[32,128]{1,0:T(8,128)(2,1)S(1)} %bitcast.7, f32[32,128]{1,0:T(8,128)S(1)} %bitcast.3, f32[32,128,128]{2,1,0:T(8,128)S(1)} %within.1.inner_ref, bf16[16,128,128]{2,1,0:T(8,128)(2,1)S(1)} %gather_entry.1.own_ref, ...), custom_call_target="tpu_custom_call" | custom-call | flops 17179869184 | bytes 1 | tf_op jit(solution)/shard_map/finish/pallas_call | solution.py:483
  68.0 2.7 %collective-permute-done.16.rest_1_ = bf16[1024,128]{1,0:T(8,128)(2,1)S(1)} collective-permute-done((bf16[1024,128]{1,0:T(8,128)(2,1)S(1)}, bf16[1024,128]{1,0:T(8,128)(2,1)S(1)}, u32[]{:S(2)}, u32[]{:S(2)}) %collective-permute-start.16) | collective-permute-done | bytes 262176 | tf_op jit(solution)/shard_map/ppermute | solution.py:511
  70.7 5.7 %collective-permute-done.17.rest_2_ = bf16[1024,128]{1,0:T(8,128)(2,1)S(1)} collective-permute-done((bf16[1024,128]{1,0:T(8,128)(2,1)S(1)}, bf16[1024,128]{1,0:T(8,128)(2,1)S(1)}, u32[]{:S(2)}, u32[]{:S(2)}) %collective-permute-start.17) | collective-permute-done | bytes 262176 | tf_op jit(solution)/shard_map/ppermute | solution.py:511
  76.3 1.4 %unpack.1 = bf16[128,32,128]{2,1,0:T(8,128)(2,1)} custom-call(s32[1]{0:T(128)} %bitcast.place_ref, bf16[1024,128]{1,0:T(8,128)(2,1)S(1)} %get-tuple-element.62.rest_0_, bf16[1024,128]{1,0:T(8,128)(2,1)S(1)} %collective-permute-done.16.rest_1_, bf16[1024,128]{1,0:T(8,128)(2,1)S(1)} %collective-permute-done.17.rest_2_, ...), custom_call_target="tpu_custom_call" | custom-call | flops 8589934592 | bytes 1 | tf_op jit(solution)/shard_map/unpack/pallas_call | solution.py:244
  (32 shorter events, 0.1 us)
Async XLA Ops:
  0.6 8.9 %collective-permute-start.2 = (bf16[128,32,128]{2,1,0:T(8,128)(2,1)}, bf16[128,32,128]{2,1,0:T(8,128)(2,1)S(1)}, u32[]{:S(2)}, u32[]{:S(2)}) collective-permute-start(bf16[128,32,128]{2,1,0:T(8,128)(2,1)} %k_ref.5), channel_id=1, source_target_pairs={{0,1},{1,0},{2,3},{3,2},{4,5},{5,4},{6,7},{7,6},{8,9},{9,8},{10,11... | collective-permute-start | bytes 3145736 | tf_op jit(solution)/shard_map/ppermute | solution.py:517
  1.1 8.4 %collective-permute-start.3 = (bf16[128,32,128]{2,1,0:T(8,128)(2,1)}, bf16[128,32,128]{2,1,0:T(8,128)(2,1)S(1)}, u32[]{:S(2)}, u32[]{:S(2)}) collective-permute-start(bf16[128,32,128]{2,1,0:T(8,128)(2,1)} %v_ref.5), channel_id=1, source_target_pairs={{0,1},{1,0},{2,3},{3,2},{4,5},{5,4},{6,7},{7,6},{8,9},{9,8},{10,11... | collective-permute-start | bytes 3145736 | tf_op jit(solution)/shard_map/ppermute | solution.py:517
  1.2 8.3 %copy-start = (bf16[128,32,128]{2,1,0:T(8,128)(2,1)S(1)}, bf16[128,32,128]{2,1,0:T(8,128)(2,1)}, u32[]{:S(2)}) copy-start(bf16[128,32,128]{2,1,0:T(8,128)(2,1)} %k_ref.5) | copy-start | bytes 3145732
  1.2 8.4 %copy-start.1 = (bf16[128,32,128]{2,1,0:T(8,128)(2,1)S(1)}, bf16[128,32,128]{2,1,0:T(8,128)(2,1)}, u32[]{:S(2)}) copy-start(bf16[128,32,128]{2,1,0:T(8,128)(2,1)} %v_ref.5) | copy-start | bytes 3145732
  1.2 8.4 %copy-start.5 = (bf16[128,32]{0,1:T(8,128)(2,1)S(1)}, bf16[128,32]{0,1:T(8,128)(2,1)}, u32[]{:S(2)}) copy-start(bf16[128,32]{0,1:T(8,128)(2,1)} %param.13) | copy-start | bytes 24580
  5.0 4.6 %collective-permute-start.4 = (bf16[25,128,128]{2,1,0:T(8,128)(2,1)}, bf16[25,128,128]{2,1,0:T(8,128)(2,1)S(1)}, u32[]{:S(2)}, u32[]{:S(2)}) collective-permute-start(bf16[25,128,128]{2,1,0:T(8,128)(2,1)} %get-tuple-element.50.rest_0_), channel_id=1, source_target_pairs={{0,1},{1,0},{2,3},{3,2},{4,5},{5,4},{6,7},{7,6},{8,9},{9,8},{10,11... | collective-permute-start | bytes 2457608 | tf_op jit(solution)/shard_map/ppermute | solution.py:517
  5.5 21.2 %collective-permute-start = (bf16[24,128,128]{2,1,0:T(8,128)(2,1)}, bf16[24,128,128]{2,1,0:T(8,128)(2,1)S(1)}, u32[]{:S(2)}, u32[]{:S(2)}) collective-permute-start(bf16[24,128,128]{2,1,0:T(8,128)(2,1)} %get-tuple-element.35), channel_id=1, source_target_pairs={{0,2},{1,3},{2,0},{3,1},{4,6},{5,7},{6,4},{7,5},{8,10},{9,11},{10,... | collective-permute-start | bytes 2359304 | tf_op jit(solution)/shard_map/ppermute | solution.py:511
  8.0 18.6 %copy-start.8 = (bf16[24,128,128]{2,1,0:T(8,128)(2,1)S(1)}, bf16[24,128,128]{2,1,0:T(8,128)(2,1)}, u32[]{:S(2)}) copy-start(bf16[24,128,128]{2,1,0:T(8,128)(2,1)} %get-tuple-element.39) | copy-start | bytes 2359300
  8.0 21.5 %copy-start.2 = (bf16[128,32,128]{2,1,0:T(8,128)(2,1)S(1)}, bf16[128,32,128]{2,1,0:T(8,128)(2,1)}, u32[]{:S(2)}) copy-start(bf16[128,32,128]{2,1,0:T(8,128)(2,1)} %q_ref.5) | copy-start | bytes 3145732
  8.0 26.8 %collective-permute-start.1 = (bf16[24,128,128]{2,1,0:T(8,128)(2,1)}, bf16[24,128,128]{2,1,0:T(8,128)(2,1)S(1)}, u32[]{:S(2)}, u32[]{:S(2)}) collective-permute-start(bf16[24,128,128]{2,1,0:T(8,128)(2,1)} %get-tuple-element.36), channel_id=1, source_target_pairs={{0,4},{1,5},{2,6},{3,7},{4,0},{5,1},{6,2},{7,3},{8,12},{9,13},{10,... | collective-permute-start | bytes 2359304 | tf_op jit(solution)/shard_map/ppermute | solution.py:511
  13.0 21.8 %collective-permute-start.6 = (bf16[528,128]{1,0:T(8,128)(2,1)S(1)}, bf16[528,128]{1,0:T(8,128)(2,1)S(1)}, u32[]{:S(2)}, u32[]{:S(2)}) collective-permute-start(bf16[528,128]{1,0:T(8,128)(2,1)S(1)} %get-tuple-element.40), channel_id=1, source_target_pairs={{0,2},{1,3},{2,0},{3,1},{4,6},{5,7},{6,4},{7,5},{8,10},{9,11},{10,... | collective-permute-start | bytes 405512 | tf_op jit(solution)/shard_map/ppermute | solution.py:511
  14.0 36.5 %collective-permute-start.7 = (bf16[528,128]{1,0:T(8,128)(2,1)S(1)}, bf16[528,128]{1,0:T(8,128)(2,1)S(1)}, u32[]{:S(2)}, u32[]{:S(2)}) collective-permute-start(bf16[528,128]{1,0:T(8,128)(2,1)S(1)} %get-tuple-element.41), channel_id=1, source_target_pairs={{0,4},{1,5},{2,6},{3,7},{4,0},{5,1},{6,2},{7,3},{8,12},{9,13},{10,... | collective-permute-start | bytes 405512 | tf_op jit(solution)/shard_map/ppermute | solution.py:511
  15.5 35.0 %collective-permute-start.8 = (bf16[528,128]{1,0:T(8,128)(2,1)S(1)}, bf16[528,128]{1,0:T(8,128)(2,1)S(1)}, u32[]{:S(2)}, u32[]{:S(2)}) collective-permute-start(bf16[528,128]{1,0:T(8,128)(2,1)S(1)} %get-tuple-element.42), channel_id=1, source_target_pairs={{0,6},{1,7},{2,4},{3,5},{4,2},{5,3},{6,0},{7,1},{8,14},{9,15},{10,... | collective-permute-start | bytes 405512 | tf_op jit(solution)/shard_map/ppermute | solution.py:511
  26.6 23.9 %collective-permute-start.5 = (bf16[24,128,128]{2,1,0:T(8,128)(2,1)S(1)}, bf16[24,128,128]{2,1,0:T(8,128)(2,1)S(1)}, u32[]{:S(2)}, u32[]{:S(2)}) collective-permute-start(bf16[24,128,128]{2,1,0:T(8,128)(2,1)S(1)} %copy-done.8), channel_id=1, source_target_pairs={{0,6},{1,7},{2,4},{3,5},{4,2},{5,3},{6,0},{7,1},{8,14},{9,15},{10,... | collective-permute-start | bytes 2359304 | tf_op jit(solution)/shard_map/ppermute | solution.py:511
  34.8 20.5 %copy-start.3 = (bf16[25,128,128]{2,1,0:T(8,128)(2,1)S(1)}, bf16[25,128,128]{2,1,0:T(8,128)(2,1)}, u32[]{:S(2)}) copy-start(bf16[25,128,128]{2,1,0:T(8,128)(2,1)} %get-tuple-element.50.rest_0_) | copy-start | bytes 2457604
  34.8 20.5 %copy-start.6 = (s32[8,8]{1,0:T(8,128)S(1)}, s32[8,8]{1,0:T(8,128)}, u32[]{:S(2)}) copy-start(s32[8,8]{1,0:T(8,128)} %bits_ref.1) | copy-start | bytes 772
  34.8 20.5 %copy-start.7 = (s32[8]{0:T(128)S(1)}, s32[8]{0:T(128)}, u32[]{:S(2)}) copy-start(s32[8]{0:T(128)} %agents_ref.1) | copy-start | bytes 100
  50.5 3.3 %collective-permute-start.9 = (bf16[24,128,128]{2,1,0:T(8,128)(2,1)S(1)}, bf16[24,128,128]{2,1,0:T(8,128)(2,1)S(1)}, u32[]{:S(2)}, u32[]{:S(2)}) collective-permute-start(bf16[24,128,128]{2,1,0:T(8,128)(2,1)S(1)} %collective-permute-done.rest_1_), channel_id=1, source_target_pairs={{0,1},{1,0},{2,3},{3,2},{4,5},{5,4},{6,7},{7,6},{8,9},{9,8},{10,11... | collective-permute-start | bytes 2359304 | tf_op jit(solution)/shard_map/ppermute | solution.py:517
  50.5 4.7 %collective-permute-start.10 = (bf16[24,128,128]{2,1,0:T(8,128)(2,1)S(1)}, bf16[24,128,128]{2,1,0:T(8,128)(2,1)S(1)}, u32[]{:S(2)}, u32[]{:S(2)}) collective-permute-start(bf16[24,128,128]{2,1,0:T(8,128)(2,1)S(1)} %collective-permute-done.1.rest_2_), channel_id=1, source_target_pairs={{0,1},{1,0},{2,3},{3,2},{4,5},{5,4},{6,7},{7,6},{8,9},{9,8},{10,11... | collective-permute-start | bytes 2359304 | tf_op jit(solution)/shard_map/ppermute | solution.py:517
  51.0 4.2 %collective-permute-start.11 = (bf16[24,128,128]{2,1,0:T(8,128)(2,1)S(1)}, bf16[24,128,128]{2,1,0:T(8,128)(2,1)S(1)}, u32[]{:S(2)}, u32[]{:S(2)}) collective-permute-start(bf16[24,128,128]{2,1,0:T(8,128)(2,1)S(1)} %collective-permute-done.5.rest_3_), channel_id=1, source_target_pairs={{0,1},{1,0},{2,3},{3,2},{4,5},{5,4},{6,7},{7,6},{8,9},{9,8},{10,11... | collective-permute-start | bytes 2359304 | tf_op jit(solution)/shard_map/ppermute | solution.py:517
  51.7 9.7 %collective-permute-start.12 = (bf16[512,128]{1,0:T(8,128)(2,1)S(1)}, bf16[512,128]{1,0:T(8,128)(2,1)S(1)}, u32[]{:S(2)}, u32[]{:S(2)}) collective-permute-start(bf16[512,128]{1,0:T(8,128)(2,1)S(1)} %get-tuple-element.56), channel_id=1, source_target_pairs={{0,2},{1,3},{2,0},{3,1},{4,6},{5,7},{6,4},{7,5},{8,10},{9,11},{10,... | collective-permute-start | bytes 393224 | tf_op jit(solution)/shard_map/ppermute | solution.py:511
  52.9 8.5 %collective-permute-start.13 = (bf16[512,128]{1,0:T(8,128)(2,1)S(1)}, bf16[512,128]{1,0:T(8,128)(2,1)S(1)}, u32[]{:S(2)}, u32[]{:S(2)}) collective-permute-start(bf16[512,128]{1,0:T(8,128)(2,1)S(1)} %get-tuple-element.58), channel_id=1, source_target_pairs={{0,4},{1,5},{2,6},{3,7},{4,0},{5,1},{6,2},{7,3},{8,12},{9,13},{10,... | collective-permute-start | bytes 393224 | tf_op jit(solution)/shard_map/ppermute | solution.py:511
  53.8 7.5 %collective-permute-start.14 = (bf16[512,128]{1,0:T(8,128)(2,1)S(1)}, bf16[512,128]{1,0:T(8,128)(2,1)S(1)}, u32[]{:S(2)}, u32[]{:S(2)}) collective-permute-start(bf16[512,128]{1,0:T(8,128)(2,1)S(1)} %get-tuple-element.60), channel_id=1, source_target_pairs={{0,6},{1,7},{2,4},{3,5},{4,2},{5,3},{6,0},{7,1},{8,14},{9,15},{10,... | collective-permute-start | bytes 393224 | tf_op jit(solution)/shard_map/ppermute | solution.py:511
  61.3 3.7 %copy-start.4 = (f32[4096]{0:T(1024)S(1)}, f32[4096]{0:T(1024)}, u32[]{:S(2)}) copy-start(f32[4096]{0:T(1024)} %param.14) | copy-start | bytes 49156
  61.4 3.6 %collective-permute-start.15 = (bf16[16,128,128]{2,1,0:T(8,128)(2,1)S(1)}, bf16[16,128,128]{2,1,0:T(8,128)(2,1)S(1)}, u32[]{:S(2)}, u32[]{:S(2)}) collective-permute-start(bf16[16,128,128]{2,1,0:T(8,128)(2,1)S(1)} %gather_entry.1.own_ref), channel_id=1, source_target_pairs={{0,1},{1,0},{2,3},{3,2},{4,5},{5,4},{6,7},{7,6},{8,9},{9,8},{10,11... | collective-permute-start | bytes 1572872 | tf_op jit(solution)/shard_map/ppermute | solution.py:517
  61.5 9.2 %collective-permute-start.16 = (bf16[1024,128]{1,0:T(8,128)(2,1)S(1)}, bf16[1024,128]{1,0:T(8,128)(2,1)S(1)}, u32[]{:S(2)}, u32[]{:S(2)}) collective-permute-start(bf16[1024,128]{1,0:T(8,128)(2,1)S(1)} %get-tuple-element.63), channel_id=1, source_target_pairs={{0,2},{1,3},{2,0},{3,1},{4,6},{5,7},{6,4},{7,5},{8,10},{9,11},{10,... | collective-permute-start | bytes 786440 | tf_op jit(solution)/shard_map/ppermute | solution.py:511
  62.3 14.0 %collective-permute-start.17 = (bf16[1024,128]{1,0:T(8,128)(2,1)S(1)}, bf16[1024,128]{1,0:T(8,128)(2,1)S(1)}, u32[]{:S(2)}, u32[]{:S(2)}) collective-permute-start(bf16[1024,128]{1,0:T(8,128)(2,1)S(1)} %get-tuple-element.64), channel_id=1, source_target_pairs={{0,4},{1,5},{2,6},{3,7},{4,0},{5,1},{6,2},{7,3},{8,12},{9,13},{10,... | collective-permute-start | bytes 786440 | tf_op jit(solution)/shard_map/ppermute | solution.py:511
  63.8 12.5 %collective-permute-start.18 = (bf16[1024,128]{1,0:T(8,128)(2,1)S(1)}, bf16[1024,128]{1,0:T(8,128)(2,1)S(1)}, u32[]{:S(2)}, u32[]{:S(2)}) collective-permute-start(bf16[1024,128]{1,0:T(8,128)(2,1)S(1)} %get-tuple-element.65), channel_id=1, source_target_pairs={{0,6},{1,7},{2,4},{3,5},{4,2},{5,3},{6,0},{7,1},{8,14},{9,15},{10,... | collective-permute-start | bytes 786440 | tf_op jit(solution)/shard_map/ppermute | solution.py:511
